TPU v7x, 32 devices: a whole 2x2x4 slice. The times are simulated.
32 devices in a mesh: groups: 2 (over x), expert: 16 (over z, y, core).
Axes of the slice: x: 2, y: 2, z: 4, core: 2. Of those that a mesh axis runs over, the one named last changes fastest.
Arguments:
- frames: bfloat16 [32, 384, 1024], P(('groups', 'expert')), parts along dimension 0, may hold values from -6 to 6
- frame_counts: int32 [32], P(('groups', 'expert')), parts along dimension 0, may hold values from 1 to 384, 4608 in all
- expert_ids: int32 [32, 384, 1], P(('groups', 'expert')), parts along dimension 0, may hold values from 0 to 7
- conv_kernel: float32 [31, 1024], replicated, may hold values from -1 to 1
- router: bfloat16 [1024, 8], replicated, may hold values from -0.1875 to 0.1875
- w_in: bfloat16 [1024, 32768], P(None, 'expert'), may hold values from -0.1875 to 0.1875
- w_out: bfloat16 [32768, 1024], P('expert'), may hold values from -0.09375 to 0.09375
- final_gain: float32 [1024], replicated, may hold values from 0.1 to 1.9
Outputs:
- block_out: bfloat16 [32, 384, 1024], P(('groups', 'expert')), parts along dimension 0
There are 2 independent parts, one for each index of `groups`. A program takes and returns all parts, laid end to end along the dimension named above; an argument that names none is the same for every part. Nothing has to cross between parts.
Inputs may be any that keep to these rules, and one draw needn't show every extreme that they name: `frame_counts`: some utterance of every part uses all 384 frames.
All inputs are finite; a program needn't handle non-finite values. No bound on the sum of `frame_counts` on one device may be relied on, other than what follows from the above.
Results may differ from a plain program's by a relative error of at most 0.0047.
Values may be sent and summed in bfloat16 or wider, within the bound.
No kernel may reach another device: no remote copies, remote signals or barrier semaphores. Data moves between devices by JAX's collectives and lax.ppermute only.
A program may use at most 64 MiB of HBM per device.

v0:
```python
import jax
import jax.numpy as jnp
from jax import lax
from jax.sharding import PartitionSpec as P


def partner(block, axis, distance):
    count = lax.axis_size(axis)
    route = []
    for low in range(count):
        high = low | 1 << distance
        if high != low and high < count:
            route += [(low, high), (high, low)]
    return lax.ppermute(block, axis, route)


def layer_norm(values):
    mean = jnp.mean(values, axis=-1, keepdims=True)
    centred = values - mean
    variance = jnp.mean(centred * centred, axis=-1, keepdims=True)
    return centred * lax.rsqrt(variance + 1e-05)


def on_device(frames, frame_counts, expert_ids, conv_kernel, router, w_in, w_out, final_gain):
    inputs = frames[0].astype(jnp.float32)
    length = inputs.shape[0]
    width = inputs.shape[1]
    taps = conv_kernel.shape[0]
    n_dev = lax.axis_size("expert")
    experts = n_dev // 2
    cap = 2 * ((5 * length + 8 * experts - 1) // (8 * experts))
    half = cap // 2
    positions = jnp.arange(length, dtype=jnp.int32)
    valid = positions < frame_counts[0]
    normed = layer_norm(inputs) * valid[:, None].astype(jnp.float32)
    reach = taps // 2
    padded = jnp.pad(normed, ((reach, reach), (0, 0)))
    conv = jnp.zeros_like(normed)
    for step in range(taps):
        conv = conv + conv_kernel[step][None, :] * padded[step : step + length, :]
    stream = (inputs + jax.nn.silu(conv)).astype(jnp.bfloat16)
    expert_in = layer_norm(stream.astype(jnp.float32)).astype(jnp.bfloat16)
    logits = jnp.dot(expert_in, router, preferred_element_type=jnp.float32)
    chosen_ids = expert_ids[0, :, 0]
    onehot = (
        (chosen_ids[:, None] == jnp.arange(experts, dtype=jnp.int32)[None, :]) & valid[:, None]
    ).astype(jnp.int32)
    before = jnp.cumsum(onehot, axis=0) - onehot
    rank = jnp.sum(before * onehot, axis=-1)
    gate = jax.nn.sigmoid(jnp.sum(logits * onehot.astype(jnp.float32), axis=-1))
    sent = valid & (rank < cap)
    slot_index = chosen_ids * cap + rank
    slot_rows = jnp.arange(experts * cap, dtype=jnp.int32)
    placing = ((slot_index[None, :] == slot_rows[:, None]) & sent[None, :]).astype(jnp.bfloat16)
    outgoing = jnp.dot(placing, expert_in, preferred_element_type=jnp.float32).astype(jnp.bfloat16)
    other_in, other_out = partner((w_in, w_out), "expert", 0)
    whole_in = jnp.concatenate([w_in, other_in], axis=1)
    whole_out = jnp.concatenate([w_out, other_out], axis=0)
    piece = lax.all_to_all(
        outgoing.reshape(n_dev, half, width), "expert", split_axis=0, concat_axis=0, tiled=True
    )
    sources = piece.shape[0]
    items = piece.shape[1]
    flat = piece.reshape(sources * items, width)
    hidden = jax.nn.silu(jnp.dot(flat, whole_in, preferred_element_type=jnp.float32)).astype(
        jnp.bfloat16
    )
    result = jnp.dot(hidden, whole_out, preferred_element_type=jnp.float32).astype(jnp.bfloat16)
    returned = lax.all_to_all(
        result.reshape(sources, items, width), "expert", split_axis=0, concat_axis=0, tiled=True
    )
    combined = returned.reshape(experts * cap, width)
    picked = lax.dot_general(
        placing, combined, (((0,), (0,)), ((), ())), preferred_element_type=jnp.float32
    )
    total = stream.astype(jnp.float32) + 0.5 * gate[:, None] * picked
    block_out = (layer_norm(total) * final_gain).astype(jnp.bfloat16)
    return block_out.reshape(1, length, width)


def solution(mesh):
    return jax.shard_map(
        on_device,
        mesh=mesh,
        in_specs=(
            P(("groups", "expert"), None, None),
            P(("groups", "expert")),
            P(("groups", "expert"), None, None),
            P(),
            P(),
            P(None, "expert"),
            P("expert", None),
            P(),
        ),
        out_specs=P(("groups", "expert"), None, None),
        check_vma=False,
    )
```

profile of v0, /device:TPU:0, one launch (start us, length us, event | category | flops | bytes accessed | tf_op | source)
XLA Modules:
  0.0 95.9 jit_solution(6106894418960230696)
XLA Ops:
  0.0 0.0 copy-start
  0.0 0.0 copy-start.1
  0.0 0.0 copy-start.3
  0.0 0.5 collective-permute-start
  0.5 0.1 collective-permute-start.1
  0.6 1.1 %fusion.78 = (f32[1,1024]{1,0:T(1,128)S(1)}, f32[1,1024]{1,0:T(1,128)S(1)}, f32[1,1024]{1,0:T(1,128)S(1)}, f32[1,1024]{1,0:T(1,128)S(1)}, f32[1,1024]{1,0:T(1,12...) fusion(f32[31,1024]{1,0:T(8,128)} %param.11), kind=kLoop, calls=%fused_computation.105 | loop fusion | bytes 98304 | tf_op jit(solution)/shard_map/slice | solution.py:40
  1.7 1.4 %fusion.77 = (f32[1,1024]{1,0:T(1,128)S(1)}, f32[1,1024]{1,0:T(1,128)S(1)}, f32[1,1024]{1,0:T(1,128)S(1)}, f32[1,1024]{1,0:T(1,128)S(1)}, f32[1,1024]{1,0:T(1,12...) fusion(f32[31,1024]{1,0:T(8,128)} %param.11), kind=kLoop, calls=%fused_computation.104 | loop fusion | bytes 155648 | tf_op jit(solution)/shard_map/slice | solution.py:40
  3.8 1.3 %convert_reduce_fusion.1 = f32[384]{0:T(512)S(1)} fusion(bf16[1,384,1024]{2,1,0:T(8,128)(2,1)} %param.8), kind=kLoop, calls=%fused_computation.13 | loop fusion | flops 786048 | bytes 787968 | tf_op jit(solution)/shard_map/reduce_sum | solution.py:18
  5.1 0.0 copy-done.1
  5.2 0.3 fusion.21
  5.5 0.0 copy-done.3
  5.6 0.9 reduce-window.6
  6.4 0.2 slice_reduce_fusion
  6.7 0.1 fusion.66
  6.8 0.3 fusion.22
  7.1 8.3 %convert_reduce_fusion = (f32[384]{0:T(512)S(1)}, bf16[384,1024]{1,0:T(8,128)(2,1)S(1)}) fusion(f32[1024]{0:T(1024)S(1)} %bitcast.74, f32[1024]{0:T(1024)S(1)} %bitcast.75, f32[1024]{0:T(1024)S(1)} %bitcast.77, f32[1024]{0:T(1024)S(1)} %bitcast.78, f32[1024]{0:T(1024)S(1)} %bitcast.79, f32[1024]{0:T(1024)S(1)} %bitcast.80, f32[1024]{0:T(1024)S(1)} %bitcast.81, ...), kind=kLoop, calls=%fused_computation.12 | loop fusion | flops 27524736 | bytes 3274240 | tf_op jit(solution)/shard_map/reduce_sum | solution.py:18
  15.4 0.3 fusion.19
  15.8 0.8 convolution_convert_fusion
  16.6 0.3 reshape.109
  16.9 32.0 %all_to_all.10 = bf16[16,30,1024]{2,1,0:T(8,128)(2,1)S(1)} all-to-all(bf16[16,30,1024]{2,1,0:T(8,128)(2,1)S(1)} %reshape.109), channel_id=1, replica_groups=mesh['groups'=2,'expert'=16] {'expert'}, dimensions={0} | all-to-all | bytes 1966080 | tf_op jit(solution)/shard_map/all_to_all | solution.py:59
  48.9 0.3 reshape.110
  49.2 0.0 collective-permute-done
  49.2 0.0 collective-permute-done.1
  49.2 14.7 %fusion.51 = bf16[480,1024]{1,0:T(8,128)(2,1)S(1)} fusion(bf16[2048,1024]{1,0:T(8,128)(2,1)} %collective-permute-done.1, bf16[2048,1024]{1,0:T(8,128)(2,1)} %param.14, bf16[480,1024]{1,0:T(8,128)(2,1)S(1)} %reshape.110, bf16[1024,2048]{1,0:T(8,128)(2,1)} %collective-permute-done, bf16[1024,2048]{1,0:T(8,128)(2,1)} %param.13), kind=kOutput, calls=%fused_computation.69 | convolution fusion | flops 8096940032 | bytes 18743296 | tf_op jit(solution)/shard_map/dot_general | solution.py:68
  63.9 1.2 %reshape.111 = bf16[16,30,1024]{2,1,0:T(8,128)(2,1)} reshape(bf16[480,1024]{1,0:T(8,128)(2,1)S(1)} %fusion.51) | data formatting | bytes 1966080 | tf_op jit(solution)/shard_map/reshape | solution.py:70
  65.1 5.0 %all-to-all-start.1 = ((bf16[16,30,1024]{2,1,0:T(8,128)(2,1)}), bf16[16,30,1024]{2,1,0:T(8,128)(2,1)S(1)}, u32[]{:S(2)}, u32[]{:S(2)}) async-start(bf16[16,30,1024]{2,1,0:T(8,128)(2,1)} %reshape.111), calls=%async_computation.1 | async-start | bytes 2097152 | tf_op jit(solution)/shard_map/all_to_all | solution.py:69
  70.1 0.0 copy-done
  70.1 0.4 fusion.56
  70.5 22.5 %all-to-all-done.1 = bf16[16,30,1024]{2,1,0:T(8,128)(2,1)S(1)} async-done(((bf16[16,30,1024]{2,1,0:T(8,128)(2,1)}), bf16[16,30,1024]{2,1,0:T(8,128)(2,1)S(1)}, u32[]{:S(2)}, u32[]{:S(2)}) %all-to-all-start.1) | async-done | bytes 983072 | tf_op jit(solution)/shard_map/all_to_all | solution.py:69
  93.0 0.3 reshape.112
  93.3 0.7 fusion.79
  94.0 0.0 copy-start.2
  94.0 0.3 multiply_reduce_fusion
  94.3 0.4 copy-done.2
  94.7 1.1 %fusion.57 = bf16[1,384,1024]{2,1,0:T(8,128)(2,1)} fusion(f32[384,1024]{1,0:T(8,128)S(1)} %get-tuple-element.39, f32[1024]{0:T(1024)S(1)} %copy-done.2, f32[384]{0:T(512)S(1)} %add_rsqrt_fusion, f32[384]{0:T(512)S(1)} %broadcast_multiply_fusion), kind=kLoop, calls=%fused_computation.73 | loop fusion | flops 1572864 | bytes 2366464 | tf_op jit(solution)/shard_map/reshape | solution.py:78
  (14 shorter events, 0.1 us)
Async XLA Ops:
  0.0 70.1 %copy-start = (bf16[1024,8]{0,1:T(8,128)(2,1)S(1)}, bf16[1024,8]{0,1:T(8,128)(2,1)}, u32[]{:S(2)}) copy-start(bf16[1024,8]{0,1:T(8,128)(2,1)} %param.12) | copy-start | bytes 49156
  0.0 5.1 %copy-start.1 = (bf16[1,384,1024]{2,1,0:T(8,128)(2,1)S(1)}, bf16[1,384,1024]{2,1,0:T(8,128)(2,1)}, u32[]{:S(2)}) copy-start(bf16[1,384,1024]{2,1,0:T(8,128)(2,1)} %param.8) | copy-start | bytes 2359300
  0.0 5.5 %copy-start.3 = (s32[1,384,1]{1,2,0:T(1,128)S(1)}, s32[1,384,1]{1,2,0:T(1,128)}, u32[]{:S(2)}) copy-start(s32[1,384,1]{1,2,0:T(1,128)} %param.10) | copy-start | bytes 4612
  0.0 49.2 %collective-permute-start = (bf16[1024,2048]{1,0:T(8,128)(2,1)}, bf16[1024,2048]{1,0:T(8,128)(2,1)}, u32[]{:S(2)}, u32[]{:S(2)}) collective-permute-start(bf16[1024,2048]{1,0:T(8,128)(2,1)} %param.13), channel_id=1, source_target_pairs={{0,1},{1,0},{2,3},{3,2},{4,5},{5,4},{6,7},{7,6},{8,9},{9,8},{10,11... | collective-permute-start | bytes 12582920 | tf_op jit(solution)/shard_map/ppermute | solution.py:14
  0.5 48.7 %collective-permute-start.1 = (bf16[2048,1024]{1,0:T(8,128)(2,1)}, bf16[2048,1024]{1,0:T(8,128)(2,1)}, u32[]{:S(2)}, u32[]{:S(2)}) collective-permute-start(bf16[2048,1024]{1,0:T(8,128)(2,1)} %param.14), channel_id=1, source_target_pairs={{0,1},{1,0},{2,3},{3,2},{4,5},{5,4},{6,7},{7,6},{8,9},{9,8},{10,11... | collective-permute-start | bytes 12582920 | tf_op jit(solution)/shard_map/ppermute | solution.py:14
  65.1 27.9 %all-to-all-start.1 = ((bf16[16,30,1024]{2,1,0:T(8,128)(2,1)}), bf16[16,30,1024]{2,1,0:T(8,128)(2,1)S(1)}, u32[]{:S(2)}, u32[]{:S(2)}) async-start(bf16[16,30,1024]{2,1,0:T(8,128)(2,1)} %reshape.111), calls=%async_computation.1 | async-start | bytes 2097152 | tf_op jit(solution)/shard_map/all_to_all | solution.py:69
  94.0 0.7 copy-start.2
where the time goes:
time: 97.5 us; the launch traced here: 95.9 us
  blocking collectives  32 us (33%)
  waiting for transfers between devices  22.5 us (23%)
  matrix products  16.6 us (17%)
  other arithmetic  13.2 us (14%)
  starting transfers between devices  5.59 us (6%)
  local copies, waits for them, and re-layouts  5.17 us (5%)
    all_to_all x1, blocking collectives, on_device(): lax.all_to_all(outgoing.reshape(n_dev, half, width), 'expert', split_axis...  32 us
    all_to_all x1, waiting for transfers between devices, on_device(): lax.all_to_all(result.reshape(sources, items, width), 'expert', split_axi...  22.5 us
    dot_general x1, matrix products, on_device(): jnp.dot(hidden, whole_out, preferred_element_type=jnp.float32)  14.7 us
    reduce_sum x2, other arithmetic, layer_norm(): mean = jnp.mean(values, axis=-1, keepdims=True)  9.64 us
    all_to_all x1, starting transfers between devices, on_device(): lax.all_to_all(result.reshape(sources, items, width), 'expert', split_axi...  4.98 us
    slice x2, local copies, waits for them, and re-layouts, on_device(): conv = conv + conv_kernel[step][None, :] * padded[step:step + length, :]  2.54 us
  transfers between devices with their start and end apart: 3, of which 1 were waited for; matrix products, arithmetic and copies ran while one was open for 17% of the time, Pallas kernels for 0%

commit v1 on v0

v1 whole, which is shorter than its diff:
```python
import functools

import jax
import jax.numpy as jnp
from jax import lax
from jax.experimental import pallas as pl
from jax.experimental.pallas import tpu as pltpu
from jax.sharding import PartitionSpec as P

LANES = 128
ROWS = 8
BLOCK = 64
EPS = 1e-05
MIB = 1 << 20


def xor_route(block, axis, distance):
    count = lax.axis_size(axis)
    return lax.ppermute(block, axis, [(i, i ^ distance) for i in range(count)])


def exchange(block, axis, chips):
    count = lax.axis_size(axis)
    same_core = [list(range(core, count, 2)) for core in range(2)]
    blocks = block.reshape(chips, block.shape[0] // chips, block.shape[1])
    moved = lax.all_to_all(blocks, axis, split_axis=0, concat_axis=0, tiled=True, axis_index_groups=same_core)
    return moved.reshape(block.shape)


def silu(value):
    return value / (1.0 + jnp.exp(-value))


def normalise(values):
    mean = jnp.mean(values, axis=-1, keepdims=True)
    centred = values - mean
    variance = jnp.mean(centred * centred, axis=-1, keepdims=True)
    return centred * lax.rsqrt(variance + EPS)


def pre_kernel(cap, pitch, count_ref, frames_ref, ids_ref, taps_ref, stream_ref, expert_in_ref, slot_ref, *rest):
    *message_refs, padded, taps_by_row, conv = rest
    length, width = frames_ref.shape
    taps = taps_ref.shape[0]
    reach = taps // 2
    groups = width // LANES
    count = count_ref[0]

    for group in range(groups):
        lanes = slice(group * LANES, (group + 1) * LANES)
        taps_by_row[pl.ds(group, taps, stride=groups), :] = taps_ref[:, lanes]
    edge = jnp.zeros((reach * groups, LANES), jnp.float32)
    padded[: reach * groups, :] = edge
    padded[(reach + length) * groups :, :] = edge
    for start in range(0, length, BLOCK):
        values = frames_ref[start : start + BLOCK, :].astype(jnp.float32)
        position = start + lax.broadcasted_iota(jnp.int32, (BLOCK, 1), 0)
        normed = jnp.where(position < count, normalise(values), 0.0)
        for group in range(groups):
            lanes = slice(group * LANES, (group + 1) * LANES)
            padded[pl.ds((reach + start) * groups + group, BLOCK, stride=groups), :] = normed[:, lanes]

    def convolve(index, carry):
        base = pl.multiple_of(index * (ROWS * groups), ROWS * groups)
        window = [padded[pl.ds(base + step * groups, groups), :] for step in range(ROWS + taps - 1)]
        sums = [None] * ROWS
        for tap in range(taps):
            weight = taps_by_row[tap * groups : (tap + 1) * groups, :]
            for row in range(ROWS):
                term = weight * window[row + tap]
                sums[row] = term if tap == 0 else sums[row] + term
        for row in range(ROWS):
            conv[pl.ds(base + row * groups, groups), :] = sums[row]
        return carry

    lax.fori_loop(0, length // ROWS, convolve, 0)

    for start in range(0, length, BLOCK):
        rows = slice(start, start + BLOCK)
        mixed = jnp.concatenate(
            [conv[pl.ds(start * groups + group, BLOCK, stride=groups), :] for group in range(groups)], axis=1
        )
        stream = (frames_ref[rows, :].astype(jnp.float32) + silu(mixed)).astype(jnp.bfloat16)
        stream_ref[rows, :] = stream
        expert_in_ref[rows, :] = normalise(stream.astype(jnp.float32)).astype(jnp.bfloat16)

    chips = slot_ref.shape[0]
    ids = ids_ref[...]
    at = lax.broadcasted_iota(jnp.int32, (chips, length), 1)
    chosen = (ids == lax.broadcasted_iota(jnp.int32, (chips, length), 0)) & (at < count)
    earlier = lax.broadcasted_iota(jnp.int32, (length, length), 0) < lax.broadcasted_iota(
        jnp.int32, (length, length), 1
    )
    before = jnp.dot(
        chosen.astype(jnp.bfloat16), earlier.astype(jnp.bfloat16), preferred_element_type=jnp.float32
    )
    rank = jnp.sum(jnp.where(chosen, before, 0.0), axis=0, keepdims=True).astype(jnp.int32)
    sent = (at[:1] < count) & (rank < cap)
    slot = jnp.where(sent, ids * pitch + rank, -1)
    slot_ref[...] = jnp.broadcast_to(slot, slot_ref.shape)
    slots = chips * pitch
    placing = (slot == lax.broadcasted_iota(jnp.int32, (slots, length), 0)).astype(jnp.bfloat16)
    span = slots // len(message_refs)
    for start in range(0, width, 256):
        columns = slice(start, start + 256)
        placed = jnp.dot(placing, expert_in_ref[:, columns], preferred_element_type=jnp.float32)
        placed = placed.astype(jnp.bfloat16)
        for number, message in enumerate(message_refs):
            message[:, columns] = placed[number * span : (number + 1) * span, :]


def prepare(frames, count, ids, taps, chips, cap, pitch, messages):
    length, width = frames.shape
    groups = width // LANES
    reach = taps.shape[0] // 2
    whole = pl.BlockSpec(memory_space=pltpu.VMEM)
    span = chips * pitch // messages
    bf16 = jnp.bfloat16
    return pl.pallas_call(
        functools.partial(pre_kernel, cap, pitch),
        in_specs=[pl.BlockSpec(memory_space=pltpu.SMEM), whole, whole, whole],
        out_specs=[whole] * (3 + messages),
        out_shape=[
            jax.ShapeDtypeStruct((length, width), bf16),
            jax.ShapeDtypeStruct((length, width), bf16),
            jax.ShapeDtypeStruct((chips, length), jnp.int32),
        ]
        + [jax.ShapeDtypeStruct((span, width), bf16)] * messages,
        scratch_shapes=[
            pltpu.VMEM(((length + 2 * reach) * groups, LANES), jnp.float32),
            pltpu.VMEM((taps.shape[0] * groups, LANES), jnp.float32),
            pltpu.VMEM((length * groups, LANES), jnp.float32),
        ],
        compiler_params=pltpu.CompilerParams(vmem_limit_bytes=24 * MIB),
        cost_estimate=pl.CostEstimate(flops=4 * 10**8, bytes_accessed=4 * 10**6, transcendentals=0),
        name="prepare",
    )(count, frames, ids, taps)


def gate_kernel(pitch, count_ref, expert_in_ref, router_ref, ids_ref, slot_ref, gate_ref, picking_ref):
    length = expert_in_ref.shape[0]
    experts = router_ref.shape[1]
    slots = picking_ref.shape[1]
    logits = jnp.dot(expert_in_ref[...], router_ref[...], preferred_element_type=jnp.float32)
    ids = jnp.broadcast_to(ids_ref[...].astype(jnp.float32), (experts, length)).T
    position = lax.broadcasted_iota(jnp.int32, (length, experts), 0)
    column = lax.broadcasted_iota(jnp.int32, (length, experts), 1).astype(jnp.float32)
    chosen = (ids == column) & (position < count_ref[0])
    logit = jnp.sum(jnp.where(chosen, logits, 0.0), axis=1, keepdims=True)
    gate_ref[...] = 0.5 / (1.0 + jnp.exp(-logit))
    slot = slot_ref[...].astype(jnp.float32).T[:, :1].astype(jnp.int32)
    picking_ref[...] = (slot == lax.broadcasted_iota(jnp.int32, (length, slots), 1)).astype(jnp.bfloat16)


def gate_and_picking(count, expert_in, router, ids, slot, pitch):
    length = expert_in.shape[0]
    slots = slot.shape[0] * pitch
    whole = pl.BlockSpec(memory_space=pltpu.VMEM)
    return pl.pallas_call(
        functools.partial(gate_kernel, pitch),
        in_specs=[pl.BlockSpec(memory_space=pltpu.SMEM)] + [whole] * 4,
        out_specs=[whole] * 2,
        out_shape=[
            jax.ShapeDtypeStruct((length, 1), jnp.float32),
            jax.ShapeDtypeStruct((length, slots), jnp.bfloat16),
        ],
        compiler_params=pltpu.CompilerParams(vmem_limit_bytes=12 * MIB),
        name="gate",
    )(count, expert_in, router, ids, slot)


def expert_kernel(parts, tile, *refs):
    inputs, (in_a, in_b, out_a, out_b) = refs[:parts], refs[parts : parts + 4]
    outputs, (rows, total) = refs[parts + 4 : 2 * parts + 4], refs[2 * parts + 4 :]
    span = inputs[0].shape[0]
    for number, part in enumerate(inputs):
        rows[number * span : (number + 1) * span, :] = part[...]
    values = rows[...]
    hidden = in_a.shape[1]

    def step(index, carry):
        units = pl.ds(pl.multiple_of(index * tile, tile), tile)
        result = None
        for first, second in ((in_a, out_a), (in_b, out_b)):
            mid = silu(jnp.dot(values, first[:, units], preferred_element_type=jnp.float32)).astype(jnp.bfloat16)
            term = jnp.dot(mid, second[units, :], preferred_element_type=jnp.float32)
            result = term if result is None else result + term

        @pl.when(index == 0)
        def _():
            total[...] = result

        @pl.when(index > 0)
        def _():
            total[...] += result

        return carry

    lax.fori_loop(0, hidden // tile, step, 0)
    for number, part in enumerate(outputs):
        part[...] = total[number * span : (number + 1) * span, :].astype(jnp.bfloat16)


def run_expert(parts, weights):
    span, width = parts[0].shape
    whole = pl.BlockSpec(memory_space=pltpu.VMEM)
    count = len(parts)
    hidden = weights[0].shape[1]
    return pl.pallas_call(
        functools.partial(expert_kernel, count, min(1024, hidden)),
        in_specs=[whole] * (count + 4),
        out_specs=[whole] * count,
        out_shape=[jax.ShapeDtypeStruct((span, width), jnp.bfloat16)] * count,
        scratch_shapes=[
            pltpu.VMEM((span * count, width), jnp.bfloat16),
            pltpu.VMEM((span * count, width), jnp.float32),
        ],
        compiler_params=pltpu.CompilerParams(vmem_limit_bytes=36 * MIB),
        cost_estimate=pl.CostEstimate(
            flops=8 * span * count * width * hidden, bytes_accessed=8 * width * hidden, transcendentals=0
        ),
        name="expert",
    )(*parts, *weights)


def final_kernel(parts, stream_ref, gate_ref, picking_ref, gain_ref, *refs):
    inputs, out_ref, results = refs[:parts], refs[parts], refs[parts + 1]
    span = inputs[0].shape[0]
    for number, part in enumerate(inputs):
        results[number * span : (number + 1) * span, :] = part[...]
    picked = jnp.dot(picking_ref[...], results[...], preferred_element_type=jnp.float32)
    total = stream_ref[...].astype(jnp.float32) + gate_ref[...] * picked
    out_ref[...] = (normalise(total) * gain_ref[...]).astype(jnp.bfloat16)


def finish(stream, gate, picking, gain, parts):
    length, width = stream.shape
    whole = pl.BlockSpec(memory_space=pltpu.VMEM)
    span = parts[0].shape[0]
    return pl.pallas_call(
        functools.partial(final_kernel, len(parts)),
        in_specs=[whole] * (4 + len(parts)),
        out_specs=whole,
        out_shape=jax.ShapeDtypeStruct((length, width), jnp.bfloat16),
        scratch_shapes=[pltpu.VMEM((span * len(parts), width), jnp.bfloat16)],
        compiler_params=pltpu.CompilerParams(vmem_limit_bytes=24 * MIB),
        name="finish",
    )(stream, gate, picking, gain, *parts)


def on_device(frames, frame_counts, expert_ids, conv_kernel, router, w_in, w_out, final_gain):
    _, length, width = frames.shape
    n_dev = lax.axis_size("expert")
    chips = n_dev // 2
    cap = 2 * ((5 * length + 8 * chips - 1) // (8 * chips))
    me = lax.axis_index("expert") // 2
    other_in = xor_route(w_in, "expert", 1)
    other_out = xor_route(w_out, "expert", 1)
    weights = (w_in, other_in, w_out, other_out)
    ids = expert_ids.reshape(1, length)
    gain = final_gain.reshape(1, width)

    if chips <= 8:
        pitch = -(-cap // 16) * 16
        stream, expert_in, slot, *messages = prepare(
            frames[0], frame_counts, ids ^ me, conv_kernel, chips, cap, pitch, chips
        )
        gate, picking = gate_and_picking(frame_counts, expert_in, router, ids, slot, pitch)
        far = [d for d in range(1, chips) if d >= chips // 2]
        near = [d for d in range(1, chips) if d < chips // 2]
        half = max(1, len(far) // 2)
        arrived = {0: messages[0]}
        for d in far + near:
            arrived[d] = xor_route(messages[d], "expert", 2 * d)
        results = {}
        for batch in (far[:half], far[half:], [0] + near):
            if batch:
                for d, part in zip(batch, run_expert([arrived[d] for d in batch], weights)):
                    results[d] = part if d == 0 else xor_route(part, "expert", 2 * d)
        parts = [results[d] for d in range(chips)]
    else:
        stream, expert_in, slot, message = prepare(frames[0], frame_counts, ids, conv_kernel, chips, cap, cap, 1)
        gate, picking = gate_and_picking(frame_counts, expert_in, router, ids, slot, cap)
        (result,) = run_expert([exchange(message, "expert", chips)], weights)
        parts = [exchange(result, "expert", chips)]
    return finish(stream, gate, picking, gain, parts).reshape(1, length, width)


def solution(mesh):
    return jax.shard_map(
        on_device,
        mesh=mesh,
        in_specs=(
            P(("groups", "expert"), None, None),
            P(("groups", "expert")),
            P(("groups", "expert"), None, None),
            P(),
            P(),
            P(None, "expert"),
            P("expert", None),
            P(),
        ),
        out_specs=P(("groups", "expert"), None, None),
        check_vma=False,
    )
```

time: 97.5 us -> 77.6 us (0.80); the launches traced: 95.9 us -> 77.4 us
  Pallas kernels: 0 us -> 32.6 us
  blocking collectives: 32 us -> 0 us
  starting transfers between devices: 5.59 us -> 30.5 us
  matrix products: 16.6 us -> 0 us
  waiting for transfers between devices: 22.5 us -> 6.2 us
  other arithmetic: 13.2 us -> 0.69 us
  local copies, waits for them, and re-layouts: 5.17 us -> 6.6 us
    pallas_call x0 -> x6, Pallas kernels: none -> 32.6 us  [the longest x3 23.8 us: run_expert(): pl.pallas_call(functools.partial(expert_kernel, count, min(1024, hidden))...]
    all_to_all x1 -> x0, blocking collectives: 32 us -> none  [on_device(): lax.all_to_all(outgoing.reshape(n_dev, half, width), 'expert', split_axis...]
    ppermute x2 -> x16, starting transfers between devices: 0.6 us -> 30.5 us  [xor_route(): return lax.ppermute(block, axis, [(i, i ^ distance) for i in range(count)])]
    all_to_all x1 -> x0, waiting for transfers between devices: 22.5 us -> none  [on_device(): lax.all_to_all(result.reshape(sources, items, width), 'expert', split_axi...]
    dot_general x4 -> x0, matrix products: 16.6 us -> none  [the longest x1 14.7 us: on_device(): jnp.dot(hidden, whole_out, preferred_element_type=jnp.float32)]
    reduce_sum x6 -> x0, other arithmetic: 10.7 us -> none  [the longest x2 9.64 us: layer_norm(): mean = jnp.mean(values, axis=-1, keepdims=True)]
    unnamed x8 -> x19, local copies, waits for them, and re-layouts: 0.38 us -> 6.6 us
    ppermute x2 -> x16, waiting for transfers between devices: 0.01 us -> 6.2 us  [xor_route(): return lax.ppermute(block, axis, [(i, i ^ distance) for i in range(count)])]
  transfers between devices with their start and end apart: 3 -> 16, of which waited for: 1 -> 4; matrix products, arithmetic and copies ran while one was open for 17% -> 1% of each run, Pallas kernels for 0% -> 40%
where the time goes in v1:
time: 77.6 us; the launch traced here: 77.4 us
  Pallas kernels  32.6 us (42%)
  starting transfers between devices  30.5 us (39%)
  local copies, waits for them, and re-layouts  6.6 us (9%)
  waiting for transfers between devices  6.2 us (8%)
    ppermute x16, starting transfers between devices, xor_route(): return lax.ppermute(block, axis, [(i, i ^ distance) for i in range(count)])  30.5 us
    pallas_call x3, Pallas kernels, run_expert(): pl.pallas_call(functools.partial(expert_kernel, count, min(1024, hidden))...  23.8 us
    unnamed x19, local copies, waits for them, and re-layouts  6.6 us
    pallas_call x1, Pallas kernels, prepare(): pl.pallas_call(functools.partial(pre_kernel, cap, pitch), in_specs=[pl.Bl...  6.45 us
    ppermute x16, waiting for transfers between devices, xor_route(): return lax.ppermute(block, axis, [(i, i ^ distance) for i in range(count)])  6.2 us
    pallas_call x1, Pallas kernels, finish(): pl.pallas_call(functools.partial(final_kernel, len(parts)), in_specs=[who...  1.85 us
  transfers between devices with their start and end apart: 16, of which 4 were waited for; matrix products, arithmetic and copies ran while one was open for 1% of the time, Pallas kernels for 40%

profile of v1, /device:TPU:0, one launch (start us, length us, event | category | flops | bytes accessed | tf_op | source)
XLA Modules:
  0.0 77.4 jit_solution(9071291350774378549)
XLA Ops:
  0.0 0.5 collective-permute-start.3
  0.5 0.1 collective-permute-start.4
  1.2 0.7 broadcast_xor_fusion.ids_ref
  1.9 0.0 copy-start.6
  1.9 1.1 %copy-done.6 = bf16[1,384,1024]{2,1,0:T(8,128)(2,1)S(1)} copy-done((bf16[1,384,1024]{2,1,0:T(8,128)(2,1)S(1)}, bf16[1,384,1024]{2,1,0:T(8,128)(2,1)}, u32[]{:S(2)}) %copy-start.6) | copy-done | bytes 786456
  3.0 0.0 copy-start.7
  3.0 0.9 %copy-done.7 = f32[31,1024]{1,0:T(8,128)S(1)} copy-done((f32[31,1024]{1,0:T(8,128)S(1)}, f32[31,1024]{1,0:T(8,128)}, u32[]{:S(2)}) %copy-start.7) | copy-done | bytes 127000
  3.9 6.4 %prepare.1 = (bf16[384,1024]{1,0:T(8,128)(2,1)S(1)}, bf16[384,1024]{1,0:T(8,128)(2,1)S(1)}, s32[8,384]{1,0:T(8,128)S(1)}, bf16[64,1024]{1,0:T(8,128)(2,1)S(1)}, ...) custom-call(s32[1]{0:T(128)S(6)} %copy.10.count_ref, ...), custom_call_target="tpu_custom_call" | custom-call | flops 400000000 | bytes 4000000 | tf_op jit(solution)/shard_map/prepare/pallas_call | solution.py:119
  10.3 5.1 %collective-permute-start.12 = (bf16[64,1024]{1,0:T(8,128)(2,1)S(1)}, bf16[64,1024]{1,0:T(8,128)(2,1)S(1)}, u32[]{:S(2)}, u32[]{:S(2)}) collective-permute-start(bf16[64,1024]{1,0:T(8,128)(2,1)S(1)} %get-tuple-element.43), channel_id=1, source_target_pairs={{0,12},{1,13},{2,14},{3,15},{4,8},{5,9},{6,10},{7,11},{8,4},{9,5},... | collective-permute-start | bytes 393224 | tf_op jit(solution)/shard_map/ppermute | solution.py:19
  15.5 1.2 %collective-permute-start.13 = (bf16[64,1024]{1,0:T(8,128)(2,1)S(1)}, bf16[64,1024]{1,0:T(8,128)(2,1)S(1)}, u32[]{:S(2)}, u32[]{:S(2)}) collective-permute-start(bf16[64,1024]{1,0:T(8,128)(2,1)S(1)} %get-tuple-element.44), channel_id=1, source_target_pairs={{0,14},{1,15},{2,12},{3,13},{4,10},{5,11},{6,8},{7,9},{8,6},{9,7},... | collective-permute-start | bytes 393224 | tf_op jit(solution)/shard_map/ppermute | solution.py:19
  16.6 0.4 collective-permute-start
  17.0 2.4 %collective-permute-done.12.refs_0_ = bf16[64,1024]{1,0:T(8,128)(2,1)S(1)} collective-permute-done((bf16[64,1024]{1,0:T(8,128)(2,1)S(1)}, bf16[64,1024]{1,0:T(8,128)(2,1)S(1)}, u32[]{:S(2)}, u32[]{:S(2)}) %collective-permute-start.12) | collective-permute-done | bytes 131104 | tf_op jit(solution)/shard_map/ppermute | solution.py:19
  19.4 6.0 %collective-permute-start.1 = (bf16[64,1024]{1,0:T(8,128)(2,1)S(1)}, bf16[64,1024]{1,0:T(8,128)(2,1)S(1)}, u32[]{:S(2)}, u32[]{:S(2)}) collective-permute-start(bf16[64,1024]{1,0:T(8,128)(2,1)S(1)} %get-tuple-element.33), channel_id=1, source_target_pairs={{0,4},{1,5},{2,6},{3,7},{4,0},{5,1},{6,2},{7,3},{8,12},{9,13},{10,... | collective-permute-start | bytes 393224 | tf_op jit(solution)/shard_map/ppermute | solution.py:19
  25.4 0.0 collective-permute-done.13.refs_1_
  25.4 2.8 %collective-permute-start.2 = (bf16[64,1024]{1,0:T(8,128)(2,1)S(1)}, bf16[64,1024]{1,0:T(8,128)(2,1)S(1)}, u32[]{:S(2)}, u32[]{:S(2)}) collective-permute-start(bf16[64,1024]{1,0:T(8,128)(2,1)S(1)} %get-tuple-element.34), channel_id=1, source_target_pairs={{0,6},{1,7},{2,4},{3,5},{4,2},{5,3},{6,0},{7,1},{8,14},{9,15},{10,... | collective-permute-start | bytes 393224 | tf_op jit(solution)/shard_map/ppermute | solution.py:19
  28.2 0.0 collective-permute-done.3.refs_5_.refs_3_
  28.2 1.3 %collective-permute-start.8 = (bf16[64,1024]{1,0:T(8,128)(2,1)S(1)}, bf16[64,1024]{1,0:T(8,128)(2,1)S(1)}, u32[]{:S(2)}, u32[]{:S(2)}) collective-permute-start(bf16[64,1024]{1,0:T(8,128)(2,1)S(1)} %get-tuple-element.39), channel_id=1, source_target_pairs={{0,8},{1,9},{2,10},{3,11},{4,12},{5,13},{6,14},{7,15},{8,0},{9,1},... | collective-permute-start | bytes 393224 | tf_op jit(solution)/shard_map/ppermute | solution.py:19
  29.4 0.0 collective-permute-done.4.refs_7_.refs_5_
  29.4 2.6 %collective-permute-start.9 = (bf16[64,1024]{1,0:T(8,128)(2,1)S(1)}, bf16[64,1024]{1,0:T(8,128)(2,1)S(1)}, u32[]{:S(2)}, u32[]{:S(2)}) collective-permute-start(bf16[64,1024]{1,0:T(8,128)(2,1)S(1)} %get-tuple-element.40), channel_id=1, source_target_pairs={{0,10},{1,11},{2,8},{3,9},{4,14},{5,15},{6,12},{7,13},{8,2},{9,3},... | collective-permute-start | bytes 393224 | tf_op jit(solution)/shard_map/ppermute | solution.py:19
  32.1 0.0 copy-start
  32.1 2.2 %copy-done = bf16[1024,2048]{1,0:T(8,128)(2,1)S(1)} copy-done((bf16[1024,2048]{1,0:T(8,128)(2,1)S(1)}, bf16[1024,2048]{1,0:T(8,128)(2,1)}, u32[]{:S(2)}) %copy-start) | copy-done | bytes 4194328
  34.2 0.0 copy-start.2
  34.2 2.2 %copy-done.2 = bf16[2048,1024]{1,0:T(8,128)(2,1)S(1)} copy-done((bf16[2048,1024]{1,0:T(8,128)(2,1)S(1)}, bf16[2048,1024]{1,0:T(8,128)(2,1)}, u32[]{:S(2)}) %copy-start.2) | copy-done | bytes 4194328
  36.4 7.0 %expert.5 = (bf16[64,1024]{1,0:T(8,128)(2,1)}, bf16[64,1024]{1,0:T(8,128)(2,1)S(1)}) custom-call(bf16[64,1024]{1,0:T(8,128)(2,1)S(1)} %collective-permute-done.12.refs_0_, bf16[64,1024]{1,0:T(8,128)(2,1)S(1)} %collective-permute-done.13.refs_1_, bf16[1024,2048]{1,0:T(8,128)(2,1)S(1)} %copy-done, bf16[1024,2048]{1,0:T(8,128)(2,1)} %collective-permute-done.3.refs_5_.refs_3_, ...), custom_call_target="tpu_custom_call" | custom-call | flops 2147483648 | bytes 16777216 | tf_op jit(solution)/shard_map/expert/pallas_call | solution.py:209
  43.4 0.0 collective-permute-done.8.refs_0_
  43.4 2.5 %collective-permute-start.14 = (bf16[64,1024]{1,0:T(8,128)(2,1)}, bf16[64,1024]{1,0:T(8,128)(2,1)S(1)}, u32[]{:S(2)}, u32[]{:S(2)}) collective-permute-start(bf16[64,1024]{1,0:T(8,128)(2,1)} %get-tuple-element.45), channel_id=1, source_target_pairs={{0,12},{1,13},{2,14},{3,15},{4,8},{5,9},{6,10},{7,11},{8,4},{9,5},... | collective-permute-start | bytes 393224 | tf_op jit(solution)/shard_map/ppermute | solution.py:19
  45.9 0.0 collective-permute-done.9.refs_1_
  45.9 0.0 copy-start.1
  45.9 0.0 copy-start.3
  45.9 1.3 %collective-permute-start.15 = (bf16[64,1024]{1,0:T(8,128)(2,1)S(1)}, bf16[64,1024]{1,0:T(8,128)(2,1)S(1)}, u32[]{:S(2)}, u32[]{:S(2)}) collective-permute-start(bf16[64,1024]{1,0:T(8,128)(2,1)S(1)} %get-tuple-element.46), channel_id=1, source_target_pairs={{0,14},{1,15},{2,12},{3,13},{4,10},{5,11},{6,8},{7,9},{8,6},{9,7},... | collective-permute-start | bytes 393224 | tf_op jit(solution)/shard_map/ppermute | solution.py:19
  47.2 7.6 %expert.4 = (bf16[64,1024]{1,0:T(8,128)(2,1)}, bf16[64,1024]{1,0:T(8,128)(2,1)S(1)}) custom-call(bf16[64,1024]{1,0:T(8,128)(2,1)S(1)} %collective-permute-done.8.refs_0_, bf16[64,1024]{1,0:T(8,128)(2,1)S(1)} %collective-permute-done.9.refs_1_, bf16[1024,2048]{1,0:T(8,128)(2,1)S(1)} %copy-done, bf16[1024,2048]{1,0:T(8,128)(2,1)} %collective-permute-done.3.refs_5_.refs_3_, ...), custom_call_target="tpu_custom_call" | custom-call | flops 2147483648 | bytes 16777216 | tf_op jit(solution)/shard_map/expert/pallas_call | solution.py:209
  54.8 0.0 collective-permute-done.refs_1_
  54.8 0.0 collective-permute-start.10
  54.8 0.0 collective-permute-done.1.refs_2_
  54.8 3.4 %collective-permute-start.11 = (bf16[64,1024]{1,0:T(8,128)(2,1)S(1)}, bf16[64,1024]{1,0:T(8,128)(2,1)S(1)}, u32[]{:S(2)}, u32[]{:S(2)}) collective-permute-start(bf16[64,1024]{1,0:T(8,128)(2,1)S(1)} %get-tuple-element.42), channel_id=1, source_target_pairs={{0,10},{1,11},{2,8},{3,9},{4,14},{5,15},{6,12},{7,13},{8,2},{9,3},... | collective-permute-start | bytes 393224 | tf_op jit(solution)/shard_map/ppermute | solution.py:19
  58.2 0.0 collective-permute-done.2.refs_3_
  58.2 0.0 copy-done.1
  58.2 0.0 copy-done.3
  58.3 0.0 copy-start.8
  58.3 0.0 copy-start.4
  58.3 0.0 copy-start.5
  58.3 9.2 %expert.3 = (bf16[64,1024]{1,0:T(8,128)(2,1)S(1)}, bf16[64,1024]{1,0:T(8,128)(2,1)}, bf16[64,1024]{1,0:T(8,128)(2,1)}, bf16[64,1024]{1,0:T(8,128)(2,1)}) custom-call(bf16[64,1024]{1,0:T(8,128)(2,1)S(1)} %get-tuple-element.31.refs_0_, bf16[64,1024]{1,0:T(8,128)(2,1)S(1)} %collective-permute-done.refs_1_, bf16[64,1024]{1,0:T(8,128)(2,1)S(1)} %collective-permute-done.1.refs_2_, ...), custom_call_target="tpu_custom_call" | custom-call | flops 4294967296 | bytes 16777216 | tf_op jit(solution)/shard_map/expert/pallas_call | solution.py:209
  67.5 1.0 %collective-permute-start.5 = (bf16[64,1024]{1,0:T(8,128)(2,1)}, bf16[64,1024]{1,0:T(8,128)(2,1)S(1)}, u32[]{:S(2)}, u32[]{:S(2)}) collective-permute-start(bf16[64,1024]{1,0:T(8,128)(2,1)} %get-tuple-element.36), channel_id=1, source_target_pairs={{0,2},{1,3},{2,0},{3,1},{4,6},{5,7},{6,4},{7,5},{8,10},{9,11},{10,... | collective-permute-start | bytes 393224 | tf_op jit(solution)/shard_map/ppermute | solution.py:19
  68.4 0.0 collective-permute-done.14.refs_6_
  68.4 0.0 collective-permute-start.6
  68.4 0.0 collective-permute-done.15.refs_7_
  68.4 2.5 %collective-permute-start.7 = (bf16[64,1024]{1,0:T(8,128)(2,1)}, bf16[64,1024]{1,0:T(8,128)(2,1)S(1)}, u32[]{:S(2)}, u32[]{:S(2)}) collective-permute-start(bf16[64,1024]{1,0:T(8,128)(2,1)} %get-tuple-element.38), channel_id=1, source_target_pairs={{0,6},{1,7},{2,4},{3,5},{4,2},{5,3},{6,0},{7,1},{8,14},{9,15},{10,... | collective-permute-start | bytes 393224 | tf_op jit(solution)/shard_map/ppermute | solution.py:19
  71.0 0.0 copy-done.8
  71.0 0.2 copy.9.router_ref
  71.2 0.0 copy-done.4
  71.2 0.6 gate.1
  71.7 0.0 collective-permute-done.10.refs_4_
  71.7 0.0 collective-permute-done.11.refs_5_
  71.7 1.4 %collective-permute-done.5.refs_1_ = bf16[64,1024]{1,0:T(8,128)(2,1)S(1)} collective-permute-done((bf16[64,1024]{1,0:T(8,128)(2,1)}, bf16[64,1024]{1,0:T(8,128)(2,1)S(1)}, u32[]{:S(2)}, u32[]{:S(2)}) %collective-permute-start.5) | collective-permute-done | bytes 131104 | tf_op jit(solution)/shard_map/ppermute | solution.py:19
  73.2 0.5 collective-permute-done.6.refs_2_
  73.6 1.9 %collective-permute-done.7.refs_3_ = bf16[64,1024]{1,0:T(8,128)(2,1)S(1)} collective-permute-done((bf16[64,1024]{1,0:T(8,128)(2,1)}, bf16[64,1024]{1,0:T(8,128)(2,1)S(1)}, u32[]{:S(2)}, u32[]{:S(2)}) %collective-permute-start.7) | collective-permute-done | bytes 131104 | tf_op jit(solution)/shard_map/ppermute | solution.py:19
  75.5 0.0 copy-done.5
  75.5 1.8 %finish.1 = bf16[384,1024]{1,0:T(8,128)(2,1)} custom-call(bf16[384,1024]{1,0:T(8,128)(2,1)S(1)} %get-tuple-element.26.stream_ref, f32[384,1]{1,0:T(8,128)S(1)} %get-tuple-element.29.gate_ref, bf16[384,512]{1,0:T(8,128)(2,1)S(1)} %get-tuple-element.30.picking_ref, f32[1,1024]{1,0:T(1,128)S(1)} %bitcast.6, bf16[64,1024]{1,0:T(8,128)(2,1)S(1)} %get-tuple-element.35.refs_0_, ...), custom_call_target="tpu_custom_call" | custom-call | tf_op jit(solution)/shard_map/finish/pallas_call | solution.py:240
Async XLA Ops:
  0.0 28.2 %collective-permute-start.3 = (bf16[1024,2048]{1,0:T(8,128)(2,1)}, bf16[1024,2048]{1,0:T(8,128)(2,1)}, u32[]{:S(2)}, u32[]{:S(2)}) collective-permute-start(bf16[1024,2048]{1,0:T(8,128)(2,1)} %refs_2_.3), channel_id=1, source_target_pairs={{0,1},{1,0},{2,3},{3,2},{4,5},{5,4},{6,7},{7,6},{8,9},{9,8},{10,11... | collective-permute-start | bytes 12582920 | tf_op jit(solution)/shard_map/ppermute | solution.py:19
  0.5 29.0 %collective-permute-start.4 = (bf16[2048,1024]{1,0:T(8,128)(2,1)}, bf16[2048,1024]{1,0:T(8,128)(2,1)}, u32[]{:S(2)}, u32[]{:S(2)}) collective-permute-start(bf16[2048,1024]{1,0:T(8,128)(2,1)} %refs_4_.5), channel_id=1, source_target_pairs={{0,1},{1,0},{2,3},{3,2},{4,5},{5,4},{6,7},{7,6},{8,9},{9,8},{10,11... | collective-permute-start | bytes 12582920 | tf_op jit(solution)/shard_map/ppermute | solution.py:19
  1.9 1.1 %copy-start.6 = (bf16[1,384,1024]{2,1,0:T(8,128)(2,1)S(1)}, bf16[1,384,1024]{2,1,0:T(8,128)(2,1)}, u32[]{:S(2)}) copy-start(bf16[1,384,1024]{2,1,0:T(8,128)(2,1)} %param.8) | copy-start | bytes 2359300
  3.0 0.9 %copy-start.7 = (f32[31,1024]{1,0:T(8,128)S(1)}, f32[31,1024]{1,0:T(8,128)}, u32[]{:S(2)}) copy-start(f32[31,1024]{1,0:T(8,128)} %taps_ref.1) | copy-start | bytes 380932
  10.3 9.0 %collective-permute-start.12 = (bf16[64,1024]{1,0:T(8,128)(2,1)S(1)}, bf16[64,1024]{1,0:T(8,128)(2,1)S(1)}, u32[]{:S(2)}, u32[]{:S(2)}) collective-permute-start(bf16[64,1024]{1,0:T(8,128)(2,1)S(1)} %get-tuple-element.43), channel_id=1, source_target_pairs={{0,12},{1,13},{2,14},{3,15},{4,8},{5,9},{6,10},{7,11},{8,4},{9,5},... | collective-permute-start | bytes 393224 | tf_op jit(solution)/shard_map/ppermute | solution.py:19
  15.5 9.9 %collective-permute-start.13 = (bf16[64,1024]{1,0:T(8,128)(2,1)S(1)}, bf16[64,1024]{1,0:T(8,128)(2,1)S(1)}, u32[]{:S(2)}, u32[]{:S(2)}) collective-permute-start(bf16[64,1024]{1,0:T(8,128)(2,1)S(1)} %get-tuple-element.44), channel_id=1, source_target_pairs={{0,14},{1,15},{2,12},{3,13},{4,10},{5,11},{6,8},{7,9},{8,6},{9,7},... | collective-permute-start | bytes 393224 | tf_op jit(solution)/shard_map/ppermute | solution.py:19
  16.6 38.2 %collective-permute-start = (bf16[64,1024]{1,0:T(8,128)(2,1)S(1)}, bf16[64,1024]{1,0:T(8,128)(2,1)S(1)}, u32[]{:S(2)}, u32[]{:S(2)}) collective-permute-start(bf16[64,1024]{1,0:T(8,128)(2,1)S(1)} %get-tuple-element.32), channel_id=1, source_target_pairs={{0,2},{1,3},{2,0},{3,1},{4,6},{5,7},{6,4},{7,5},{8,10},{9,11},{10,... | collective-permute-start | bytes 393224 | tf_op jit(solution)/shard_map/ppermute | solution.py:19
  19.4 35.4 %collective-permute-start.1 = (bf16[64,1024]{1,0:T(8,128)(2,1)S(1)}, bf16[64,1024]{1,0:T(8,128)(2,1)S(1)}, u32[]{:S(2)}, u32[]{:S(2)}) collective-permute-start(bf16[64,1024]{1,0:T(8,128)(2,1)S(1)} %get-tuple-element.33), channel_id=1, source_target_pairs={{0,4},{1,5},{2,6},{3,7},{4,0},{5,1},{6,2},{7,3},{8,12},{9,13},{10,... | collective-permute-start | bytes 393224 | tf_op jit(solution)/shard_map/ppermute | solution.py:19
  25.4 32.8 %collective-permute-start.2 = (bf16[64,1024]{1,0:T(8,128)(2,1)S(1)}, bf16[64,1024]{1,0:T(8,128)(2,1)S(1)}, u32[]{:S(2)}, u32[]{:S(2)}) collective-permute-start(bf16[64,1024]{1,0:T(8,128)(2,1)S(1)} %get-tuple-element.34), channel_id=1, source_target_pairs={{0,6},{1,7},{2,4},{3,5},{4,2},{5,3},{6,0},{7,1},{8,14},{9,15},{10,... | collective-permute-start | bytes 393224 | tf_op jit(solution)/shard_map/ppermute | solution.py:19
  28.2 15.3 %collective-permute-start.8 = (bf16[64,1024]{1,0:T(8,128)(2,1)S(1)}, bf16[64,1024]{1,0:T(8,128)(2,1)S(1)}, u32[]{:S(2)}, u32[]{:S(2)}) collective-permute-start(bf16[64,1024]{1,0:T(8,128)(2,1)S(1)} %get-tuple-element.39), channel_id=1, source_target_pairs={{0,8},{1,9},{2,10},{3,11},{4,12},{5,13},{6,14},{7,15},{8,0},{9,1},... | collective-permute-start | bytes 393224 | tf_op jit(solution)/shard_map/ppermute | solution.py:19
  29.4 16.5 %collective-permute-start.9 = (bf16[64,1024]{1,0:T(8,128)(2,1)S(1)}, bf16[64,1024]{1,0:T(8,128)(2,1)S(1)}, u32[]{:S(2)}, u32[]{:S(2)}) collective-permute-start(bf16[64,1024]{1,0:T(8,128)(2,1)S(1)} %get-tuple-element.40), channel_id=1, source_target_pairs={{0,10},{1,11},{2,8},{3,9},{4,14},{5,15},{6,12},{7,13},{8,2},{9,3},... | collective-permute-start | bytes 393224 | tf_op jit(solution)/shard_map/ppermute | solution.py:19
  32.1 2.2 %copy-start = (bf16[1024,2048]{1,0:T(8,128)(2,1)S(1)}, bf16[1024,2048]{1,0:T(8,128)(2,1)}, u32[]{:S(2)}) copy-start(bf16[1024,2048]{1,0:T(8,128)(2,1)} %refs_2_.3) | copy-start | bytes 12582916
  34.2 2.2 %copy-start.2 = (bf16[2048,1024]{1,0:T(8,128)(2,1)S(1)}, bf16[2048,1024]{1,0:T(8,128)(2,1)}, u32[]{:S(2)}) copy-start(bf16[2048,1024]{1,0:T(8,128)(2,1)} %refs_4_.5) | copy-start | bytes 12582916
  43.4 25.0 %collective-permute-start.14 = (bf16[64,1024]{1,0:T(8,128)(2,1)}, bf16[64,1024]{1,0:T(8,128)(2,1)S(1)}, u32[]{:S(2)}, u32[]{:S(2)}) collective-permute-start(bf16[64,1024]{1,0:T(8,128)(2,1)} %get-tuple-element.45), channel_id=1, source_target_pairs={{0,12},{1,13},{2,14},{3,15},{4,8},{5,9},{6,10},{7,11},{8,4},{9,5},... | collective-permute-start | bytes 393224 | tf_op jit(solution)/shard_map/ppermute | solution.py:19
  45.9 12.3 %copy-start.1 = (bf16[1024,2048]{1,0:T(8,128)(2,1)S(1)}, bf16[1024,2048]{1,0:T(8,128)(2,1)}, u32[]{:S(2)}) copy-start(bf16[1024,2048]{1,0:T(8,128)(2,1)} %refs_2_.3) | copy-start | bytes 12582916
  45.9 12.3 %copy-start.3 = (bf16[2048,1024]{1,0:T(8,128)(2,1)S(1)}, bf16[2048,1024]{1,0:T(8,128)(2,1)}, u32[]{:S(2)}) copy-start(bf16[2048,1024]{1,0:T(8,128)(2,1)} %refs_4_.5) | copy-start | bytes 12582916
  45.9 22.5 %collective-permute-start.15 = (bf16[64,1024]{1,0:T(8,128)(2,1)S(1)}, bf16[64,1024]{1,0:T(8,128)(2,1)S(1)}, u32[]{:S(2)}, u32[]{:S(2)}) collective-permute-start(bf16[64,1024]{1,0:T(8,128)(2,1)S(1)} %get-tuple-element.46), channel_id=1, source_target_pairs={{0,14},{1,15},{2,12},{3,13},{4,10},{5,11},{6,8},{7,9},{8,6},{9,7},... | collective-permute-start | bytes 393224 | tf_op jit(solution)/shard_map/ppermute | solution.py:19
  54.8 16.9 %collective-permute-start.10 = (bf16[64,1024]{1,0:T(8,128)(2,1)}, bf16[64,1024]{1,0:T(8,128)(2,1)S(1)}, u32[]{:S(2)}, u32[]{:S(2)}) collective-permute-start(bf16[64,1024]{1,0:T(8,128)(2,1)} %get-tuple-element.41), channel_id=1, source_target_pairs={{0,8},{1,9},{2,10},{3,11},{4,12},{5,13},{6,14},{7,15},{8,0},{9,1},... | collective-permute-start | bytes 393224 | tf_op jit(solution)/shard_map/ppermute | solution.py:19
  54.8 16.9 %collective-permute-start.11 = (bf16[64,1024]{1,0:T(8,128)(2,1)S(1)}, bf16[64,1024]{1,0:T(8,128)(2,1)S(1)}, u32[]{:S(2)}, u32[]{:S(2)}) collective-permute-start(bf16[64,1024]{1,0:T(8,128)(2,1)S(1)} %get-tuple-element.42), channel_id=1, source_target_pairs={{0,10},{1,11},{2,8},{3,9},{4,14},{5,15},{6,12},{7,13},{8,2},{9,3},... | collective-permute-start | bytes 393224 | tf_op jit(solution)/shard_map/ppermute | solution.py:19
  58.3 12.7 %copy-start.8 = (bf16[1024,8]{0,1:T(8,128)(2,1)S(1)}, bf16[1024,8]{0,1:T(8,128)(2,1)}, u32[]{:S(2)}) copy-start(bf16[1024,8]{0,1:T(8,128)(2,1)} %param.12) | copy-start | bytes 49156
  58.3 12.9 %copy-start.4 = (s32[1,384,1]{1,2,0:T(1,128)S(1)}, s32[1,384,1]{1,2,0:T(1,128)}, u32[]{:S(2)}) copy-start(s32[1,384,1]{1,2,0:T(1,128)} %param.10) | copy-start | bytes 4612
  58.3 17.2 %copy-start.5 = (f32[1024]{0:T(1024)S(1)}, f32[1024]{0:T(1024)}, u32[]{:S(2)}) copy-start(f32[1024]{0:T(1024)} %param.15) | copy-start | bytes 12292
  67.5 5.7 %collective-permute-start.5 = (bf16[64,1024]{1,0:T(8,128)(2,1)}, bf16[64,1024]{1,0:T(8,128)(2,1)S(1)}, u32[]{:S(2)}, u32[]{:S(2)}) collective-permute-start(bf16[64,1024]{1,0:T(8,128)(2,1)} %get-tuple-element.36), channel_id=1, source_target_pairs={{0,2},{1,3},{2,0},{3,1},{4,6},{5,7},{6,4},{7,5},{8,10},{9,11},{10,... | collective-permute-start | bytes 393224 | tf_op jit(solution)/shard_map/ppermute | solution.py:19
  68.4 5.2 %collective-permute-start.6 = (bf16[64,1024]{1,0:T(8,128)(2,1)}, bf16[64,1024]{1,0:T(8,128)(2,1)S(1)}, u32[]{:S(2)}, u32[]{:S(2)}) collective-permute-start(bf16[64,1024]{1,0:T(8,128)(2,1)} %get-tuple-element.37), channel_id=1, source_target_pairs={{0,4},{1,5},{2,6},{3,7},{4,0},{5,1},{6,2},{7,3},{8,12},{9,13},{10,... | collective-permute-start | bytes 393224 | tf_op jit(solution)/shard_map/ppermute | solution.py:19
  68.4 7.1 %collective-permute-start.7 = (bf16[64,1024]{1,0:T(8,128)(2,1)}, bf16[64,1024]{1,0:T(8,128)(2,1)S(1)}, u32[]{:S(2)}, u32[]{:S(2)}) collective-permute-start(bf16[64,1024]{1,0:T(8,128)(2,1)} %get-tuple-element.38), channel_id=1, source_target_pairs={{0,6},{1,7},{2,4},{3,5},{4,2},{5,3},{6,0},{7,1},{8,14},{9,15},{10,... | collective-permute-start | bytes 393224 | tf_op jit(solution)/shard_map/ppermute | solution.py:19

commit v2 on v1

--- a/solution.py
+++ b/solution.py
@@ -11,12 +11,17 @@
 ROWS = 8
 BLOCK = 64
 EPS = 1e-05
+SMALL = pl.CostEstimate(flops=1, bytes_accessed=1, transcendentals=0)
 MIB = 1 << 20
 
 
 def xor_route(block, axis, distance):
     count = lax.axis_size(axis)
     return lax.ppermute(block, axis, [(i, i ^ distance) for i in range(count)])
+
+
+def after(values, earlier):
+    return lax.optimization_barrier((values, earlier))[0]
 
 
 def exchange(block, axis, chips):
@@ -27,6 +32,10 @@
     return moved.reshape(block.shape)
 
 
+def in_hbm(array):
+    return pltpu.with_memory_space_constraint(array, pltpu.HBM)
+
+
 def silu(value):
     return value / (1.0 + jnp.exp(-value))
 
@@ -38,27 +47,48 @@
     return centred * lax.rsqrt(variance + EPS)
 
 
-def pre_kernel(cap, pitch, count_ref, frames_ref, ids_ref, taps_ref, stream_ref, expert_in_ref, slot_ref, *rest):
-    *message_refs, padded, taps_by_row, conv = rest
+def pre_kernel(cap, pitch, count_ref, me_ref, frames_hbm, ids_ref, taps_hbm, in_hbm, out_hbm, *rest):
+    in_ref, out_ref, stream_ref, expert_in_ref, slot_ref, *rest = rest
+    *message_refs, frames_ref, taps_ref, padded, taps_by_row, conv, frame_sems, taps_sem, weight_sems = rest
     length, width = frames_ref.shape
     taps = taps_ref.shape[0]
     reach = taps // 2
     groups = width // LANES
     count = count_ref[0]
 
-    for group in range(groups):
-        lanes = slice(group * LANES, (group + 1) * LANES)
-        taps_by_row[pl.ds(group, taps, stride=groups), :] = taps_ref[:, lanes]
+    frame_copies = [
+        pltpu.make_async_copy(
+            frames_hbm.at[0, pl.ds(start, BLOCK), :], frames_ref.at[pl.ds(start, BLOCK), :], frame_sems.at[number]
+        )
+        for number, start in enumerate(range(0, length, BLOCK))
+    ]
+    taps_copy = pltpu.make_async_copy(taps_hbm, taps_ref, taps_sem)
+    for copy in frame_copies:
+        copy.start()
+    taps_copy.start()
+    weight_copies = [
+        pltpu.make_async_copy(in_hbm, in_ref, weight_sems.at[0]),
+        pltpu.make_async_copy(out_hbm, out_ref, weight_sems.at[1]),
+    ]
+    for copy in weight_copies:
+        copy.start()
+
     edge = jnp.zeros((reach * groups, LANES), jnp.float32)
     padded[: reach * groups, :] = edge
     padded[(reach + length) * groups :, :] = edge
-    for start in range(0, length, BLOCK):
+    for number, start in enumerate(range(0, length, BLOCK)):
+        frame_copies[number].wait()
         values = frames_ref[start : start + BLOCK, :].astype(jnp.float32)
         position = start + lax.broadcasted_iota(jnp.int32, (BLOCK, 1), 0)
         normed = jnp.where(position < count, normalise(values), 0.0)
         for group in range(groups):
             lanes = slice(group * LANES, (group + 1) * LANES)
             padded[pl.ds((reach + start) * groups + group, BLOCK, stride=groups), :] = normed[:, lanes]
+
+    taps_copy.wait()
+    for group in range(groups):
+        lanes = slice(group * LANES, (group + 1) * LANES)
+        taps_by_row[pl.ds(group, taps, stride=groups), :] = taps_ref[:, lanes]
 
     def convolve(index, carry):
         base = pl.multiple_of(index * (ROWS * groups), ROWS * groups)
@@ -85,7 +115,7 @@
         expert_in_ref[rows, :] = normalise(stream.astype(jnp.float32)).astype(jnp.bfloat16)
 
     chips = slot_ref.shape[0]
-    ids = ids_ref[...]
+    ids = ids_ref[...] ^ me_ref[0]
     at = lax.broadcasted_iota(jnp.int32, (chips, length), 1)
     chosen = (ids == lax.broadcasted_iota(jnp.int32, (chips, length), 0)) & (at < count)
     earlier = lax.broadcasted_iota(jnp.int32, (length, length), 0) < lax.broadcasted_iota(
@@ -107,34 +137,67 @@
         placed = placed.astype(jnp.bfloat16)
         for number, message in enumerate(message_refs):
             message[:, columns] = placed[number * span : (number + 1) * span, :]
-
-
-def prepare(frames, count, ids, taps, chips, cap, pitch, messages):
-    length, width = frames.shape
+    for copy in weight_copies:
+        copy.wait()
+
+
+def prepare(frames, count, me, ids, taps, w_in, w_out, chips, cap, pitch, messages):
+    _, length, width = frames.shape
     groups = width // LANES
     reach = taps.shape[0] // 2
     whole = pl.BlockSpec(memory_space=pltpu.VMEM)
+    anywhere = pl.BlockSpec(memory_space=pl.ANY)
     span = chips * pitch // messages
     bf16 = jnp.bfloat16
     return pl.pallas_call(
         functools.partial(pre_kernel, cap, pitch),
-        in_specs=[pl.BlockSpec(memory_space=pltpu.SMEM), whole, whole, whole],
-        out_specs=[whole] * (3 + messages),
+        in_specs=[pl.BlockSpec(memory_space=pltpu.SMEM)] * 2 + [anywhere, whole] + [anywhere] * 3,
+        out_specs=[whole] * (5 + messages),
         out_shape=[
+            pltpu.VMEM(w_in.shape, bf16),
+            pltpu.VMEM(w_out.shape, bf16),
             jax.ShapeDtypeStruct((length, width), bf16),
             jax.ShapeDtypeStruct((length, width), bf16),
             jax.ShapeDtypeStruct((chips, length), jnp.int32),
         ]
         + [jax.ShapeDtypeStruct((span, width), bf16)] * messages,
         scratch_shapes=[
+            pltpu.VMEM((length, width), bf16),
+            pltpu.VMEM(taps.shape, jnp.float32),
             pltpu.VMEM(((length + 2 * reach) * groups, LANES), jnp.float32),
             pltpu.VMEM((taps.shape[0] * groups, LANES), jnp.float32),
             pltpu.VMEM((length * groups, LANES), jnp.float32),
+            pltpu.SemaphoreType.DMA((length // BLOCK,)),
+            pltpu.SemaphoreType.DMA,
+            pltpu.SemaphoreType.DMA((2,)),
         ],
         compiler_params=pltpu.CompilerParams(vmem_limit_bytes=24 * MIB),
-        cost_estimate=pl.CostEstimate(flops=4 * 10**8, bytes_accessed=4 * 10**6, transcendentals=0),
+        cost_estimate=SMALL,
         name="prepare",
-    )(count, frames, ids, taps)
+    )(count, me, in_hbm(frames), ids, in_hbm(taps), in_hbm(w_in), in_hbm(w_out))
+
+
+def load_kernel(count, *refs):
+    sources, targets, sems = refs[:count], refs[count : 2 * count], refs[2 * count]
+    copies = [pltpu.make_async_copy(a, b, sems.at[i]) for i, (a, b) in enumerate(zip(sources, targets))]
+    for copy in copies:
+        copy.start()
+    for copy in copies:
+        copy.wait()
+
+
+def load(*arrays):
+    count = len(arrays)
+    return pl.pallas_call(
+        functools.partial(load_kernel, count),
+        in_specs=[pl.BlockSpec(memory_space=pl.ANY)] * count,
+        out_specs=[pl.BlockSpec(memory_space=pltpu.VMEM)] * count,
+        out_shape=[pltpu.VMEM(array.shape, array.dtype) for array in arrays],
+        scratch_shapes=[pltpu.SemaphoreType.DMA((count,))],
+        compiler_params=pltpu.CompilerParams(vmem_limit_bytes=4 * MIB),
+        cost_estimate=SMALL,
+        name="load",
+    )(*[in_hbm(array) for array in arrays])
 
 
 def gate_kernel(pitch, count_ref, expert_in_ref, router_ref, ids_ref, slot_ref, gate_ref, picking_ref):
@@ -165,6 +228,7 @@
             jax.ShapeDtypeStruct((length, slots), jnp.bfloat16),
         ],
         compiler_params=pltpu.CompilerParams(vmem_limit_bytes=12 * MIB),
+        cost_estimate=SMALL,
         name="gate",
     )(count, expert_in, router, ids, slot)
 
@@ -215,37 +279,49 @@
             pltpu.VMEM((span * count, width), jnp.bfloat16),
             pltpu.VMEM((span * count, width), jnp.float32),
         ],
-        compiler_params=pltpu.CompilerParams(vmem_limit_bytes=36 * MIB),
-        cost_estimate=pl.CostEstimate(
-            flops=8 * span * count * width * hidden, bytes_accessed=8 * width * hidden, transcendentals=0
-        ),
+        compiler_params=pltpu.CompilerParams(vmem_limit_bytes=16 * MIB),
+        cost_estimate=SMALL,
         name="expert",
     )(*parts, *weights)
 
 
-def final_kernel(parts, stream_ref, gate_ref, picking_ref, gain_ref, *refs):
+def add_kernel(parts, order, picking_ref, so_far_ref, gate_ref, *refs):
     inputs, out_ref, results = refs[:parts], refs[parts], refs[parts + 1]
     span = inputs[0].shape[0]
-    for number, part in enumerate(inputs):
+    places = []
+    for number, (part, at) in enumerate(zip(inputs, order)):
         results[number * span : (number + 1) * span, :] = part[...]
-    picked = jnp.dot(picking_ref[...], results[...], preferred_element_type=jnp.float32)
-    total = stream_ref[...].astype(jnp.float32) + gate_ref[...] * picked
-    out_ref[...] = (normalise(total) * gain_ref[...]).astype(jnp.bfloat16)
-
-
-def finish(stream, gate, picking, gain, parts):
-    length, width = stream.shape
+        places.append(picking_ref[:, at * span : (at + 1) * span])
+    picking = jnp.concatenate(places, axis=1) if parts > 1 else places[0]
+    picked = jnp.dot(picking, results[...], preferred_element_type=jnp.float32)
+    out_ref[...] = so_far_ref[...].astype(jnp.float32) + gate_ref[...] * picked
+
+
+def close_kernel(parts, order, picking_ref, so_far_ref, gate_ref, gain_ref, *refs):
+    *refs, out_ref, results, total = refs
+    add_kernel(parts, order, picking_ref, so_far_ref, gate_ref, *refs, total, results)
+    out_ref[...] = (normalise(total[...]) * gain_ref[...]).astype(jnp.bfloat16)
+
+
+def add_results(so_far, gate, picking, parts, gain=None):
+    length, width = so_far.shape
     whole = pl.BlockSpec(memory_space=pltpu.VMEM)
-    span = parts[0].shape[0]
-    return pl.pallas_call(
-        functools.partial(final_kernel, len(parts)),
-        in_specs=[whole] * (4 + len(parts)),
+    order, values = tuple(parts), [parts[at] for at in parts]
+    span = values[0].shape[0]
+    scratch = [pltpu.VMEM((span * len(parts), width), jnp.bfloat16)]
+    last = gain is not None
+    if last:
+        scratch.append(pltpu.VMEM((length, width), jnp.float32))
+    return pl.pallas_call(
+        functools.partial(close_kernel if last else add_kernel, len(parts), order),
+        in_specs=[whole] * (3 + last + len(parts)),
         out_specs=whole,
-        out_shape=jax.ShapeDtypeStruct((length, width), jnp.bfloat16),
-        scratch_shapes=[pltpu.VMEM((span * len(parts), width), jnp.bfloat16)],
+        out_shape=jax.ShapeDtypeStruct((length, width), jnp.bfloat16 if last else jnp.float32),
+        scratch_shapes=scratch,
         compiler_params=pltpu.CompilerParams(vmem_limit_bytes=24 * MIB),
-        name="finish",
-    )(stream, gate, picking, gain, *parts)
+        cost_estimate=SMALL,
+        name="finish" if last else "add",
+    )(picking, so_far, gate, *([gain] if last else []), *values)
 
 
 def on_device(frames, frame_counts, expert_ids, conv_kernel, router, w_in, w_out, final_gain):
@@ -253,37 +329,51 @@
     n_dev = lax.axis_size("expert")
     chips = n_dev // 2
     cap = 2 * ((5 * length + 8 * chips - 1) // (8 * chips))
-    me = lax.axis_index("expert") // 2
+    chip = (lax.axis_index("expert") // 2).astype(jnp.int32).reshape(1)
     other_in = xor_route(w_in, "expert", 1)
     other_out = xor_route(w_out, "expert", 1)
-    weights = (w_in, other_in, w_out, other_out)
     ids = expert_ids.reshape(1, length)
     gain = final_gain.reshape(1, width)
 
     if chips <= 8:
         pitch = -(-cap // 16) * 16
-        stream, expert_in, slot, *messages = prepare(
-            frames[0], frame_counts, ids ^ me, conv_kernel, chips, cap, pitch, chips
+        own_in, own_out, stream, expert_in, slot, *messages = prepare(
+            frames, frame_counts, chip, ids, conv_kernel, w_in, w_out, chips, cap, pitch, chips
         )
-        gate, picking = gate_and_picking(frame_counts, expert_in, router, ids, slot, pitch)
+        send = lambda part, d: xor_route(part, "expert", 2 * d)
         far = [d for d in range(1, chips) if d >= chips // 2]
         near = [d for d in range(1, chips) if d < chips // 2]
         half = max(1, len(far) // 2)
-        arrived = {0: messages[0]}
-        for d in far + near:
-            arrived[d] = xor_route(messages[d], "expert", 2 * d)
+        first, second = far[:half], far[half:]
+        arrived = {d: send(messages[d], d) for d in far}
+        other_in, other_out = load(other_in, other_out)
+        weights = (own_in, other_in, own_out, other_out)
         results = {}
-        for batch in (far[:half], far[half:], [0] + near):
-            if batch:
-                for d, part in zip(batch, run_expert([arrived[d] for d in batch], weights)):
-                    results[d] = part if d == 0 else xor_route(part, "expert", 2 * d)
-        parts = [results[d] for d in range(chips)]
+        first_out = run_expert([arrived[d] for d in first], weights)
+        for d, part in zip(first, first_out):
+            results[d] = send(part, d)
+        gate, picking = gate_and_picking(frame_counts, expert_in, router, ids, slot, pitch)
+        held = after([messages[d] for d in near], [arrived[d] for d in first])
+        for d, part in zip(near, held):
+            arrived[d] = send(part, d)
+        second_out = run_expert(after([arrived[d] for d in second], first_out), weights)
+        for d, part in zip(second, second_out):
+            results[d] = send(part, d)
+        close = run_expert([messages[0]] + after([arrived[d] for d in near], second_out), weights)
+        for d, part in zip([0] + near, close):
+            results[d] = part if d == 0 else send(part, d)
+        total = add_results(stream, gate, picking, {d: results[d] for d in first})
+        output = add_results(total, gate, picking, {d: results[d] for d in second + [0] + near}, gain)
     else:
-        stream, expert_in, slot, message = prepare(frames[0], frame_counts, ids, conv_kernel, chips, cap, cap, 1)
+        home = jnp.zeros((1,), jnp.int32)
+        own_in, own_out, stream, expert_in, slot, message = prepare(
+            frames, frame_counts, home, ids, conv_kernel, w_in, w_out, chips, cap, cap, 1
+        )
         gate, picking = gate_and_picking(frame_counts, expert_in, router, ids, slot, cap)
-        (result,) = run_expert([exchange(message, "expert", chips)], weights)
-        parts = [exchange(result, "expert", chips)]
-    return finish(stream, gate, picking, gain, parts).reshape(1, length, width)
+        other_in, other_out = load(other_in, other_out)
+        (result,) = run_expert([exchange(message, "expert", chips)], (own_in, other_in, own_out, other_out))
+        output = add_results(stream, gate, picking, {0: exchange(result, "expert", chips)}, gain)
+    return output.reshape(1, length, width)
 
 
 def solution(mesh):

time: 77.6 us -> 68.7 us (0.89)
  Pallas kernels: 32.6 us -> 26.3 us
  waiting for transfers between devices: 6.2 us -> 12.2 us
  local copies, waits for them, and re-layouts: 6.6 us -> 0.86 us
  starting transfers between devices: 30.5 us -> 28.4 us
    pallas_call x3, Pallas kernels: 23.8 us -> 11.5 us  [run_expert(): pl.pallas_call(functools.partial(expert_kernel, count, min(1024, hidden))...]
    ppermute x16, waiting for transfers between devices: 6.2 us -> 12.2 us  [xor_route(): return lax.ppermute(block, axis, [(i, i ^ distance) for i in range(count)])]
    unnamed x19 -> x9, local copies, waits for them, and re-layouts: 6.6 us -> 0.86 us
    pallas_call x1 -> x3, Pallas kernels: 1.85 us -> 5.69 us  [the longest x1 3.48 us: load(): pl.pallas_call(functools.partial(load_kernel, count), in_specs=[pl.BlockS...]
    ppermute x16, starting transfers between devices: 30.5 us -> 28.4 us  [xor_route(): return lax.ppermute(block, axis, [(i, i ^ distance) for i in range(count)])]
    pallas_call x1, Pallas kernels: 6.45 us -> 8.48 us  [prepare(): pl.pallas_call(functools.partial(pre_kernel, cap, pitch), in_specs=[pl.Bl...]
  transfers between devices with their start and end apart: 16 -> 16, of which waited for: 4 -> 4; matrix products, arithmetic and copies ran while one was open for 1% -> 0% of each run, Pallas kernels for 40% -> 36%
where the time goes in v2:
time: 68.7 us; the launch traced here: 68.5 us
  starting transfers between devices  28.4 us (41%)
  Pallas kernels  26.3 us (38%)
  waiting for transfers between devices  12.2 us (18%)
  local copies, waits for them, and re-layouts  0.86 us (1%)
  between operations  0.79 us (1%)
    ppermute x16, starting transfers between devices, xor_route(): return lax.ppermute(block, axis, [(i, i ^ distance) for i in range(count)])  28.4 us
    ppermute x16, waiting for transfers between devices, xor_route(): return lax.ppermute(block, axis, [(i, i ^ distance) for i in range(count)])  12.2 us
    pallas_call x3, Pallas kernels, run_expert(): pl.pallas_call(functools.partial(expert_kernel, count, min(1024, hidden))...  11.5 us
    pallas_call x1, Pallas kernels, prepare(): pl.pallas_call(functools.partial(pre_kernel, cap, pitch), in_specs=[pl.Bl...  8.48 us
    pallas_call x1, Pallas kernels, load(): pl.pallas_call(functools.partial(load_kernel, count), in_specs=[pl.BlockS...  3.48 us
    pallas_call x2, Pallas kernels, add_results(): pl.pallas_call(functools.partial(close_kernel if last else add_kernel, le...  2.21 us
  transfers between devices with their start and end apart: 16, of which 4 were waited for; matrix products, arithmetic and copies ran while one was open for 0% of the time, Pallas kernels for 36%

profile of v2, /device:TPU:0, one launch (start us, length us, event | category | flops | bytes accessed | tf_op | source)
XLA Modules:
  0.0 68.5 jit_solution(6168845138282107940)
XLA Ops:
  0.0 0.5 collective-permute-start.2
  0.5 0.1 collective-permute-start.3
  1.2 0.0 copy-start
  1.2 0.7 copy-done
  1.9 8.5 %prepare.1 = (bf16[1024,2048]{1,0:T(8,128)(2,1)S(1)}, bf16[2048,1024]{1,0:T(8,128)(2,1)S(1)}, bf16[384,1024]{1,0:T(8,128)(2,1)S(1)}, bf16[384,1024]{1,0:T(8,128)...) custom-call(s32[1]{0:T(128)S(6)} %copy.10.count_ref, ...), custom_call_target="tpu_custom_call" | custom-call | flops 1 | bytes 1 | tf_op jit(solution)/shard_map/prepare/pallas_call | solution.py:152
  10.3 4.1 %collective-permute-start = (bf16[64,1024]{1,0:T(8,128)(2,1)S(1)}, bf16[64,1024]{1,0:T(8,128)(2,1)S(1)}, u32[]{:S(2)}, u32[]{:S(2)}) collective-permute-start(bf16[64,1024]{1,0:T(8,128)(2,1)S(1)} %get-tuple-element.43), channel_id=1, source_target_pairs={{0,8},{1,9},{2,10},{3,11},{4,12},{5,13},{6,14},{7,15},{8,0},{9,1},... | collective-permute-start | bytes 393224 | tf_op jit(solution)/shard_map/ppermute | solution.py:20
  14.4 1.3 %collective-permute-start.1 = (bf16[64,1024]{1,0:T(8,128)(2,1)S(1)}, bf16[64,1024]{1,0:T(8,128)(2,1)S(1)}, u32[]{:S(2)}, u32[]{:S(2)}) collective-permute-start(bf16[64,1024]{1,0:T(8,128)(2,1)S(1)} %get-tuple-element.44), channel_id=1, source_target_pairs={{0,10},{1,11},{2,8},{3,9},{4,14},{5,15},{6,12},{7,13},{8,2},{9,3},... | collective-permute-start | bytes 393224 | tf_op jit(solution)/shard_map/ppermute | solution.py:20
  15.7 3.6 %collective-permute-start.6 = (bf16[64,1024]{1,0:T(8,128)(2,1)S(1)}, bf16[64,1024]{1,0:T(8,128)(2,1)S(1)}, u32[]{:S(2)}, u32[]{:S(2)}) collective-permute-start(bf16[64,1024]{1,0:T(8,128)(2,1)S(1)} %get-tuple-element.51), channel_id=1, source_target_pairs={{0,12},{1,13},{2,14},{3,15},{4,8},{5,9},{6,10},{7,11},{8,4},{9,5},... | collective-permute-start | bytes 393224 | tf_op jit(solution)/shard_map/ppermute | solution.py:20
  19.3 7.8 %collective-permute-done.refs_0_ = bf16[64,1024]{1,0:T(8,128)(2,1)S(1)} collective-permute-done((bf16[64,1024]{1,0:T(8,128)(2,1)S(1)}, bf16[64,1024]{1,0:T(8,128)(2,1)S(1)}, u32[]{:S(2)}, u32[]{:S(2)}) %collective-permute-start) | collective-permute-done | bytes 131104 | tf_op jit(solution)/shard_map/ppermute | solution.py:20
  27.2 3.9 %collective-permute-start.7 = (bf16[64,1024]{1,0:T(8,128)(2,1)S(1)}, bf16[64,1024]{1,0:T(8,128)(2,1)S(1)}, u32[]{:S(2)}, u32[]{:S(2)}) collective-permute-start(bf16[64,1024]{1,0:T(8,128)(2,1)S(1)} %get-tuple-element.52), channel_id=1, source_target_pairs={{0,14},{1,15},{2,12},{3,13},{4,10},{5,11},{6,8},{7,9},{8,6},{9,7},... | collective-permute-start | bytes 393224 | tf_op jit(solution)/shard_map/ppermute | solution.py:20
  31.1 0.2 collective-permute-done.1.refs_1_
  31.3 0.3 collective-permute-start.10
  31.6 0.0 collective-permute-done.2.refs_0_
  31.6 0.0 collective-permute-start.11
  31.7 0.0 collective-permute-done.3.refs_1_
  31.7 3.1 %collective-permute-start.12 = (bf16[64,1024]{1,0:T(8,128)(2,1)S(1)}, bf16[64,1024]{1,0:T(8,128)(2,1)S(1)}, u32[]{:S(2)}, u32[]{:S(2)}) collective-permute-start(bf16[64,1024]{1,0:T(8,128)(2,1)S(1)} %get-tuple-element.63), channel_id=1, source_target_pairs={{0,6},{1,7},{2,4},{3,5},{4,2},{5,3},{6,0},{7,1},{8,14},{9,15},{10,... | collective-permute-start | bytes 393224 | tf_op jit(solution)/shard_map/ppermute | solution.py:20
  34.8 3.5 %load.1 = (bf16[1024,2048]{1,0:T(8,128)(2,1)S(1)}, bf16[2048,1024]{1,0:T(8,128)(2,1)S(1)}) custom-call(bf16[1024,2048]{1,0:T(8,128)(2,1)} %collective-permute-done.2.refs_0_, bf16[2048,1024]{1,0:T(8,128)(2,1)} %collective-permute-done.3.refs_1_), custom_call_target="tpu_custom_call" | custom-call | flops 1 | bytes 1 | tf_op jit(solution)/shard_map/load/pallas_call | solution.py:191
  38.3 2.9 %expert.3 = (bf16[64,1024]{1,0:T(8,128)(2,1)S(1)}, bf16[64,1024]{1,0:T(8,128)(2,1)S(1)}) custom-call(bf16[64,1024]{1,0:T(8,128)(2,1)S(1)} %collective-permute-done.refs_0_, bf16[64,1024]{1,0:T(8,128)(2,1)S(1)} %collective-permute-done.1.refs_1_, bf16[1024,2048]{1,0:T(8,128)(2,1)S(1)} %get-tuple-element.45.refs_2_.refs_4_, ...), custom_call_target="tpu_custom_call" | custom-call | flops 1 | bytes 1 | tf_op jit(solution)/shard_map/expert/pallas_call | solution.py:273
  41.2 0.0 collective-permute-done.6.refs_0_
  41.2 1.3 %collective-permute-start.4 = (bf16[64,1024]{1,0:T(8,128)(2,1)S(1)}, bf16[64,1024]{1,0:T(8,128)(2,1)S(1)}, u32[]{:S(2)}, u32[]{:S(2)}) collective-permute-start(bf16[64,1024]{1,0:T(8,128)(2,1)S(1)} %get-tuple-element.49), channel_id=1, source_target_pairs={{0,8},{1,9},{2,10},{3,11},{4,12},{5,13},{6,14},{7,15},{8,0},{9,1},... | collective-permute-start | bytes 393224 | tf_op jit(solution)/shard_map/ppermute | solution.py:20
  42.5 0.0 collective-permute-done.7.refs_1_
  42.5 1.5 %collective-permute-start.5 = (bf16[64,1024]{1,0:T(8,128)(2,1)S(1)}, bf16[64,1024]{1,0:T(8,128)(2,1)S(1)}, u32[]{:S(2)}, u32[]{:S(2)}) collective-permute-start(bf16[64,1024]{1,0:T(8,128)(2,1)S(1)} %get-tuple-element.50), channel_id=1, source_target_pairs={{0,10},{1,11},{2,8},{3,9},{4,14},{5,15},{6,12},{7,13},{8,2},{9,3},... | collective-permute-start | bytes 393224 | tf_op jit(solution)/shard_map/ppermute | solution.py:20
  44.0 2.9 %expert.4 = (bf16[64,1024]{1,0:T(8,128)(2,1)S(1)}, bf16[64,1024]{1,0:T(8,128)(2,1)S(1)}) custom-call(bf16[64,1024]{1,0:T(8,128)(2,1)S(1)} %collective-permute-done.6.refs_0_, bf16[64,1024]{1,0:T(8,128)(2,1)S(1)} %collective-permute-done.7.refs_1_, bf16[1024,2048]{1,0:T(8,128)(2,1)S(1)} %get-tuple-element.45.refs_2_.refs_4_, ...), custom_call_target="tpu_custom_call" | custom-call | flops 1 | bytes 1 | tf_op jit(solution)/shard_map/expert/pallas_call | solution.py:273
  46.9 0.0 collective-permute-done.10.refs_1_
  46.9 2.9 %collective-permute-start.8 = (bf16[64,1024]{1,0:T(8,128)(2,1)S(1)}, bf16[64,1024]{1,0:T(8,128)(2,1)S(1)}, u32[]{:S(2)}, u32[]{:S(2)}) collective-permute-start(bf16[64,1024]{1,0:T(8,128)(2,1)S(1)} %get-tuple-element.55), channel_id=1, source_target_pairs={{0,12},{1,13},{2,14},{3,15},{4,8},{5,9},{6,10},{7,11},{8,4},{9,5},... | collective-permute-start | bytes 393224 | tf_op jit(solution)/shard_map/ppermute | solution.py:20
  49.8 0.0 collective-permute-done.11.refs_2_
  49.8 0.0 collective-permute-done.12.refs_3_
  49.8 0.0 copy-start.3
  49.8 0.0 copy-start.1
  49.8 5.7 %expert.5 = (bf16[64,1024]{1,0:T(8,128)(2,1)S(1)}, bf16[64,1024]{1,0:T(8,128)(2,1)}, bf16[64,1024]{1,0:T(8,128)(2,1)S(1)}, bf16[64,1024]{1,0:T(8,128)(2,1)S(1)}) custom-call(bf16[64,1024]{1,0:T(8,128)(2,1)S(1)} %get-tuple-element.57.refs_0_, bf16[64,1024]{1,0:T(8,128)(2,1)S(1)} %collective-permute-done.10.refs_1_, ...), custom_call_target="tpu_custom_call" | custom-call | flops 1 | bytes 1 | tf_op jit(solution)/shard_map/expert/pallas_call | solution.py:273
  55.5 0.0 copy-start.2
  55.5 1.5 %collective-permute-start.13 = (bf16[64,1024]{1,0:T(8,128)(2,1)}, bf16[64,1024]{1,0:T(8,128)(2,1)S(1)}, u32[]{:S(2)}, u32[]{:S(2)}) collective-permute-start(bf16[64,1024]{1,0:T(8,128)(2,1)} %get-tuple-element.68), channel_id=1, source_target_pairs={{0,2},{1,3},{2,0},{3,1},{4,6},{5,7},{6,4},{7,5},{8,10},{9,11},{10,... | collective-permute-start | bytes 393224 | tf_op jit(solution)/shard_map/ppermute | solution.py:20
  57.0 0.0 collective-permute-start.14
  57.0 0.0 collective-permute-done.4.refs_0_
  57.0 2.0 %collective-permute-start.15 = (bf16[64,1024]{1,0:T(8,128)(2,1)S(1)}, bf16[64,1024]{1,0:T(8,128)(2,1)S(1)}, u32[]{:S(2)}, u32[]{:S(2)}) collective-permute-start(bf16[64,1024]{1,0:T(8,128)(2,1)S(1)} %get-tuple-element.70), channel_id=1, source_target_pairs={{0,6},{1,7},{2,4},{3,5},{4,2},{5,3},{6,0},{7,1},{8,14},{9,15},{10,... | collective-permute-start | bytes 393224 | tf_op jit(solution)/shard_map/ppermute | solution.py:20
  59.0 0.0 collective-permute-done.5.refs_1_
  59.0 2.4 %collective-permute-start.9 = (bf16[64,1024]{1,0:T(8,128)(2,1)S(1)}, bf16[64,1024]{1,0:T(8,128)(2,1)S(1)}, u32[]{:S(2)}, u32[]{:S(2)}) collective-permute-start(bf16[64,1024]{1,0:T(8,128)(2,1)S(1)} %get-tuple-element.56), channel_id=1, source_target_pairs={{0,14},{1,15},{2,12},{3,13},{4,10},{5,11},{6,8},{7,9},{8,6},{9,7},... | collective-permute-start | bytes 393224 | tf_op jit(solution)/shard_map/ppermute | solution.py:20
  61.4 0.0 copy-done.3
  61.4 0.2 copy.9.router_ref
  61.6 0.0 copy-done.1
  61.6 0.6 gate.1
  62.1 0.4 add.2.so_far_ref
  62.5 0.0 collective-permute-done.13.refs_3_
  62.5 0.0 collective-permute-done.14.refs_4_
  62.5 2.3 %collective-permute-done.15.refs_5_ = bf16[64,1024]{1,0:T(8,128)(2,1)S(1)} collective-permute-done((bf16[64,1024]{1,0:T(8,128)(2,1)S(1)}, bf16[64,1024]{1,0:T(8,128)(2,1)S(1)}, u32[]{:S(2)}, u32[]{:S(2)}) %collective-permute-start.15) | collective-permute-done | bytes 131104 | tf_op jit(solution)/shard_map/ppermute | solution.py:20
  64.8 0.0 collective-permute-done.8.refs_0_
  64.8 1.8 %collective-permute-done.9.refs_1_ = bf16[64,1024]{1,0:T(8,128)(2,1)S(1)} collective-permute-done((bf16[64,1024]{1,0:T(8,128)(2,1)S(1)}, bf16[64,1024]{1,0:T(8,128)(2,1)S(1)}, u32[]{:S(2)}, u32[]{:S(2)}) %collective-permute-start.9) | collective-permute-done | bytes 131104 | tf_op jit(solution)/shard_map/ppermute | solution.py:20
  66.7 0.0 copy-done.2
  66.7 1.9 %finish.1 = bf16[384,1024]{1,0:T(8,128)(2,1)} custom-call(bf16[384,512]{1,0:T(8,128)(2,1)S(1)} %get-tuple-element.40.picking_ref, f32[384,1024]{1,0:T(8,128)S(1)} %add.2.so_far_ref, f32[384,1]{1,0:T(8,128)S(1)} %get-tuple-element.42.gate_ref, f32[1,1024]{1,0:T(1,128)S(1)} %bitcast.6, bf16[64,1024]{1,0:T(8,128)(2,1)S(1)} %collective-permute-done.8.refs_0_, ...), custom_call_target="tpu_custom_call" | custom-call | flops 1 | bytes 1 | tf_op jit(solution)/shard_map/finish/pallas_call | solution.py:315
Async XLA Ops:
  0.0 31.6 %collective-permute-start.2 = (bf16[1024,2048]{1,0:T(8,128)(2,1)}, bf16[1024,2048]{1,0:T(8,128)(2,1)}, u32[]{:S(2)}, u32[]{:S(2)}) collective-permute-start(bf16[1024,2048]{1,0:T(8,128)(2,1)} %in_hbm.1), channel_id=1, source_target_pairs={{0,1},{1,0},{2,3},{3,2},{4,5},{5,4},{6,7},{7,6},{8,9},{9,8},{10,11... | collective-permute-start | bytes 12582920 | tf_op jit(solution)/shard_map/ppermute | solution.py:20
  0.5 31.2 %collective-permute-start.3 = (bf16[2048,1024]{1,0:T(8,128)(2,1)}, bf16[2048,1024]{1,0:T(8,128)(2,1)}, u32[]{:S(2)}, u32[]{:S(2)}) collective-permute-start(bf16[2048,1024]{1,0:T(8,128)(2,1)} %out_hbm.1), channel_id=1, source_target_pairs={{0,1},{1,0},{2,3},{3,2},{4,5},{5,4},{6,7},{7,6},{8,9},{9,8},{10,11... | collective-permute-start | bytes 12582920 | tf_op jit(solution)/shard_map/ppermute | solution.py:20
  1.2 0.7 copy-start
  10.3 16.8 %collective-permute-start = (bf16[64,1024]{1,0:T(8,128)(2,1)S(1)}, bf16[64,1024]{1,0:T(8,128)(2,1)S(1)}, u32[]{:S(2)}, u32[]{:S(2)}) collective-permute-start(bf16[64,1024]{1,0:T(8,128)(2,1)S(1)} %get-tuple-element.43), channel_id=1, source_target_pairs={{0,8},{1,9},{2,10},{3,11},{4,12},{5,13},{6,14},{7,15},{8,0},{9,1},... | collective-permute-start | bytes 393224 | tf_op jit(solution)/shard_map/ppermute | solution.py:20
  14.4 16.9 %collective-permute-start.1 = (bf16[64,1024]{1,0:T(8,128)(2,1)S(1)}, bf16[64,1024]{1,0:T(8,128)(2,1)S(1)}, u32[]{:S(2)}, u32[]{:S(2)}) collective-permute-start(bf16[64,1024]{1,0:T(8,128)(2,1)S(1)} %get-tuple-element.44), channel_id=1, source_target_pairs={{0,10},{1,11},{2,8},{3,9},{4,14},{5,15},{6,12},{7,13},{8,2},{9,3},... | collective-permute-start | bytes 393224 | tf_op jit(solution)/shard_map/ppermute | solution.py:20
  15.7 25.5 %collective-permute-start.6 = (bf16[64,1024]{1,0:T(8,128)(2,1)S(1)}, bf16[64,1024]{1,0:T(8,128)(2,1)S(1)}, u32[]{:S(2)}, u32[]{:S(2)}) collective-permute-start(bf16[64,1024]{1,0:T(8,128)(2,1)S(1)} %get-tuple-element.51), channel_id=1, source_target_pairs={{0,12},{1,13},{2,14},{3,15},{4,8},{5,9},{6,10},{7,11},{8,4},{9,5},... | collective-permute-start | bytes 393224 | tf_op jit(solution)/shard_map/ppermute | solution.py:20
  27.2 15.3 %collective-permute-start.7 = (bf16[64,1024]{1,0:T(8,128)(2,1)S(1)}, bf16[64,1024]{1,0:T(8,128)(2,1)S(1)}, u32[]{:S(2)}, u32[]{:S(2)}) collective-permute-start(bf16[64,1024]{1,0:T(8,128)(2,1)S(1)} %get-tuple-element.52), channel_id=1, source_target_pairs={{0,14},{1,15},{2,12},{3,13},{4,10},{5,11},{6,8},{7,9},{8,6},{9,7},... | collective-permute-start | bytes 393224 | tf_op jit(solution)/shard_map/ppermute | solution.py:20
  31.3 15.6 %collective-permute-start.10 = (bf16[64,1024]{1,0:T(8,128)(2,1)S(1)}, bf16[64,1024]{1,0:T(8,128)(2,1)S(1)}, u32[]{:S(2)}, u32[]{:S(2)}) collective-permute-start(bf16[64,1024]{1,0:T(8,128)(2,1)S(1)} %get-tuple-element.61), channel_id=1, source_target_pairs={{0,2},{1,3},{2,0},{3,1},{4,6},{5,7},{6,4},{7,5},{8,10},{9,11},{10,... | collective-permute-start | bytes 393224 | tf_op jit(solution)/shard_map/ppermute | solution.py:20
  31.6 18.1 %collective-permute-start.11 = (bf16[64,1024]{1,0:T(8,128)(2,1)S(1)}, bf16[64,1024]{1,0:T(8,128)(2,1)S(1)}, u32[]{:S(2)}, u32[]{:S(2)}) collective-permute-start(bf16[64,1024]{1,0:T(8,128)(2,1)S(1)} %get-tuple-element.62), channel_id=1, source_target_pairs={{0,4},{1,5},{2,6},{3,7},{4,0},{5,1},{6,2},{7,3},{8,12},{9,13},{10,... | collective-permute-start | bytes 393224 | tf_op jit(solution)/shard_map/ppermute | solution.py:20
  31.7 18.1 %collective-permute-start.12 = (bf16[64,1024]{1,0:T(8,128)(2,1)S(1)}, bf16[64,1024]{1,0:T(8,128)(2,1)S(1)}, u32[]{:S(2)}, u32[]{:S(2)}) collective-permute-start(bf16[64,1024]{1,0:T(8,128)(2,1)S(1)} %get-tuple-element.63), channel_id=1, source_target_pairs={{0,6},{1,7},{2,4},{3,5},{4,2},{5,3},{6,0},{7,1},{8,14},{9,15},{10,... | collective-permute-start | bytes 393224 | tf_op jit(solution)/shard_map/ppermute | solution.py:20
  41.2 15.8 %collective-permute-start.4 = (bf16[64,1024]{1,0:T(8,128)(2,1)S(1)}, bf16[64,1024]{1,0:T(8,128)(2,1)S(1)}, u32[]{:S(2)}, u32[]{:S(2)}) collective-permute-start(bf16[64,1024]{1,0:T(8,128)(2,1)S(1)} %get-tuple-element.49), channel_id=1, source_target_pairs={{0,8},{1,9},{2,10},{3,11},{4,12},{5,13},{6,14},{7,15},{8,0},{9,1},... | collective-permute-start | bytes 393224 | tf_op jit(solution)/shard_map/ppermute | solution.py:20
  42.5 16.5 %collective-permute-start.5 = (bf16[64,1024]{1,0:T(8,128)(2,1)S(1)}, bf16[64,1024]{1,0:T(8,128)(2,1)S(1)}, u32[]{:S(2)}, u32[]{:S(2)}) collective-permute-start(bf16[64,1024]{1,0:T(8,128)(2,1)S(1)} %get-tuple-element.50), channel_id=1, source_target_pairs={{0,10},{1,11},{2,8},{3,9},{4,14},{5,15},{6,12},{7,13},{8,2},{9,3},... | collective-permute-start | bytes 393224 | tf_op jit(solution)/shard_map/ppermute | solution.py:20
  46.9 17.9 %collective-permute-start.8 = (bf16[64,1024]{1,0:T(8,128)(2,1)S(1)}, bf16[64,1024]{1,0:T(8,128)(2,1)S(1)}, u32[]{:S(2)}, u32[]{:S(2)}) collective-permute-start(bf16[64,1024]{1,0:T(8,128)(2,1)S(1)} %get-tuple-element.55), channel_id=1, source_target_pairs={{0,12},{1,13},{2,14},{3,15},{4,8},{5,9},{6,10},{7,11},{8,4},{9,5},... | collective-permute-start | bytes 393224 | tf_op jit(solution)/shard_map/ppermute | solution.py:20
  49.8 11.6 %copy-start.3 = (bf16[1024,8]{0,1:T(8,128)(2,1)S(1)}, bf16[1024,8]{0,1:T(8,128)(2,1)}, u32[]{:S(2)}) copy-start(bf16[1024,8]{0,1:T(8,128)(2,1)} %param.12) | copy-start | bytes 49156
  49.8 11.8 %copy-start.1 = (s32[1,384,1]{1,2,0:T(1,128)S(1)}, s32[1,384,1]{1,2,0:T(1,128)}, u32[]{:S(2)}) copy-start(s32[1,384,1]{1,2,0:T(1,128)} %param.10) | copy-start | bytes 4612
  55.5 11.2 %copy-start.2 = (f32[1024]{0:T(1024)S(1)}, f32[1024]{0:T(1024)}, u32[]{:S(2)}) copy-start(f32[1024]{0:T(1024)} %param.15) | copy-start | bytes 12292
  55.5 7.0 %collective-permute-start.13 = (bf16[64,1024]{1,0:T(8,128)(2,1)}, bf16[64,1024]{1,0:T(8,128)(2,1)S(1)}, u32[]{:S(2)}, u32[]{:S(2)}) collective-permute-start(bf16[64,1024]{1,0:T(8,128)(2,1)} %get-tuple-element.68), channel_id=1, source_target_pairs={{0,2},{1,3},{2,0},{3,1},{4,6},{5,7},{6,4},{7,5},{8,10},{9,11},{10,... | collective-permute-start | bytes 393224 | tf_op jit(solution)/shard_map/ppermute | solution.py:20
  57.0 5.5 %collective-permute-start.14 = (bf16[64,1024]{1,0:T(8,128)(2,1)S(1)}, bf16[64,1024]{1,0:T(8,128)(2,1)S(1)}, u32[]{:S(2)}, u32[]{:S(2)}) collective-permute-start(bf16[64,1024]{1,0:T(8,128)(2,1)S(1)} %get-tuple-element.69), channel_id=1, source_target_pairs={{0,4},{1,5},{2,6},{3,7},{4,0},{5,1},{6,2},{7,3},{8,12},{9,13},{10,... | collective-permute-start | bytes 393224 | tf_op jit(solution)/shard_map/ppermute | solution.py:20
  57.0 7.8 %collective-permute-start.15 = (bf16[64,1024]{1,0:T(8,128)(2,1)S(1)}, bf16[64,1024]{1,0:T(8,128)(2,1)S(1)}, u32[]{:S(2)}, u32[]{:S(2)}) collective-permute-start(bf16[64,1024]{1,0:T(8,128)(2,1)S(1)} %get-tuple-element.70), channel_id=1, source_target_pairs={{0,6},{1,7},{2,4},{3,5},{4,2},{5,3},{6,0},{7,1},{8,14},{9,15},{10,... | collective-permute-start | bytes 393224 | tf_op jit(solution)/shard_map/ppermute | solution.py:20
  59.0 7.7 %collective-permute-start.9 = (bf16[64,1024]{1,0:T(8,128)(2,1)S(1)}, bf16[64,1024]{1,0:T(8,128)(2,1)S(1)}, u32[]{:S(2)}, u32[]{:S(2)}) collective-permute-start(bf16[64,1024]{1,0:T(8,128)(2,1)S(1)} %get-tuple-element.56), channel_id=1, source_target_pairs={{0,14},{1,15},{2,12},{3,13},{4,10},{5,11},{6,8},{7,9},{8,6},{9,7},... | collective-permute-start | bytes 393224 | tf_op jit(solution)/shard_map/ppermute | solution.py:20

commit v3 on v2

--- a/solution.py
+++ b/solution.py
@@ -37,7 +37,7 @@
 
 
 def silu(value):
-    return value / (1.0 + jnp.exp(-value))
+    return 0.5 * value * (1.0 + jnp.tanh(0.5 * value))
 
 
 def normalise(values):
@@ -47,9 +47,9 @@
     return centred * lax.rsqrt(variance + EPS)
 
 
-def pre_kernel(cap, pitch, count_ref, me_ref, frames_hbm, ids_ref, taps_hbm, in_hbm, out_hbm, *rest):
+def pre_kernel(cap, pitch, count_ref, me_ref, frames_hbm, ids_hbm, taps_hbm, in_hbm, out_hbm, *rest):
     in_ref, out_ref, stream_ref, expert_in_ref, slot_ref, *rest = rest
-    *message_refs, frames_ref, taps_ref, padded, taps_by_row, conv, frame_sems, taps_sem, weight_sems = rest
+    *message_refs, frames_ref, taps_ref, ids_ref, padded, conv, frame_sems, taps_sem, ids_sem, weight_sems = rest
     length, width = frames_ref.shape
     taps = taps_ref.shape[0]
     reach = taps // 2
@@ -66,55 +66,48 @@
     for copy in frame_copies:
         copy.start()
     taps_copy.start()
+    ids_copy = pltpu.make_async_copy(ids_hbm, ids_ref, ids_sem)
+    ids_copy.start()
     weight_copies = [
         pltpu.make_async_copy(in_hbm, in_ref, weight_sems.at[0]),
         pltpu.make_async_copy(out_hbm, out_ref, weight_sems.at[1]),
     ]
-    for copy in weight_copies:
-        copy.start()
-
-    edge = jnp.zeros((reach * groups, LANES), jnp.float32)
-    padded[: reach * groups, :] = edge
-    padded[(reach + length) * groups :, :] = edge
+    lead = padded.shape[1] - length - reach
+    padded[:, :lead, :] = jnp.zeros((groups, lead, LANES), jnp.float32)
+    padded[:, lead + length :, :] = jnp.zeros((groups, reach, LANES), jnp.float32)
     for number, start in enumerate(range(0, length, BLOCK)):
         frame_copies[number].wait()
         values = frames_ref[start : start + BLOCK, :].astype(jnp.float32)
         position = start + lax.broadcasted_iota(jnp.int32, (BLOCK, 1), 0)
         normed = jnp.where(position < count, normalise(values), 0.0)
         for group in range(groups):
-            lanes = slice(group * LANES, (group + 1) * LANES)
-            padded[pl.ds((reach + start) * groups + group, BLOCK, stride=groups), :] = normed[:, lanes]
-
+            padded[group, lead + start : lead + start + BLOCK, :] = normed[:, group * LANES : (group + 1) * LANES]
+
+    for copy in weight_copies:
+        copy.start()
     taps_copy.wait()
-    for group in range(groups):
-        lanes = slice(group * LANES, (group + 1) * LANES)
-        taps_by_row[pl.ds(group, taps, stride=groups), :] = taps_ref[:, lanes]
 
     def convolve(index, carry):
-        base = pl.multiple_of(index * (ROWS * groups), ROWS * groups)
-        window = [padded[pl.ds(base + step * groups, groups), :] for step in range(ROWS + taps - 1)]
-        sums = [None] * ROWS
+        group = lax.rem(index, groups)
+        start = pl.multiple_of(lax.div(index, groups) * BLOCK, BLOCK)
+        lanes = pl.ds(pl.multiple_of(group * LANES, LANES), LANES)
+        total = None
         for tap in range(taps):
-            weight = taps_by_row[tap * groups : (tap + 1) * groups, :]
-            for row in range(ROWS):
-                term = weight * window[row + tap]
-                sums[row] = term if tap == 0 else sums[row] + term
-        for row in range(ROWS):
-            conv[pl.ds(base + row * groups, groups), :] = sums[row]
+            term = taps_ref[pl.ds(tap, 1), lanes] * padded[group, pl.ds(start + (lead - reach + tap), BLOCK), :]
+            total = term if tap == 0 else total + term
+        conv[pl.ds(start, BLOCK), lanes] = total
         return carry
 
-    lax.fori_loop(0, length // ROWS, convolve, 0)
+    lax.fori_loop(0, groups * (length // BLOCK), convolve, 0)
 
     for start in range(0, length, BLOCK):
         rows = slice(start, start + BLOCK)
-        mixed = jnp.concatenate(
-            [conv[pl.ds(start * groups + group, BLOCK, stride=groups), :] for group in range(groups)], axis=1
-        )
-        stream = (frames_ref[rows, :].astype(jnp.float32) + silu(mixed)).astype(jnp.bfloat16)
+        stream = (frames_ref[rows, :].astype(jnp.float32) + silu(conv[rows, :])).astype(jnp.bfloat16)
         stream_ref[rows, :] = stream
         expert_in_ref[rows, :] = normalise(stream.astype(jnp.float32)).astype(jnp.bfloat16)
 
     chips = slot_ref.shape[0]
+    ids_copy.wait()
     ids = ids_ref[...] ^ me_ref[0]
     at = lax.broadcasted_iota(jnp.int32, (chips, length), 1)
     chosen = (ids == lax.broadcasted_iota(jnp.int32, (chips, length), 0)) & (at < count)
@@ -151,7 +144,7 @@
     bf16 = jnp.bfloat16
     return pl.pallas_call(
         functools.partial(pre_kernel, cap, pitch),
-        in_specs=[pl.BlockSpec(memory_space=pltpu.SMEM)] * 2 + [anywhere, whole] + [anywhere] * 3,
+        in_specs=[pl.BlockSpec(memory_space=pltpu.SMEM)] * 2 + [anywhere] * 5,
         out_specs=[whole] * (5 + messages),
         out_shape=[
             pltpu.VMEM(w_in.shape, bf16),
@@ -164,17 +157,18 @@
         scratch_shapes=[
             pltpu.VMEM((length, width), bf16),
             pltpu.VMEM(taps.shape, jnp.float32),
-            pltpu.VMEM(((length + 2 * reach) * groups, LANES), jnp.float32),
-            pltpu.VMEM((taps.shape[0] * groups, LANES), jnp.float32),
-            pltpu.VMEM((length * groups, LANES), jnp.float32),
+            pltpu.VMEM(ids.shape, jnp.int32),
+            pltpu.VMEM((groups, -(-reach // 8) * 8 + length + reach, LANES), jnp.float32),
+            pltpu.VMEM((length, width), jnp.float32),
             pltpu.SemaphoreType.DMA((length // BLOCK,)),
+            pltpu.SemaphoreType.DMA,
             pltpu.SemaphoreType.DMA,
             pltpu.SemaphoreType.DMA((2,)),
         ],
-        compiler_params=pltpu.CompilerParams(vmem_limit_bytes=24 * MIB),
+        compiler_params=pltpu.CompilerParams(vmem_limit_bytes=12 * MIB),
         cost_estimate=SMALL,
         name="prepare",
-    )(count, me, in_hbm(frames), ids, in_hbm(taps), in_hbm(w_in), in_hbm(w_out))
+    )(count, me, in_hbm(frames), in_hbm(ids), in_hbm(taps), in_hbm(w_in), in_hbm(w_out))
 
 
 def load_kernel(count, *refs):
@@ -202,9 +196,11 @@
 
 def gate_kernel(pitch, count_ref, expert_in_ref, router_ref, ids_ref, slot_ref, gate_ref, picking_ref):
     length = expert_in_ref.shape[0]
-    experts = router_ref.shape[1]
+    experts = router_ref.shape[0]
     slots = picking_ref.shape[1]
-    logits = jnp.dot(expert_in_ref[...], router_ref[...], preferred_element_type=jnp.float32)
+    logits = lax.dot_general(
+        expert_in_ref[...], router_ref[...], (((1,), (1,)), ((), ())), preferred_element_type=jnp.float32
+    )
     ids = jnp.broadcast_to(ids_ref[...].astype(jnp.float32), (experts, length)).T
     position = lax.broadcasted_iota(jnp.int32, (length, experts), 0)
     column = lax.broadcasted_iota(jnp.int32, (length, experts), 1).astype(jnp.float32)
@@ -230,7 +226,7 @@
         compiler_params=pltpu.CompilerParams(vmem_limit_bytes=12 * MIB),
         cost_estimate=SMALL,
         name="gate",
-    )(count, expert_in, router, ids, slot)
+    )(count, expert_in, router.T, ids, slot)
 
 
 def expert_kernel(parts, tile, *refs):
@@ -279,7 +275,7 @@
             pltpu.VMEM((span * count, width), jnp.bfloat16),
             pltpu.VMEM((span * count, width), jnp.float32),
         ],
-        compiler_params=pltpu.CompilerParams(vmem_limit_bytes=16 * MIB),
+        compiler_params=pltpu.CompilerParams(vmem_limit_bytes=10 * MIB),
         cost_estimate=SMALL,
         name="expert",
     )(*parts, *weights)
@@ -298,9 +294,20 @@
 
 
 def close_kernel(parts, order, picking_ref, so_far_ref, gate_ref, gain_ref, *refs):
-    *refs, out_ref, results, total = refs
+    *refs, out_hbm, results, total, out_ref, sems = refs
     add_kernel(parts, order, picking_ref, so_far_ref, gate_ref, *refs, total, results)
-    out_ref[...] = (normalise(total[...]) * gain_ref[...]).astype(jnp.bfloat16)
+    copies = []
+    for number, start in enumerate(range(0, total.shape[0], BLOCK)):
+        rows = slice(start, start + BLOCK)
+        out_ref[rows, :] = (normalise(total[rows, :]) * gain_ref[...]).astype(jnp.bfloat16)
+        copies.append(
+            pltpu.make_async_copy(
+                out_ref.at[pl.ds(start, BLOCK), :], out_hbm.at[pl.ds(start, BLOCK), :], sems.at[number]
+            )
+        )
+        copies[-1].start()
+    for copy in copies:
+        copy.wait()
 
 
 def add_results(so_far, gate, picking, parts, gain=None):
@@ -312,13 +319,15 @@
     last = gain is not None
     if last:
         scratch.append(pltpu.VMEM((length, width), jnp.float32))
+        scratch.append(pltpu.VMEM((length, width), jnp.bfloat16))
+        scratch.append(pltpu.SemaphoreType.DMA((length // BLOCK,)))
     return pl.pallas_call(
         functools.partial(close_kernel if last else add_kernel, len(parts), order),
         in_specs=[whole] * (3 + last + len(parts)),
-        out_specs=whole,
+        out_specs=pl.BlockSpec(memory_space=pl.ANY) if last else whole,
         out_shape=jax.ShapeDtypeStruct((length, width), jnp.bfloat16 if last else jnp.float32),
         scratch_shapes=scratch,
-        compiler_params=pltpu.CompilerParams(vmem_limit_bytes=24 * MIB),
+        compiler_params=pltpu.CompilerParams(vmem_limit_bytes=12 * MIB),
         cost_estimate=SMALL,
         name="finish" if last else "add",
     )(picking, so_far, gate, *([gain] if last else []), *values)
@@ -343,27 +352,29 @@
         send = lambda part, d: xor_route(part, "expert", 2 * d)
         far = [d for d in range(1, chips) if d >= chips // 2]
         near = [d for d in range(1, chips) if d < chips // 2]
-        half = max(1, len(far) // 2)
-        first, second = far[:half], far[half:]
-        arrived = {d: send(messages[d], d) for d in far}
+        first, second = far[::2], far[1::2]
+        arrived = {d: send(messages[d], d) for d in first}
         other_in, other_out = load(other_in, other_out)
         weights = (own_in, other_in, own_out, other_out)
+        for d, part in zip(second, after([messages[d] for d in second], other_in)):
+            arrived[d] = send(part, d)
+        for d, part in zip(near, [messages[d] for d in near]):
+            arrived[d] = send(part, d)
+        first_out = run_expert([arrived[d] for d in first], weights)
         results = {}
-        first_out = run_expert([arrived[d] for d in first], weights)
         for d, part in zip(first, first_out):
             results[d] = send(part, d)
         gate, picking = gate_and_picking(frame_counts, expert_in, router, ids, slot, pitch)
-        held = after([messages[d] for d in near], [arrived[d] for d in first])
-        for d, part in zip(near, held):
-            arrived[d] = send(part, d)
-        second_out = run_expert(after([arrived[d] for d in second], first_out), weights)
+        close = run_expert([messages[0]] + after([arrived[d] for d in near], first_out), weights)
+        results[0] = close[0]
+        second_out = run_expert(after([arrived[d] for d in second], (first_out, close)), weights)
         for d, part in zip(second, second_out):
             results[d] = send(part, d)
-        close = run_expert([messages[0]] + after([arrived[d] for d in near], second_out), weights)
-        for d, part in zip([0] + near, close):
-            results[d] = part if d == 0 else send(part, d)
-        total = add_results(stream, gate, picking, {d: results[d] for d in first})
-        output = add_results(total, gate, picking, {d: results[d] for d in second + [0] + near}, gain)
+        for d, part in zip(near, close[1:]):
+            results[d] = send(part, d)
+        total = add_results(stream, gate, picking, {d: results[d] for d in [0] + first})
+        total = add_results(total, gate, picking, {d: results[d] for d in near})
+        output = add_results(total, gate, picking, {d: results[d] for d in second}, gain)
     else:
         home = jnp.zeros((1,), jnp.int32)
         own_in, own_out, stream, expert_in, slot, message = prepare(

time: 68.7 us -> 62.5 us (0.910)
  waiting for transfers between devices: 12.2 us -> 9.39 us
  starting transfers between devices: 28.4 us -> 26.5 us
  Pallas kernels: 26.3 us -> 25.4 us
  local copies, waits for them, and re-layouts: 0.86 us -> 0.01 us
    ppermute x16, waiting for transfers between devices: 12.2 us -> 9.39 us  [xor_route(): return lax.ppermute(block, axis, [(i, i ^ distance) for i in range(count)])]
    ppermute x16, starting transfers between devices: 28.4 us -> 26.5 us  [xor_route(): return lax.ppermute(block, axis, [(i, i ^ distance) for i in range(count)])]
    unnamed x9 -> x6, local copies, waits for them, and re-layouts: 0.86 us -> 0.01 us
    pallas_call x3, Pallas kernels: 11.5 us -> 10.8 us  [run_expert(): pl.pallas_call(functools.partial(expert_kernel, count, min(1024, hidden))...]
    pallas_call x2 -> x3, Pallas kernels: 2.21 us -> 2.4 us  [add_results(): pl.pallas_call(functools.partial(close_kernel if last else add_kernel, le...]
  transfers between devices with their start and end apart: 16 -> 16, of which waited for: 4 -> 3; matrix products, arithmetic and copies ran while one was open for 0% -> 0% of each run, Pallas kernels for 36% -> 38%
where the time goes in v3:
time: 62.5 us; the launch traced here: 62.1 us
  starting transfers between devices  26.5 us (42%)
  Pallas kernels  25.4 us (41%)
  waiting for transfers between devices  9.39 us (15%)
  between operations  0.78 us (1%)
    ppermute x16, starting transfers between devices, xor_route(): return lax.ppermute(block, axis, [(i, i ^ distance) for i in range(count)])  26.5 us
    pallas_call x3, Pallas kernels, run_expert(): pl.pallas_call(functools.partial(expert_kernel, count, min(1024, hidden))...  10.8 us
    ppermute x16, waiting for transfers between devices, xor_route(): return lax.ppermute(block, axis, [(i, i ^ distance) for i in range(count)])  9.39 us
    pallas_call x1, Pallas kernels, prepare(): pl.pallas_call(functools.partial(pre_kernel, cap, pitch), in_specs=[pl.Bl...  8.19 us
    pallas_call x1, Pallas kernels, load(): pl.pallas_call(functools.partial(load_kernel, count), in_specs=[pl.BlockS...  3.48 us
    pallas_call x3, Pallas kernels, add_results(): pl.pallas_call(functools.partial(close_kernel if last else add_kernel, le...  2.4 us
  transfers between devices with their start and end apart: 16, of which 3 were waited for; matrix products, arithmetic and copies ran while one was open for 0% of the time, Pallas kernels for 38%

profile of v3, /device:TPU:0, one launch (start us, length us, event | category | flops | bytes accessed | tf_op | source)
XLA Modules:
  0.0 62.1 jit_solution(8256433850804965849)
XLA Ops:
  0.0 0.5 collective-permute-start.5
  0.5 0.1 collective-permute-start.6
  1.2 8.2 %prepare.1 = (bf16[1024,2048]{1,0:T(8,128)(2,1)S(1)}, bf16[2048,1024]{1,0:T(8,128)(2,1)S(1)}, bf16[384,1024]{1,0:T(8,128)(2,1)S(1)}, bf16[384,1024]{1,0:T(8,128)...) custom-call(s32[1]{0:T(128)S(6)} %copy.9.count_ref, ...), custom_call_target="tpu_custom_call" | custom-call | flops 1 | bytes 1 | tf_op jit(solution)/shard_map/prepare/pallas_call | solution.py:145
  9.4 4.1 %collective-permute-start.3 = (bf16[64,1024]{1,0:T(8,128)(2,1)S(1)}, bf16[64,1024]{1,0:T(8,128)(2,1)S(1)}, u32[]{:S(2)}, u32[]{:S(2)}) collective-permute-start(bf16[64,1024]{1,0:T(8,128)(2,1)S(1)} %get-tuple-element.46), channel_id=1, source_target_pairs={{0,8},{1,9},{2,10},{3,11},{4,12},{5,13},{6,14},{7,15},{8,0},{9,1},... | collective-permute-start | bytes 393224 | tf_op jit(solution)/shard_map/ppermute | solution.py:20
  13.5 1.4 %collective-permute-start.4 = (bf16[64,1024]{1,0:T(8,128)(2,1)S(1)}, bf16[64,1024]{1,0:T(8,128)(2,1)S(1)}, u32[]{:S(2)}, u32[]{:S(2)}) collective-permute-start(bf16[64,1024]{1,0:T(8,128)(2,1)S(1)} %get-tuple-element.47), channel_id=1, source_target_pairs={{0,12},{1,13},{2,14},{3,15},{4,8},{5,9},{6,10},{7,11},{8,4},{9,5},... | collective-permute-start | bytes 393224 | tf_op jit(solution)/shard_map/ppermute | solution.py:20
  14.8 1.5 %collective-permute-start = (bf16[64,1024]{1,0:T(8,128)(2,1)S(1)}, bf16[64,1024]{1,0:T(8,128)(2,1)S(1)}, u32[]{:S(2)}, u32[]{:S(2)}) collective-permute-start(bf16[64,1024]{1,0:T(8,128)(2,1)S(1)} %get-tuple-element.43), channel_id=1, source_target_pairs={{0,2},{1,3},{2,0},{3,1},{4,6},{5,7},{6,4},{7,5},{8,10},{9,11},{10,... | collective-permute-start | bytes 393224 | tf_op jit(solution)/shard_map/ppermute | solution.py:20
  16.3 0.0 collective-permute-done.5.refs_0_
  16.3 0.2 collective-permute-start.1
  16.6 0.0 collective-permute-done.6.refs_1_
  16.6 1.7 %collective-permute-start.2 = (bf16[64,1024]{1,0:T(8,128)(2,1)S(1)}, bf16[64,1024]{1,0:T(8,128)(2,1)S(1)}, u32[]{:S(2)}, u32[]{:S(2)}) collective-permute-start(bf16[64,1024]{1,0:T(8,128)(2,1)S(1)} %get-tuple-element.45), channel_id=1, source_target_pairs={{0,6},{1,7},{2,4},{3,5},{4,2},{5,3},{6,0},{7,1},{8,14},{9,15},{10,... | collective-permute-start | bytes 393224 | tf_op jit(solution)/shard_map/ppermute | solution.py:20
  18.3 3.5 %load.1 = (bf16[1024,2048]{1,0:T(8,128)(2,1)S(1)}, bf16[2048,1024]{1,0:T(8,128)(2,1)S(1)}) custom-call(bf16[1024,2048]{1,0:T(8,128)(2,1)} %collective-permute-done.5.refs_0_, bf16[2048,1024]{1,0:T(8,128)(2,1)} %collective-permute-done.6.refs_1_), custom_call_target="tpu_custom_call" | custom-call | flops 1 | bytes 1 | tf_op jit(solution)/shard_map/load/pallas_call | solution.py:185
  21.8 1.6 %collective-permute-done.3.refs_0_ = bf16[64,1024]{1,0:T(8,128)(2,1)S(1)} collective-permute-done((bf16[64,1024]{1,0:T(8,128)(2,1)S(1)}, bf16[64,1024]{1,0:T(8,128)(2,1)S(1)}, u32[]{:S(2)}, u32[]{:S(2)}) %collective-permute-start.3) | collective-permute-done | bytes 131104 | tf_op jit(solution)/shard_map/ppermute | solution.py:20
  23.4 1.1 %collective-permute-start.12 = (bf16[64,1024]{1,0:T(8,128)(2,1)S(1)}, bf16[64,1024]{1,0:T(8,128)(2,1)S(1)}, u32[]{:S(2)}, u32[]{:S(2)}) collective-permute-start(bf16[64,1024]{1,0:T(8,128)(2,1)S(1)} %get-tuple-element.63), channel_id=1, source_target_pairs={{0,10},{1,11},{2,8},{3,9},{4,14},{5,15},{6,12},{7,13},{8,2},{9,3},... | collective-permute-start | bytes 393224 | tf_op jit(solution)/shard_map/ppermute | solution.py:20
  24.5 0.0 collective-permute-done.4.refs_1_
  24.5 2.9 %collective-permute-start.13 = (bf16[64,1024]{1,0:T(8,128)(2,1)S(1)}, bf16[64,1024]{1,0:T(8,128)(2,1)S(1)}, u32[]{:S(2)}, u32[]{:S(2)}) collective-permute-start(bf16[64,1024]{1,0:T(8,128)(2,1)S(1)} %get-tuple-element.64), channel_id=1, source_target_pairs={{0,14},{1,15},{2,12},{3,13},{4,10},{5,11},{6,8},{7,9},{8,6},{9,7},... | collective-permute-start | bytes 393224 | tf_op jit(solution)/shard_map/ppermute | solution.py:20
  27.4 2.9 %expert.3 = (bf16[64,1024]{1,0:T(8,128)(2,1)S(1)}, bf16[64,1024]{1,0:T(8,128)(2,1)S(1)}) custom-call(bf16[64,1024]{1,0:T(8,128)(2,1)S(1)} %collective-permute-done.3.refs_0_, bf16[64,1024]{1,0:T(8,128)(2,1)S(1)} %collective-permute-done.4.refs_1_, bf16[1024,2048]{1,0:T(8,128)(2,1)S(1)} %get-tuple-element.48.refs_2_.refs_4_, ...), custom_call_target="tpu_custom_call" | custom-call | flops 1 | bytes 1 | tf_op jit(solution)/shard_map/expert/pallas_call | solution.py:269
  30.2 0.0 collective-permute-done.refs_1_
  30.3 2.2 %collective-permute-start.7 = (bf16[64,1024]{1,0:T(8,128)(2,1)S(1)}, bf16[64,1024]{1,0:T(8,128)(2,1)S(1)}, u32[]{:S(2)}, u32[]{:S(2)}) collective-permute-start(bf16[64,1024]{1,0:T(8,128)(2,1)S(1)} %get-tuple-element.52), channel_id=1, source_target_pairs={{0,8},{1,9},{2,10},{3,11},{4,12},{5,13},{6,14},{7,15},{8,0},{9,1},... | collective-permute-start | bytes 393224 | tf_op jit(solution)/shard_map/ppermute | solution.py:20
  32.5 0.0 collective-permute-done.1.refs_2_
  32.5 3.6 %collective-permute-start.8 = (bf16[64,1024]{1,0:T(8,128)(2,1)S(1)}, bf16[64,1024]{1,0:T(8,128)(2,1)S(1)}, u32[]{:S(2)}, u32[]{:S(2)}) collective-permute-start(bf16[64,1024]{1,0:T(8,128)(2,1)S(1)} %get-tuple-element.53), channel_id=1, source_target_pairs={{0,12},{1,13},{2,14},{3,15},{4,8},{5,9},{6,10},{7,11},{8,4},{9,5},... | collective-permute-start | bytes 393224 | tf_op jit(solution)/shard_map/ppermute | solution.py:20
  36.1 0.0 collective-permute-done.2.refs_3_
  36.1 5.1 %expert.4 = (bf16[64,1024]{1,0:T(8,128)(2,1)S(1)}, bf16[64,1024]{1,0:T(8,128)(2,1)S(1)}, bf16[64,1024]{1,0:T(8,128)(2,1)S(1)}, bf16[64,1024]{1,0:T(8,128)(2,1)S(1)}) custom-call(bf16[64,1024]{1,0:T(8,128)(2,1)S(1)} %get-tuple-element.42.refs_0_, bf16[64,1024]{1,0:T(8,128)(2,1)S(1)} %collective-permute-done.refs_1_, ...), custom_call_target="tpu_custom_call" | custom-call | flops 1 | bytes 1 | tf_op jit(solution)/shard_map/expert/pallas_call | solution.py:269
  41.2 0.5 collective-permute-start.9
  41.7 0.3 collective-permute-done.12.refs_0_
  42.0 0.0 collective-permute-start.10
  42.0 0.0 collective-permute-done.13.refs_1_
  42.0 3.9 %collective-permute-start.11 = (bf16[64,1024]{1,0:T(8,128)(2,1)S(1)}, bf16[64,1024]{1,0:T(8,128)(2,1)S(1)}, u32[]{:S(2)}, u32[]{:S(2)}) collective-permute-start(bf16[64,1024]{1,0:T(8,128)(2,1)S(1)} %get-tuple-element.60), channel_id=1, source_target_pairs={{0,6},{1,7},{2,4},{3,5},{4,2},{5,3},{6,0},{7,1},{8,14},{9,15},{10,... | collective-permute-start | bytes 393224 | tf_op jit(solution)/shard_map/ppermute | solution.py:20
  45.9 0.0 copy-start
  45.9 0.0 copy-start.1
  45.9 2.9 %expert.5 = (bf16[64,1024]{1,0:T(8,128)(2,1)S(1)}, bf16[64,1024]{1,0:T(8,128)(2,1)S(1)}) custom-call(bf16[64,1024]{1,0:T(8,128)(2,1)S(1)} %collective-permute-done.12.refs_0_, bf16[64,1024]{1,0:T(8,128)(2,1)S(1)} %collective-permute-done.13.refs_1_, bf16[1024,2048]{1,0:T(8,128)(2,1)S(1)} %get-tuple-element.48.refs_2_.refs_4_, ...), custom_call_target="tpu_custom_call" | custom-call | flops 1 | bytes 1 | tf_op jit(solution)/shard_map/expert/pallas_call | solution.py:269
  48.8 0.0 copy-start.2
  48.8 0.0 collective-permute-done.7.refs_1_
  48.8 0.3 collective-permute-start.14
  49.1 0.0 collective-permute-done.8.refs_2_
  49.1 2.6 %collective-permute-start.15 = (bf16[64,1024]{1,0:T(8,128)(2,1)S(1)}, bf16[64,1024]{1,0:T(8,128)(2,1)S(1)}, u32[]{:S(2)}, u32[]{:S(2)}) collective-permute-start(bf16[64,1024]{1,0:T(8,128)(2,1)S(1)} %get-tuple-element.68), channel_id=1, source_target_pairs={{0,14},{1,15},{2,12},{3,13},{4,10},{5,11},{6,8},{7,9},{8,6},{9,7},... | collective-permute-start | bytes 393224 | tf_op jit(solution)/shard_map/ppermute | solution.py:20
  51.7 0.0 copy-done
  51.7 0.0 copy-done.1
  51.7 0.5 gate.1
  52.2 0.4 add.3.so_far_ref
  52.6 0.0 collective-permute-done.9.refs_0_
  52.6 0.0 collective-permute-done.10.refs_1_
  52.6 0.0 collective-permute-done.11.refs_2_
  52.7 0.4 add.4.so_far_ref
  53.1 7.4 %collective-permute-done.14.refs_0_ = bf16[64,1024]{1,0:T(8,128)(2,1)S(1)} collective-permute-done((bf16[64,1024]{1,0:T(8,128)(2,1)S(1)}, bf16[64,1024]{1,0:T(8,128)(2,1)S(1)}, u32[]{:S(2)}, u32[]{:S(2)}) %collective-permute-start.14) | collective-permute-done | bytes 131104 | tf_op jit(solution)/shard_map/ppermute | solution.py:20
  60.5 0.0 collective-permute-done.15.refs_1_
  60.5 0.0 copy-done.2
  60.5 1.6 %finish.1 = bf16[384,1024]{1,0:T(8,128)(2,1)} custom-call(bf16[384,512]{1,0:T(8,128)(2,1)S(1)} %get-tuple-element.39.picking_ref, f32[384,1024]{1,0:T(8,128)S(1)} %add.4.so_far_ref, f32[384,1]{1,0:T(8,128)S(1)} %get-tuple-element.41.gate_ref, f32[1,1024]{1,0:T(1,128)S(1)} %bitcast.8, bf16[64,1024]{1,0:T(8,128)(2,1)S(1)} %collective-permute-done.14.refs_0_, ...), custom_call_target="tpu_custom_call" | custom-call | flops 1 | bytes 1 | tf_op jit(solution)/shard_map/finish/pallas_call | solution.py:324
Async XLA Ops:
  0.0 16.3 %collective-permute-start.5 = (bf16[1024,2048]{1,0:T(8,128)(2,1)}, bf16[1024,2048]{1,0:T(8,128)(2,1)}, u32[]{:S(2)}, u32[]{:S(2)}) collective-permute-start(bf16[1024,2048]{1,0:T(8,128)(2,1)} %in_hbm.1), channel_id=1, source_target_pairs={{0,1},{1,0},{2,3},{3,2},{4,5},{5,4},{6,7},{7,6},{8,9},{9,8},{10,11... | collective-permute-start | bytes 12582920 | tf_op jit(solution)/shard_map/ppermute | solution.py:20
  0.5 16.1 %collective-permute-start.6 = (bf16[2048,1024]{1,0:T(8,128)(2,1)}, bf16[2048,1024]{1,0:T(8,128)(2,1)}, u32[]{:S(2)}, u32[]{:S(2)}) collective-permute-start(bf16[2048,1024]{1,0:T(8,128)(2,1)} %out_hbm.1), channel_id=1, source_target_pairs={{0,1},{1,0},{2,3},{3,2},{4,5},{5,4},{6,7},{7,6},{8,9},{9,8},{10,11... | collective-permute-start | bytes 12582920 | tf_op jit(solution)/shard_map/ppermute | solution.py:20
  9.4 14.1 %collective-permute-start.3 = (bf16[64,1024]{1,0:T(8,128)(2,1)S(1)}, bf16[64,1024]{1,0:T(8,128)(2,1)S(1)}, u32[]{:S(2)}, u32[]{:S(2)}) collective-permute-start(bf16[64,1024]{1,0:T(8,128)(2,1)S(1)} %get-tuple-element.46), channel_id=1, source_target_pairs={{0,8},{1,9},{2,10},{3,11},{4,12},{5,13},{6,14},{7,15},{8,0},{9,1},... | collective-permute-start | bytes 393224 | tf_op jit(solution)/shard_map/ppermute | solution.py:20
  13.5 11.1 %collective-permute-start.4 = (bf16[64,1024]{1,0:T(8,128)(2,1)S(1)}, bf16[64,1024]{1,0:T(8,128)(2,1)S(1)}, u32[]{:S(2)}, u32[]{:S(2)}) collective-permute-start(bf16[64,1024]{1,0:T(8,128)(2,1)S(1)} %get-tuple-element.47), channel_id=1, source_target_pairs={{0,12},{1,13},{2,14},{3,15},{4,8},{5,9},{6,10},{7,11},{8,4},{9,5},... | collective-permute-start | bytes 393224 | tf_op jit(solution)/shard_map/ppermute | solution.py:20
  14.8 15.4 %collective-permute-start = (bf16[64,1024]{1,0:T(8,128)(2,1)S(1)}, bf16[64,1024]{1,0:T(8,128)(2,1)S(1)}, u32[]{:S(2)}, u32[]{:S(2)}) collective-permute-start(bf16[64,1024]{1,0:T(8,128)(2,1)S(1)} %get-tuple-element.43), channel_id=1, source_target_pairs={{0,2},{1,3},{2,0},{3,1},{4,6},{5,7},{6,4},{7,5},{8,10},{9,11},{10,... | collective-permute-start | bytes 393224 | tf_op jit(solution)/shard_map/ppermute | solution.py:20
  16.3 16.2 %collective-permute-start.1 = (bf16[64,1024]{1,0:T(8,128)(2,1)S(1)}, bf16[64,1024]{1,0:T(8,128)(2,1)S(1)}, u32[]{:S(2)}, u32[]{:S(2)}) collective-permute-start(bf16[64,1024]{1,0:T(8,128)(2,1)S(1)} %get-tuple-element.44), channel_id=1, source_target_pairs={{0,4},{1,5},{2,6},{3,7},{4,0},{5,1},{6,2},{7,3},{8,12},{9,13},{10,... | collective-permute-start | bytes 393224 | tf_op jit(solution)/shard_map/ppermute | solution.py:20
  16.6 19.6 %collective-permute-start.2 = (bf16[64,1024]{1,0:T(8,128)(2,1)S(1)}, bf16[64,1024]{1,0:T(8,128)(2,1)S(1)}, u32[]{:S(2)}, u32[]{:S(2)}) collective-permute-start(bf16[64,1024]{1,0:T(8,128)(2,1)S(1)} %get-tuple-element.45), channel_id=1, source_target_pairs={{0,6},{1,7},{2,4},{3,5},{4,2},{5,3},{6,0},{7,1},{8,14},{9,15},{10,... | collective-permute-start | bytes 393224 | tf_op jit(solution)/shard_map/ppermute | solution.py:20
  23.4 18.6 %collective-permute-start.12 = (bf16[64,1024]{1,0:T(8,128)(2,1)S(1)}, bf16[64,1024]{1,0:T(8,128)(2,1)S(1)}, u32[]{:S(2)}, u32[]{:S(2)}) collective-permute-start(bf16[64,1024]{1,0:T(8,128)(2,1)S(1)} %get-tuple-element.63), channel_id=1, source_target_pairs={{0,10},{1,11},{2,8},{3,9},{4,14},{5,15},{6,12},{7,13},{8,2},{9,3},... | collective-permute-start | bytes 393224 | tf_op jit(solution)/shard_map/ppermute | solution.py:20
  24.5 17.5 %collective-permute-start.13 = (bf16[64,1024]{1,0:T(8,128)(2,1)S(1)}, bf16[64,1024]{1,0:T(8,128)(2,1)S(1)}, u32[]{:S(2)}, u32[]{:S(2)}) collective-permute-start(bf16[64,1024]{1,0:T(8,128)(2,1)S(1)} %get-tuple-element.64), channel_id=1, source_target_pairs={{0,14},{1,15},{2,12},{3,13},{4,10},{5,11},{6,8},{7,9},{8,6},{9,7},... | collective-permute-start | bytes 393224 | tf_op jit(solution)/shard_map/ppermute | solution.py:20
  30.3 18.6 %collective-permute-start.7 = (bf16[64,1024]{1,0:T(8,128)(2,1)S(1)}, bf16[64,1024]{1,0:T(8,128)(2,1)S(1)}, u32[]{:S(2)}, u32[]{:S(2)}) collective-permute-start(bf16[64,1024]{1,0:T(8,128)(2,1)S(1)} %get-tuple-element.52), channel_id=1, source_target_pairs={{0,8},{1,9},{2,10},{3,11},{4,12},{5,13},{6,14},{7,15},{8,0},{9,1},... | collective-permute-start | bytes 393224 | tf_op jit(solution)/shard_map/ppermute | solution.py:20
  32.5 16.6 %collective-permute-start.8 = (bf16[64,1024]{1,0:T(8,128)(2,1)S(1)}, bf16[64,1024]{1,0:T(8,128)(2,1)S(1)}, u32[]{:S(2)}, u32[]{:S(2)}) collective-permute-start(bf16[64,1024]{1,0:T(8,128)(2,1)S(1)} %get-tuple-element.53), channel_id=1, source_target_pairs={{0,12},{1,13},{2,14},{3,15},{4,8},{5,9},{6,10},{7,11},{8,4},{9,5},... | collective-permute-start | bytes 393224 | tf_op jit(solution)/shard_map/ppermute | solution.py:20
  41.2 11.4 %collective-permute-start.9 = (bf16[64,1024]{1,0:T(8,128)(2,1)S(1)}, bf16[64,1024]{1,0:T(8,128)(2,1)S(1)}, u32[]{:S(2)}, u32[]{:S(2)}) collective-permute-start(bf16[64,1024]{1,0:T(8,128)(2,1)S(1)} %get-tuple-element.58), channel_id=1, source_target_pairs={{0,2},{1,3},{2,0},{3,1},{4,6},{5,7},{6,4},{7,5},{8,10},{9,11},{10,... | collective-permute-start | bytes 393224 | tf_op jit(solution)/shard_map/ppermute | solution.py:20
  42.0 10.6 %collective-permute-start.10 = (bf16[64,1024]{1,0:T(8,128)(2,1)S(1)}, bf16[64,1024]{1,0:T(8,128)(2,1)S(1)}, u32[]{:S(2)}, u32[]{:S(2)}) collective-permute-start(bf16[64,1024]{1,0:T(8,128)(2,1)S(1)} %get-tuple-element.59), channel_id=1, source_target_pairs={{0,4},{1,5},{2,6},{3,7},{4,0},{5,1},{6,2},{7,3},{8,12},{9,13},{10,... | collective-permute-start | bytes 393224 | tf_op jit(solution)/shard_map/ppermute | solution.py:20
  42.0 10.6 %collective-permute-start.11 = (bf16[64,1024]{1,0:T(8,128)(2,1)S(1)}, bf16[64,1024]{1,0:T(8,128)(2,1)S(1)}, u32[]{:S(2)}, u32[]{:S(2)}) collective-permute-start(bf16[64,1024]{1,0:T(8,128)(2,1)S(1)} %get-tuple-element.60), channel_id=1, source_target_pairs={{0,6},{1,7},{2,4},{3,5},{4,2},{5,3},{6,0},{7,1},{8,14},{9,15},{10,... | collective-permute-start | bytes 393224 | tf_op jit(solution)/shard_map/ppermute | solution.py:20
  45.9 5.7 %copy-start = (bf16[1024,8]{0,1:T(8,128)(2,1)S(1)}, bf16[1024,8]{0,1:T(8,128)(2,1)}, u32[]{:S(2)}) copy-start(bf16[1024,8]{0,1:T(8,128)(2,1)} %param.12) | copy-start | bytes 49156
  45.9 5.7 %copy-start.1 = (s32[1,384,1]{1,2,0:T(1,128)S(1)}, s32[1,384,1]{1,2,0:T(1,128)}, u32[]{:S(2)}) copy-start(s32[1,384,1]{1,2,0:T(1,128)} %param.10) | copy-start | bytes 4612
  48.8 11.7 %copy-start.2 = (f32[1024]{0:T(1024)S(1)}, f32[1024]{0:T(1024)}, u32[]{:S(2)}) copy-start(f32[1024]{0:T(1024)} %param.15) | copy-start | bytes 12292
  48.8 11.7 %collective-permute-start.14 = (bf16[64,1024]{1,0:T(8,128)(2,1)S(1)}, bf16[64,1024]{1,0:T(8,128)(2,1)S(1)}, u32[]{:S(2)}, u32[]{:S(2)}) collective-permute-start(bf16[64,1024]{1,0:T(8,128)(2,1)S(1)} %get-tuple-element.67), channel_id=1, source_target_pairs={{0,10},{1,11},{2,8},{3,9},{4,14},{5,15},{6,12},{7,13},{8,2},{9,3},... | collective-permute-start | bytes 393224 | tf_op jit(solution)/shard_map/ppermute | solution.py:20
  49.1 11.4 %collective-permute-start.15 = (bf16[64,1024]{1,0:T(8,128)(2,1)S(1)}, bf16[64,1024]{1,0:T(8,128)(2,1)S(1)}, u32[]{:S(2)}, u32[]{:S(2)}) collective-permute-start(bf16[64,1024]{1,0:T(8,128)(2,1)S(1)} %get-tuple-element.68), channel_id=1, source_target_pairs={{0,14},{1,15},{2,12},{3,13},{4,10},{5,11},{6,8},{7,9},{8,6},{9,7},... | collective-permute-start | bytes 393224 | tf_op jit(solution)/shard_map/ppermute | solution.py:20

commit v4 on v3

--- a/solution.py
+++ b/solution.py
@@ -49,7 +49,8 @@
 
 def pre_kernel(cap, pitch, count_ref, me_ref, frames_hbm, ids_hbm, taps_hbm, in_hbm, out_hbm, *rest):
     in_ref, out_ref, stream_ref, expert_in_ref, slot_ref, *rest = rest
-    *message_refs, frames_ref, taps_ref, ids_ref, padded, conv, frame_sems, taps_sem, ids_sem, weight_sems = rest
+    *message_refs, frames_ref, taps_ref, ids_ref, padded, taps_by_row, weights, pieces, conv = rest[:-4]
+    frame_sems, taps_sem, ids_sem, weight_sems = rest[-4:]
     length, width = frames_ref.shape
     taps = taps_ref.shape[0]
     reach = taps // 2
@@ -72,37 +73,86 @@
         pltpu.make_async_copy(in_hbm, in_ref, weight_sems.at[0]),
         pltpu.make_async_copy(out_hbm, out_ref, weight_sems.at[1]),
     ]
-    lead = padded.shape[1] - length - reach
-    padded[:, :lead, :] = jnp.zeros((groups, lead, LANES), jnp.float32)
-    padded[:, lead + length :, :] = jnp.zeros((groups, reach, LANES), jnp.float32)
+    phases = 4
+    depth = weights.shape[1] // groups
+    edge = jnp.zeros((reach * groups, LANES), jnp.float32)
+    padded[: reach * groups, :] = edge
+    tail = (reach + length) * groups
+    padded[tail:, :] = jnp.zeros((padded.shape[0] - tail, LANES), jnp.float32)
+    taps_by_row[taps * groups :, :] = jnp.zeros(((phases * depth - taps) * groups, LANES), jnp.float32)
+    taps_copy.wait()
+    for group in range(groups):
+        lanes = slice(group * LANES, (group + 1) * LANES)
+        taps_by_row[pl.ds(group, taps, stride=groups), :] = taps_ref[:, lanes]
+    for step in range(depth):
+        w = [taps_by_row[(phases * step + i) * groups : (phases * step + i + 1) * groups, :] for i in range(phases)]
+        halves = ((w[0] + w[1], w[2] + w[3]), (w[0], w[2]), (w[1], w[3]))
+        for number, (even, odd) in enumerate(halves):
+            for kind, value in enumerate((even + odd, even, odd)):
+                weights[3 * number + kind, step * groups : (step + 1) * groups, :] = value
+
     for number, start in enumerate(range(0, length, BLOCK)):
         frame_copies[number].wait()
         values = frames_ref[start : start + BLOCK, :].astype(jnp.float32)
         position = start + lax.broadcasted_iota(jnp.int32, (BLOCK, 1), 0)
         normed = jnp.where(position < count, normalise(values), 0.0)
         for group in range(groups):
-            padded[group, lead + start : lead + start + BLOCK, :] = normed[:, group * LANES : (group + 1) * LANES]
-
+            lanes = slice(group * LANES, (group + 1) * LANES)
+            padded[pl.ds((reach + start) * groups + group, BLOCK, stride=groups), :] = normed[:, lanes]
     for copy in weight_copies:
         copy.start()
-    taps_copy.wait()
-
-    def convolve(index, carry):
-        group = lax.rem(index, groups)
-        start = pl.multiple_of(lax.div(index, groups) * BLOCK, BLOCK)
-        lanes = pl.ds(pl.multiple_of(group * LANES, LANES), LANES)
-        total = None
-        for tap in range(taps):
-            term = taps_ref[pl.ds(tap, 1), lanes] * padded[group, pl.ds(start + (lead - reach + tap), BLOCK), :]
-            total = term if tap == 0 else total + term
-        conv[pl.ds(start, BLOCK), lanes] = total
+
+    def split(index, carry):
+        base = pl.multiple_of(index * (phases * ROWS * groups), phases * ROWS * groups)
+        here = pl.multiple_of(index * (ROWS * groups), ROWS * groups)
+        p = [padded[pl.ds(base + i * groups, groups), :] for i in range(phases * ROWS + 3)]
+        pairs = 2 * ROWS + 1
+        streams = (
+            [p[2 * i + 1] for i in range(pairs)],
+            [p[2 * i] - p[2 * i + 1] for i in range(pairs)],
+            [p[2 * i + 2] - p[2 * i + 1] for i in range(pairs)],
+        )
+        for number, q in enumerate(streams):
+            for row in range(ROWS):
+                trio = (q[2 * row + 1], q[2 * row] - q[2 * row + 1], q[2 * row + 2] - q[2 * row + 1])
+                for kind, value in enumerate(trio):
+                    pieces[3 * number + kind, pl.ds(here + row * groups, groups), :] = value
         return carry
 
-    lax.fori_loop(0, groups * (length // BLOCK), convolve, 0)
+    lax.fori_loop(0, pieces.shape[1] // (ROWS * groups), split, 0)
+
+    def correlate(index, carry):
+        here = pl.multiple_of(index * (ROWS * groups), ROWS * groups)
+        base = pl.multiple_of(index * (phases * ROWS * groups), phases * ROWS * groups)
+
+        def piece(number):
+            window = [pieces[number, pl.ds(here + i * groups, groups), :] for i in range(ROWS + depth - 1)]
+            sums = None
+            for step in range(depth):
+                weight = weights[number, step * groups : (step + 1) * groups, :]
+                terms = [weight * window[row + step] for row in range(ROWS)]
+                sums = terms if sums is None else [a + b for a, b in zip(sums, terms)]
+            return sums
+
+        shared = piece(0)
+        common = [[a + b for a, b in zip(shared, piece(1 + kind))] for kind in range(2)]
+        for parity in range(2):
+            shared = piece(3 + 3 * parity)
+            for kind in range(2):
+                last = piece(4 + 3 * parity + kind)
+                for row in range(ROWS):
+                    at = base + (phases * row + 2 * kind + parity) * groups
+                    conv[pl.ds(at, groups), :] = (shared[row] + last[row]) + common[kind][row]
+        return carry
+
+    lax.fori_loop(0, length // (phases * ROWS), correlate, 0)
 
     for start in range(0, length, BLOCK):
         rows = slice(start, start + BLOCK)
-        stream = (frames_ref[rows, :].astype(jnp.float32) + silu(conv[rows, :])).astype(jnp.bfloat16)
+        mixed = jnp.concatenate(
+            [conv[pl.ds(start * groups + group, BLOCK, stride=groups), :] for group in range(groups)], axis=1
+        )
+        stream = (frames_ref[rows, :].astype(jnp.float32) + silu(mixed)).astype(jnp.bfloat16)
         stream_ref[rows, :] = stream
         expert_in_ref[rows, :] = normalise(stream.astype(jnp.float32)).astype(jnp.bfloat16)
 
@@ -140,6 +190,8 @@
     reach = taps.shape[0] // 2
     whole = pl.BlockSpec(memory_space=pltpu.VMEM)
     anywhere = pl.BlockSpec(memory_space=pl.ANY)
+    depth = -(-taps.shape[0] // 4)
+    steps = length // 4 + -(-(depth - 1) // ROWS) * ROWS
     span = chips * pitch // messages
     bf16 = jnp.bfloat16
     return pl.pallas_call(
@@ -158,8 +210,11 @@
             pltpu.VMEM((length, width), bf16),
             pltpu.VMEM(taps.shape, jnp.float32),
             pltpu.VMEM(ids.shape, jnp.int32),
-            pltpu.VMEM((groups, -(-reach // 8) * 8 + length + reach, LANES), jnp.float32),
-            pltpu.VMEM((length, width), jnp.float32),
+            pltpu.VMEM(((4 * steps + 8) * groups, LANES), jnp.float32),
+            pltpu.VMEM((4 * depth * groups, LANES), jnp.float32),
+            pltpu.VMEM((9, depth * groups, LANES), jnp.float32),
+            pltpu.VMEM((9, steps * groups, LANES), jnp.float32),
+            pltpu.VMEM((length * groups, LANES), jnp.float32),
             pltpu.SemaphoreType.DMA((length // BLOCK,)),
             pltpu.SemaphoreType.DMA,
             pltpu.SemaphoreType.DMA,
@@ -370,11 +425,13 @@
         second_out = run_expert(after([arrived[d] for d in second], (first_out, close)), weights)
         for d, part in zip(second, second_out):
             results[d] = send(part, d)
-        for d, part in zip(near, close[1:]):
+        for d, part in zip(near[:2], close[1:3]):
+            results[d] = send(part, d)
+        for d, part in zip(near[2:], after(close[3:], second_out)):
             results[d] = send(part, d)
         total = add_results(stream, gate, picking, {d: results[d] for d in [0] + first})
-        total = add_results(total, gate, picking, {d: results[d] for d in near})
-        output = add_results(total, gate, picking, {d: results[d] for d in second}, gain)
+        total = add_results(total, gate, picking, {d: results[d] for d in near[:2]})
+        output = add_results(total, gate, picking, {d: results[d] for d in second + near[2:]}, gain)
     else:
         home = jnp.zeros((1,), jnp.int32)
         own_in, own_out, stream, expert_in, slot, message = prepare(

time: 62.5 us -> 60.2 us (0.963)
  Pallas kernels: 25.4 us -> 24.1 us
    pallas_call x1, Pallas kernels: 8.19 us -> 6.79 us  [prepare(): pl.pallas_call(functools.partial(pre_kernel, cap, pitch), in_specs=[pl.Bl...]
  transfers between devices with their start and end apart: 16 -> 16, of which waited for: 3 -> 3; matrix products, arithmetic and copies ran while one was open for 0% -> 0% of each run, Pallas kernels for 38% -> 37%
where the time goes in v4:
time: 60.2 us; the launch traced here: 60 us
  starting transfers between devices  26.1 us (43%)
  Pallas kernels  24.1 us (40%)
  waiting for transfers between devices  9.05 us (15%)
  between operations  0.79 us (1%)
    ppermute x16, starting transfers between devices, xor_route(): return lax.ppermute(block, axis, [(i, i ^ distance) for i in range(count)])  26.1 us
    pallas_call x3, Pallas kernels, run_expert(): pl.pallas_call(functools.partial(expert_kernel, count, min(1024, hidden))...  10.8 us
    ppermute x16, waiting for transfers between devices, xor_route(): return lax.ppermute(block, axis, [(i, i ^ distance) for i in range(count)])  9.05 us
    pallas_call x1, Pallas kernels, prepare(): pl.pallas_call(functools.partial(pre_kernel, cap, pitch), in_specs=[pl.Bl...  6.79 us
    pallas_call x1, Pallas kernels, load(): pl.pallas_call(functools.partial(load_kernel, count), in_specs=[pl.BlockS...  3.48 us
    pallas_call x3, Pallas kernels, add_results(): pl.pallas_call(functools.partial(close_kernel if last else add_kernel, le...  2.44 us
  transfers between devices with their start and end apart: 16, of which 3 were waited for; matrix products, arithmetic and copies ran while one was open for 0% of the time, Pallas kernels for 37%

profile of v4, /device:TPU:0, one launch (start us, length us, event | category | flops | bytes accessed | tf_op | source)
XLA Modules:
  0.0 60.0 jit_solution(2713664576369978573)
XLA Ops:
  0.0 0.5 collective-permute-start.5
  0.5 0.1 collective-permute-start.6
  1.2 6.8 %prepare.1 = (bf16[1024,2048]{1,0:T(8,128)(2,1)S(1)}, bf16[2048,1024]{1,0:T(8,128)(2,1)S(1)}, bf16[384,1024]{1,0:T(8,128)(2,1)S(1)}, bf16[384,1024]{1,0:T(8,128)...) custom-call(s32[1]{0:T(128)S(6)} %copy.9.count_ref, ...), custom_call_target="tpu_custom_call" | custom-call | flops 1 | bytes 1 | tf_op jit(solution)/shard_map/prepare/pallas_call | solution.py:197
  8.0 4.1 %collective-permute-start.3 = (bf16[64,1024]{1,0:T(8,128)(2,1)S(1)}, bf16[64,1024]{1,0:T(8,128)(2,1)S(1)}, u32[]{:S(2)}, u32[]{:S(2)}) collective-permute-start(bf16[64,1024]{1,0:T(8,128)(2,1)S(1)} %get-tuple-element.47), channel_id=1, source_target_pairs={{0,8},{1,9},{2,10},{3,11},{4,12},{5,13},{6,14},{7,15},{8,0},{9,1},... | collective-permute-start | bytes 393224 | tf_op jit(solution)/shard_map/ppermute | solution.py:20
  12.1 1.3 %collective-permute-start.4 = (bf16[64,1024]{1,0:T(8,128)(2,1)S(1)}, bf16[64,1024]{1,0:T(8,128)(2,1)S(1)}, u32[]{:S(2)}, u32[]{:S(2)}) collective-permute-start(bf16[64,1024]{1,0:T(8,128)(2,1)S(1)} %get-tuple-element.48), channel_id=1, source_target_pairs={{0,12},{1,13},{2,14},{3,15},{4,8},{5,9},{6,10},{7,11},{8,4},{9,5},... | collective-permute-start | bytes 393224 | tf_op jit(solution)/shard_map/ppermute | solution.py:20
  13.4 1.5 %collective-permute-start = (bf16[64,1024]{1,0:T(8,128)(2,1)S(1)}, bf16[64,1024]{1,0:T(8,128)(2,1)S(1)}, u32[]{:S(2)}, u32[]{:S(2)}) collective-permute-start(bf16[64,1024]{1,0:T(8,128)(2,1)S(1)} %get-tuple-element.44), channel_id=1, source_target_pairs={{0,2},{1,3},{2,0},{3,1},{4,6},{5,7},{6,4},{7,5},{8,10},{9,11},{10,... | collective-permute-start | bytes 393224 | tf_op jit(solution)/shard_map/ppermute | solution.py:20
  14.9 0.0 collective-permute-done.5.refs_0_
  14.9 0.2 collective-permute-start.1
  15.2 0.0 collective-permute-done.6.refs_1_
  15.2 2.3 %collective-permute-start.2 = (bf16[64,1024]{1,0:T(8,128)(2,1)S(1)}, bf16[64,1024]{1,0:T(8,128)(2,1)S(1)}, u32[]{:S(2)}, u32[]{:S(2)}) collective-permute-start(bf16[64,1024]{1,0:T(8,128)(2,1)S(1)} %get-tuple-element.46), channel_id=1, source_target_pairs={{0,6},{1,7},{2,4},{3,5},{4,2},{5,3},{6,0},{7,1},{8,14},{9,15},{10,... | collective-permute-start | bytes 393224 | tf_op jit(solution)/shard_map/ppermute | solution.py:20
  17.5 3.5 %load.1 = (bf16[1024,2048]{1,0:T(8,128)(2,1)S(1)}, bf16[2048,1024]{1,0:T(8,128)(2,1)S(1)}) custom-call(bf16[1024,2048]{1,0:T(8,128)(2,1)} %collective-permute-done.5.refs_0_, bf16[2048,1024]{1,0:T(8,128)(2,1)} %collective-permute-done.6.refs_1_), custom_call_target="tpu_custom_call" | custom-call | flops 1 | bytes 1 | tf_op jit(solution)/shard_map/load/pallas_call | solution.py:240
  21.0 1.1 %collective-permute-done.3.refs_0_ = bf16[64,1024]{1,0:T(8,128)(2,1)S(1)} collective-permute-done((bf16[64,1024]{1,0:T(8,128)(2,1)S(1)}, bf16[64,1024]{1,0:T(8,128)(2,1)S(1)}, u32[]{:S(2)}, u32[]{:S(2)}) %collective-permute-start.3) | collective-permute-done | bytes 131104 | tf_op jit(solution)/shard_map/ppermute | solution.py:20
  22.0 1.5 %collective-permute-start.11 = (bf16[64,1024]{1,0:T(8,128)(2,1)S(1)}, bf16[64,1024]{1,0:T(8,128)(2,1)S(1)}, u32[]{:S(2)}, u32[]{:S(2)}) collective-permute-start(bf16[64,1024]{1,0:T(8,128)(2,1)S(1)} %get-tuple-element.63), channel_id=1, source_target_pairs={{0,10},{1,11},{2,8},{3,9},{4,14},{5,15},{6,12},{7,13},{8,2},{9,3},... | collective-permute-start | bytes 393224 | tf_op jit(solution)/shard_map/ppermute | solution.py:20
  23.6 0.0 collective-permute-done.4.refs_1_
  23.6 2.4 %collective-permute-start.12 = (bf16[64,1024]{1,0:T(8,128)(2,1)S(1)}, bf16[64,1024]{1,0:T(8,128)(2,1)S(1)}, u32[]{:S(2)}, u32[]{:S(2)}) collective-permute-start(bf16[64,1024]{1,0:T(8,128)(2,1)S(1)} %get-tuple-element.64), channel_id=1, source_target_pairs={{0,14},{1,15},{2,12},{3,13},{4,10},{5,11},{6,8},{7,9},{8,6},{9,7},... | collective-permute-start | bytes 393224 | tf_op jit(solution)/shard_map/ppermute | solution.py:20
  26.0 2.9 %expert.3 = (bf16[64,1024]{1,0:T(8,128)(2,1)S(1)}, bf16[64,1024]{1,0:T(8,128)(2,1)S(1)}) custom-call(bf16[64,1024]{1,0:T(8,128)(2,1)S(1)} %collective-permute-done.3.refs_0_, bf16[64,1024]{1,0:T(8,128)(2,1)S(1)} %collective-permute-done.4.refs_1_, bf16[1024,2048]{1,0:T(8,128)(2,1)S(1)} %get-tuple-element.49.refs_2_.refs_4_, ...), custom_call_target="tpu_custom_call" | custom-call | flops 1 | bytes 1 | tf_op jit(solution)/shard_map/expert/pallas_call | solution.py:324
  28.8 0.0 collective-permute-done.refs_1_
  28.9 2.0 %collective-permute-start.7 = (bf16[64,1024]{1,0:T(8,128)(2,1)S(1)}, bf16[64,1024]{1,0:T(8,128)(2,1)S(1)}, u32[]{:S(2)}, u32[]{:S(2)}) collective-permute-start(bf16[64,1024]{1,0:T(8,128)(2,1)S(1)} %get-tuple-element.53), channel_id=1, source_target_pairs={{0,8},{1,9},{2,10},{3,11},{4,12},{5,13},{6,14},{7,15},{8,0},{9,1},... | collective-permute-start | bytes 393224 | tf_op jit(solution)/shard_map/ppermute | solution.py:20
  30.9 0.0 collective-permute-done.1.refs_2_
  30.9 2.8 %collective-permute-start.8 = (bf16[64,1024]{1,0:T(8,128)(2,1)S(1)}, bf16[64,1024]{1,0:T(8,128)(2,1)S(1)}, u32[]{:S(2)}, u32[]{:S(2)}) collective-permute-start(bf16[64,1024]{1,0:T(8,128)(2,1)S(1)} %get-tuple-element.54), channel_id=1, source_target_pairs={{0,12},{1,13},{2,14},{3,15},{4,8},{5,9},{6,10},{7,11},{8,4},{9,5},... | collective-permute-start | bytes 393224 | tf_op jit(solution)/shard_map/ppermute | solution.py:20
  33.7 0.0 collective-permute-done.2.refs_3_
  33.7 5.1 %expert.4 = (bf16[64,1024]{1,0:T(8,128)(2,1)S(1)}, bf16[64,1024]{1,0:T(8,128)(2,1)S(1)}, bf16[64,1024]{1,0:T(8,128)(2,1)S(1)}, bf16[64,1024]{1,0:T(8,128)(2,1)S(1)}) custom-call(bf16[64,1024]{1,0:T(8,128)(2,1)S(1)} %get-tuple-element.43.refs_0_, bf16[64,1024]{1,0:T(8,128)(2,1)S(1)} %collective-permute-done.refs_1_, ...), custom_call_target="tpu_custom_call" | custom-call | flops 1 | bytes 1 | tf_op jit(solution)/shard_map/expert/pallas_call | solution.py:324
  38.8 0.6 collective-permute-start.9
  39.3 1.4 %collective-permute-done.11.refs_0_ = bf16[64,1024]{1,0:T(8,128)(2,1)S(1)} collective-permute-done((bf16[64,1024]{1,0:T(8,128)(2,1)S(1)}, bf16[64,1024]{1,0:T(8,128)(2,1)S(1)}, u32[]{:S(2)}, u32[]{:S(2)}) %collective-permute-start.11) | collective-permute-done | bytes 131104 | tf_op jit(solution)/shard_map/ppermute | solution.py:20
  40.7 0.0 collective-permute-start.10
  40.7 0.0 collective-permute-done.12.refs_1_
  40.7 0.0 copy-start
  40.7 0.0 copy-start.1
  40.7 2.9 %expert.5 = (bf16[64,1024]{1,0:T(8,128)(2,1)S(1)}, bf16[64,1024]{1,0:T(8,128)(2,1)S(1)}) custom-call(bf16[64,1024]{1,0:T(8,128)(2,1)S(1)} %collective-permute-done.11.refs_0_, bf16[64,1024]{1,0:T(8,128)(2,1)S(1)} %collective-permute-done.12.refs_1_, bf16[1024,2048]{1,0:T(8,128)(2,1)S(1)} %get-tuple-element.49.refs_2_.refs_4_, ...), custom_call_target="tpu_custom_call" | custom-call | flops 1 | bytes 1 | tf_op jit(solution)/shard_map/expert/pallas_call | solution.py:324
  43.6 0.0 copy-start.2
  43.6 4.2 %collective-permute-start.13 = (bf16[64,1024]{1,0:T(8,128)(2,1)S(1)}, bf16[64,1024]{1,0:T(8,128)(2,1)S(1)}, u32[]{:S(2)}, u32[]{:S(2)}) collective-permute-start(bf16[64,1024]{1,0:T(8,128)(2,1)S(1)} %get-tuple-element.68), channel_id=1, source_target_pairs={{0,10},{1,11},{2,8},{3,9},{4,14},{5,15},{6,12},{7,13},{8,2},{9,3},... | collective-permute-start | bytes 393224 | tf_op jit(solution)/shard_map/ppermute | solution.py:20
  47.8 0.0 collective-permute-done.7.refs_1_
  47.8 0.0 collective-permute-start.15
  47.8 0.0 collective-permute-done.8.refs_2_
  47.8 2.6 %collective-permute-start.14 = (bf16[64,1024]{1,0:T(8,128)(2,1)S(1)}, bf16[64,1024]{1,0:T(8,128)(2,1)S(1)}, u32[]{:S(2)}, u32[]{:S(2)}) collective-permute-start(bf16[64,1024]{1,0:T(8,128)(2,1)S(1)} %get-tuple-element.69), channel_id=1, source_target_pairs={{0,14},{1,15},{2,12},{3,13},{4,10},{5,11},{6,8},{7,9},{8,6},{9,7},... | collective-permute-start | bytes 393224 | tf_op jit(solution)/shard_map/ppermute | solution.py:20
  50.4 0.0 copy-done
  50.4 0.0 copy-done.1
  50.4 0.5 gate.1
  50.9 0.4 add.3.so_far_ref
  51.3 0.0 collective-permute-done.9.refs_0_
  51.4 0.0 collective-permute-done.10.refs_1_
  51.4 0.4 add.4.so_far_ref
  51.8 6.6 %collective-permute-done.15.refs_2_ = bf16[64,1024]{1,0:T(8,128)(2,1)S(1)} collective-permute-done((bf16[64,1024]{1,0:T(8,128)(2,1)S(1)}, bf16[64,1024]{1,0:T(8,128)(2,1)S(1)}, u32[]{:S(2)}, u32[]{:S(2)}) %collective-permute-start.15) | collective-permute-done | bytes 131104 | tf_op jit(solution)/shard_map/ppermute | solution.py:20
  58.4 0.0 collective-permute-done.13.refs_0_
  58.4 0.0 collective-permute-done.14.refs_1_
  58.4 0.0 copy-done.2
  58.4 1.6 %finish.1 = bf16[384,1024]{1,0:T(8,128)(2,1)} custom-call(bf16[384,512]{1,0:T(8,128)(2,1)S(1)} %get-tuple-element.40.picking_ref, f32[384,1024]{1,0:T(8,128)S(1)} %add.4.so_far_ref, f32[384,1]{1,0:T(8,128)S(1)} %get-tuple-element.42.gate_ref, f32[1,1024]{1,0:T(1,128)S(1)} %bitcast.8, bf16[64,1024]{1,0:T(8,128)(2,1)S(1)} %collective-permute-done.13.refs_0_, ...), custom_call_target="tpu_custom_call" | custom-call | flops 1 | bytes 1 | tf_op jit(solution)/shard_map/finish/pallas_call | solution.py:379
Async XLA Ops:
  0.0 14.9 %collective-permute-start.5 = (bf16[1024,2048]{1,0:T(8,128)(2,1)}, bf16[1024,2048]{1,0:T(8,128)(2,1)}, u32[]{:S(2)}, u32[]{:S(2)}) collective-permute-start(bf16[1024,2048]{1,0:T(8,128)(2,1)} %in_hbm.1), channel_id=1, source_target_pairs={{0,1},{1,0},{2,3},{3,2},{4,5},{5,4},{6,7},{7,6},{8,9},{9,8},{10,11... | collective-permute-start | bytes 12582920 | tf_op jit(solution)/shard_map/ppermute | solution.py:20
  0.5 14.7 %collective-permute-start.6 = (bf16[2048,1024]{1,0:T(8,128)(2,1)}, bf16[2048,1024]{1,0:T(8,128)(2,1)}, u32[]{:S(2)}, u32[]{:S(2)}) collective-permute-start(bf16[2048,1024]{1,0:T(8,128)(2,1)} %out_hbm.1), channel_id=1, source_target_pairs={{0,1},{1,0},{2,3},{3,2},{4,5},{5,4},{6,7},{7,6},{8,9},{9,8},{10,11... | collective-permute-start | bytes 12582920 | tf_op jit(solution)/shard_map/ppermute | solution.py:20
  8.0 14.1 %collective-permute-start.3 = (bf16[64,1024]{1,0:T(8,128)(2,1)S(1)}, bf16[64,1024]{1,0:T(8,128)(2,1)S(1)}, u32[]{:S(2)}, u32[]{:S(2)}) collective-permute-start(bf16[64,1024]{1,0:T(8,128)(2,1)S(1)} %get-tuple-element.47), channel_id=1, source_target_pairs={{0,8},{1,9},{2,10},{3,11},{4,12},{5,13},{6,14},{7,15},{8,0},{9,1},... | collective-permute-start | bytes 393224 | tf_op jit(solution)/shard_map/ppermute | solution.py:20
  12.1 11.5 %collective-permute-start.4 = (bf16[64,1024]{1,0:T(8,128)(2,1)S(1)}, bf16[64,1024]{1,0:T(8,128)(2,1)S(1)}, u32[]{:S(2)}, u32[]{:S(2)}) collective-permute-start(bf16[64,1024]{1,0:T(8,128)(2,1)S(1)} %get-tuple-element.48), channel_id=1, source_target_pairs={{0,12},{1,13},{2,14},{3,15},{4,8},{5,9},{6,10},{7,11},{8,4},{9,5},... | collective-permute-start | bytes 393224 | tf_op jit(solution)/shard_map/ppermute | solution.py:20
  13.4 15.4 %collective-permute-start = (bf16[64,1024]{1,0:T(8,128)(2,1)S(1)}, bf16[64,1024]{1,0:T(8,128)(2,1)S(1)}, u32[]{:S(2)}, u32[]{:S(2)}) collective-permute-start(bf16[64,1024]{1,0:T(8,128)(2,1)S(1)} %get-tuple-element.44), channel_id=1, source_target_pairs={{0,2},{1,3},{2,0},{3,1},{4,6},{5,7},{6,4},{7,5},{8,10},{9,11},{10,... | collective-permute-start | bytes 393224 | tf_op jit(solution)/shard_map/ppermute | solution.py:20
  14.9 15.9 %collective-permute-start.1 = (bf16[64,1024]{1,0:T(8,128)(2,1)S(1)}, bf16[64,1024]{1,0:T(8,128)(2,1)S(1)}, u32[]{:S(2)}, u32[]{:S(2)}) collective-permute-start(bf16[64,1024]{1,0:T(8,128)(2,1)S(1)} %get-tuple-element.45), channel_id=1, source_target_pairs={{0,4},{1,5},{2,6},{3,7},{4,0},{5,1},{6,2},{7,3},{8,12},{9,13},{10,... | collective-permute-start | bytes 393224 | tf_op jit(solution)/shard_map/ppermute | solution.py:20
  15.2 18.5 %collective-permute-start.2 = (bf16[64,1024]{1,0:T(8,128)(2,1)S(1)}, bf16[64,1024]{1,0:T(8,128)(2,1)S(1)}, u32[]{:S(2)}, u32[]{:S(2)}) collective-permute-start(bf16[64,1024]{1,0:T(8,128)(2,1)S(1)} %get-tuple-element.46), channel_id=1, source_target_pairs={{0,6},{1,7},{2,4},{3,5},{4,2},{5,3},{6,0},{7,1},{8,14},{9,15},{10,... | collective-permute-start | bytes 393224 | tf_op jit(solution)/shard_map/ppermute | solution.py:20
  22.0 18.7 %collective-permute-start.11 = (bf16[64,1024]{1,0:T(8,128)(2,1)S(1)}, bf16[64,1024]{1,0:T(8,128)(2,1)S(1)}, u32[]{:S(2)}, u32[]{:S(2)}) collective-permute-start(bf16[64,1024]{1,0:T(8,128)(2,1)S(1)} %get-tuple-element.63), channel_id=1, source_target_pairs={{0,10},{1,11},{2,8},{3,9},{4,14},{5,15},{6,12},{7,13},{8,2},{9,3},... | collective-permute-start | bytes 393224 | tf_op jit(solution)/shard_map/ppermute | solution.py:20
  23.6 17.1 %collective-permute-start.12 = (bf16[64,1024]{1,0:T(8,128)(2,1)S(1)}, bf16[64,1024]{1,0:T(8,128)(2,1)S(1)}, u32[]{:S(2)}, u32[]{:S(2)}) collective-permute-start(bf16[64,1024]{1,0:T(8,128)(2,1)S(1)} %get-tuple-element.64), channel_id=1, source_target_pairs={{0,14},{1,15},{2,12},{3,13},{4,10},{5,11},{6,8},{7,9},{8,6},{9,7},... | collective-permute-start | bytes 393224 | tf_op jit(solution)/shard_map/ppermute | solution.py:20
  28.9 18.9 %collective-permute-start.7 = (bf16[64,1024]{1,0:T(8,128)(2,1)S(1)}, bf16[64,1024]{1,0:T(8,128)(2,1)S(1)}, u32[]{:S(2)}, u32[]{:S(2)}) collective-permute-start(bf16[64,1024]{1,0:T(8,128)(2,1)S(1)} %get-tuple-element.53), channel_id=1, source_target_pairs={{0,8},{1,9},{2,10},{3,11},{4,12},{5,13},{6,14},{7,15},{8,0},{9,1},... | collective-permute-start | bytes 393224 | tf_op jit(solution)/shard_map/ppermute | solution.py:20
  30.9 16.9 %collective-permute-start.8 = (bf16[64,1024]{1,0:T(8,128)(2,1)S(1)}, bf16[64,1024]{1,0:T(8,128)(2,1)S(1)}, u32[]{:S(2)}, u32[]{:S(2)}) collective-permute-start(bf16[64,1024]{1,0:T(8,128)(2,1)S(1)} %get-tuple-element.54), channel_id=1, source_target_pairs={{0,12},{1,13},{2,14},{3,15},{4,8},{5,9},{6,10},{7,11},{8,4},{9,5},... | collective-permute-start | bytes 393224 | tf_op jit(solution)/shard_map/ppermute | solution.py:20
  38.8 12.6 %collective-permute-start.9 = (bf16[64,1024]{1,0:T(8,128)(2,1)S(1)}, bf16[64,1024]{1,0:T(8,128)(2,1)S(1)}, u32[]{:S(2)}, u32[]{:S(2)}) collective-permute-start(bf16[64,1024]{1,0:T(8,128)(2,1)S(1)} %get-tuple-element.59), channel_id=1, source_target_pairs={{0,2},{1,3},{2,0},{3,1},{4,6},{5,7},{6,4},{7,5},{8,10},{9,11},{10,... | collective-permute-start | bytes 393224 | tf_op jit(solution)/shard_map/ppermute | solution.py:20
  40.7 10.6 %collective-permute-start.10 = (bf16[64,1024]{1,0:T(8,128)(2,1)S(1)}, bf16[64,1024]{1,0:T(8,128)(2,1)S(1)}, u32[]{:S(2)}, u32[]{:S(2)}) collective-permute-start(bf16[64,1024]{1,0:T(8,128)(2,1)S(1)} %get-tuple-element.60), channel_id=1, source_target_pairs={{0,4},{1,5},{2,6},{3,7},{4,0},{5,1},{6,2},{7,3},{8,12},{9,13},{10,... | collective-permute-start | bytes 393224 | tf_op jit(solution)/shard_map/ppermute | solution.py:20
  40.7 9.7 %copy-start = (bf16[1024,8]{0,1:T(8,128)(2,1)S(1)}, bf16[1024,8]{0,1:T(8,128)(2,1)}, u32[]{:S(2)}) copy-start(bf16[1024,8]{0,1:T(8,128)(2,1)} %param.12) | copy-start | bytes 49156
  40.7 9.6 %copy-start.1 = (s32[1,384,1]{1,2,0:T(1,128)S(1)}, s32[1,384,1]{1,2,0:T(1,128)}, u32[]{:S(2)}) copy-start(s32[1,384,1]{1,2,0:T(1,128)} %param.10) | copy-start | bytes 4612
  43.6 14.8 %copy-start.2 = (f32[1024]{0:T(1024)S(1)}, f32[1024]{0:T(1024)}, u32[]{:S(2)}) copy-start(f32[1024]{0:T(1024)} %param.15) | copy-start | bytes 12292
  43.6 14.8 %collective-permute-start.13 = (bf16[64,1024]{1,0:T(8,128)(2,1)S(1)}, bf16[64,1024]{1,0:T(8,128)(2,1)S(1)}, u32[]{:S(2)}, u32[]{:S(2)}) collective-permute-start(bf16[64,1024]{1,0:T(8,128)(2,1)S(1)} %get-tuple-element.68), channel_id=1, source_target_pairs={{0,10},{1,11},{2,8},{3,9},{4,14},{5,15},{6,12},{7,13},{8,2},{9,3},... | collective-permute-start | bytes 393224 | tf_op jit(solution)/shard_map/ppermute | solution.py:20
  47.8 10.6 %collective-permute-start.15 = (bf16[64,1024]{1,0:T(8,128)(2,1)S(1)}, bf16[64,1024]{1,0:T(8,128)(2,1)S(1)}, u32[]{:S(2)}, u32[]{:S(2)}) collective-permute-start(bf16[64,1024]{1,0:T(8,128)(2,1)S(1)} %get-tuple-element.70), channel_id=1, source_target_pairs={{0,6},{1,7},{2,4},{3,5},{4,2},{5,3},{6,0},{7,1},{8,14},{9,15},{10,... | collective-permute-start | bytes 393224 | tf_op jit(solution)/shard_map/ppermute | solution.py:20
  47.8 10.6 %collective-permute-start.14 = (bf16[64,1024]{1,0:T(8,128)(2,1)S(1)}, bf16[64,1024]{1,0:T(8,128)(2,1)S(1)}, u32[]{:S(2)}, u32[]{:S(2)}) collective-permute-start(bf16[64,1024]{1,0:T(8,128)(2,1)S(1)} %get-tuple-element.69), channel_id=1, source_target_pairs={{0,14},{1,15},{2,12},{3,13},{4,10},{5,11},{6,8},{7,9},{8,6},{9,7},... | collective-permute-start | bytes 393224 | tf_op jit(solution)/shard_map/ppermute | solution.py:20

commit v5 on v4

--- a/solution.py
+++ b/solution.py
@@ -38,6 +38,31 @@
 
 def silu(value):
     return 0.5 * value * (1.0 + jnp.tanh(0.5 * value))
+
+
+def fold(values, rows):
+    half = values.shape[1] // 2
+    return jnp.concatenate([values[:rows, :half], values[:rows, half:]], axis=0)
+
+
+def unfold(values):
+    rows = values.shape[0] // 2
+    values = values.astype(jnp.float32)
+    return jnp.concatenate([values[:rows, :], values[rows:, :]], axis=1)
+
+
+def pad_rows(values, rows):
+    missing = rows - values.shape[0]
+    if not missing:
+        return values
+    return jnp.concatenate([values, jnp.zeros((missing, values.shape[1]), values.dtype)], axis=0)
+
+
+def read_part(part, width, pitch):
+    values = part[...]
+    if values.shape[1] == width:
+        return values
+    return pad_rows(unfold(values), pitch).astype(jnp.bfloat16)
 
 
 def normalise(values):
@@ -174,17 +199,24 @@
     slots = chips * pitch
     placing = (slot == lax.broadcasted_iota(jnp.int32, (slots, length), 0)).astype(jnp.bfloat16)
     span = slots // len(message_refs)
-    for start in range(0, width, 256):
-        columns = slice(start, start + 256)
-        placed = jnp.dot(placing, expert_in_ref[:, columns], preferred_element_type=jnp.float32)
-        placed = placed.astype(jnp.bfloat16)
+    folded = message_refs[0].shape[1] != width
+    part = width // 4
+    for start in range(0, width // 2 if folded else width, part):
+        placed = [
+            jnp.dot(placing, expert_in_ref[:, at : at + part], preferred_element_type=jnp.float32)
+            for at in ((start, width // 2 + start) if folded else (start,))
+        ]
         for number, message in enumerate(message_refs):
-            message[:, columns] = placed[number * span : (number + 1) * span, :]
+            rows = slice(number * span, (number + 1) * span)
+            value = placed[0][rows, :]
+            if folded:
+                value = fold(jnp.concatenate([value, placed[1][rows, :]], axis=1), cap)
+            message[:, start : start + part] = value.astype(jnp.bfloat16)
     for copy in weight_copies:
         copy.wait()
 
 
-def prepare(frames, count, me, ids, taps, w_in, w_out, chips, cap, pitch, messages):
+def prepare(frames, count, me, ids, taps, w_in, w_out, chips, cap, pitch, messages, folded):
     _, length, width = frames.shape
     groups = width // LANES
     reach = taps.shape[0] // 2
@@ -205,7 +237,7 @@
             jax.ShapeDtypeStruct((length, width), bf16),
             jax.ShapeDtypeStruct((chips, length), jnp.int32),
         ]
-        + [jax.ShapeDtypeStruct((span, width), bf16)] * messages,
+        + [jax.ShapeDtypeStruct((2 * cap, width // 2) if folded else (span, width), bf16)] * messages,
         scratch_shapes=[
             pltpu.VMEM((length, width), bf16),
             pltpu.VMEM(taps.shape, jnp.float32),
@@ -284,12 +316,12 @@
     )(count, expert_in, router.T, ids, slot)
 
 
-def expert_kernel(parts, tile, *refs):
+def expert_kernel(parts, span, tile, *refs):
     inputs, (in_a, in_b, out_a, out_b) = refs[:parts], refs[parts : parts + 4]
     outputs, (rows, total) = refs[parts + 4 : 2 * parts + 4], refs[2 * parts + 4 :]
-    span = inputs[0].shape[0]
+    width = rows.shape[1]
     for number, part in enumerate(inputs):
-        rows[number * span : (number + 1) * span, :] = part[...]
+        rows[number * span : (number + 1) * span, :] = read_part(part, width, span)
     values = rows[...]
     hidden = in_a.shape[1]
 
@@ -313,19 +345,22 @@
 
     lax.fori_loop(0, hidden // tile, step, 0)
     for number, part in enumerate(outputs):
-        part[...] = total[number * span : (number + 1) * span, :].astype(jnp.bfloat16)
-
-
-def run_expert(parts, weights):
-    span, width = parts[0].shape
+        value = total[number * span : (number + 1) * span, :]
+        if part.shape[1] != width:
+            value = fold(value, part.shape[0] // 2)
+        part[...] = value.astype(jnp.bfloat16)
+
+
+def run_expert(parts, weights, span):
+    width = weights[0].shape[0]
     whole = pl.BlockSpec(memory_space=pltpu.VMEM)
     count = len(parts)
     hidden = weights[0].shape[1]
     return pl.pallas_call(
-        functools.partial(expert_kernel, count, min(1024, hidden)),
+        functools.partial(expert_kernel, count, span, min(1024, hidden)),
         in_specs=[whole] * (count + 4),
         out_specs=[whole] * count,
-        out_shape=[jax.ShapeDtypeStruct((span, width), jnp.bfloat16)] * count,
+        out_shape=[jax.ShapeDtypeStruct(parts[0].shape, jnp.bfloat16)] * count,
         scratch_shapes=[
             pltpu.VMEM((span * count, width), jnp.bfloat16),
             pltpu.VMEM((span * count, width), jnp.float32),
@@ -336,21 +371,20 @@
     )(*parts, *weights)
 
 
-def add_kernel(parts, order, picking_ref, so_far_ref, gate_ref, *refs):
+def add_kernel(parts, order, span, picking_ref, so_far_ref, gate_ref, *refs):
     inputs, out_ref, results = refs[:parts], refs[parts], refs[parts + 1]
-    span = inputs[0].shape[0]
     places = []
     for number, (part, at) in enumerate(zip(inputs, order)):
-        results[number * span : (number + 1) * span, :] = part[...]
+        results[number * span : (number + 1) * span, :] = read_part(part, results.shape[1], span)
         places.append(picking_ref[:, at * span : (at + 1) * span])
     picking = jnp.concatenate(places, axis=1) if parts > 1 else places[0]
     picked = jnp.dot(picking, results[...], preferred_element_type=jnp.float32)
     out_ref[...] = so_far_ref[...].astype(jnp.float32) + gate_ref[...] * picked
 
 
-def close_kernel(parts, order, picking_ref, so_far_ref, gate_ref, gain_ref, *refs):
+def close_kernel(parts, order, span, picking_ref, so_far_ref, gate_ref, gain_ref, *refs):
     *refs, out_hbm, results, total, out_ref, sems = refs
-    add_kernel(parts, order, picking_ref, so_far_ref, gate_ref, *refs, total, results)
+    add_kernel(parts, order, span, picking_ref, so_far_ref, gate_ref, *refs, total, results)
     copies = []
     for number, start in enumerate(range(0, total.shape[0], BLOCK)):
         rows = slice(start, start + BLOCK)
@@ -365,11 +399,10 @@
         copy.wait()
 
 
-def add_results(so_far, gate, picking, parts, gain=None):
+def add_results(so_far, gate, picking, parts, span, gain=None):
     length, width = so_far.shape
     whole = pl.BlockSpec(memory_space=pltpu.VMEM)
     order, values = tuple(parts), [parts[at] for at in parts]
-    span = values[0].shape[0]
     scratch = [pltpu.VMEM((span * len(parts), width), jnp.bfloat16)]
     last = gain is not None
     if last:
@@ -377,7 +410,7 @@
         scratch.append(pltpu.VMEM((length, width), jnp.bfloat16))
         scratch.append(pltpu.SemaphoreType.DMA((length // BLOCK,)))
     return pl.pallas_call(
-        functools.partial(close_kernel if last else add_kernel, len(parts), order),
+        functools.partial(close_kernel if last else add_kernel, len(parts), order, span),
         in_specs=[whole] * (3 + last + len(parts)),
         out_specs=pl.BlockSpec(memory_space=pl.ANY) if last else whole,
         out_shape=jax.ShapeDtypeStruct((length, width), jnp.bfloat16 if last else jnp.float32),
@@ -401,8 +434,9 @@
 
     if chips <= 8:
         pitch = -(-cap // 16) * 16
+        folded = cap % 8 == 4
         own_in, own_out, stream, expert_in, slot, *messages = prepare(
-            frames, frame_counts, chip, ids, conv_kernel, w_in, w_out, chips, cap, pitch, chips
+            frames, frame_counts, chip, ids, conv_kernel, w_in, w_out, chips, cap, pitch, chips, folded
         )
         send = lambda part, d: xor_route(part, "expert", 2 * d)
         far = [d for d in range(1, chips) if d >= chips // 2]
@@ -415,32 +449,32 @@
             arrived[d] = send(part, d)
         for d, part in zip(near, [messages[d] for d in near]):
             arrived[d] = send(part, d)
-        first_out = run_expert([arrived[d] for d in first], weights)
+        first_out = run_expert([arrived[d] for d in first], weights, pitch)
         results = {}
         for d, part in zip(first, first_out):
             results[d] = send(part, d)
         gate, picking = gate_and_picking(frame_counts, expert_in, router, ids, slot, pitch)
-        close = run_expert([messages[0]] + after([arrived[d] for d in near], first_out), weights)
+        close = run_expert([messages[0]] + after([arrived[d] for d in near], first_out), weights, pitch)
         results[0] = close[0]
-        second_out = run_expert(after([arrived[d] for d in second], (first_out, close)), weights)
+        second_out = run_expert(after([arrived[d] for d in second], (first_out, close)), weights, pitch)
         for d, part in zip(second, second_out):
             results[d] = send(part, d)
         for d, part in zip(near[:2], close[1:3]):
             results[d] = send(part, d)
         for d, part in zip(near[2:], after(close[3:], second_out)):
             results[d] = send(part, d)
-        total = add_results(stream, gate, picking, {d: results[d] for d in [0] + first})
-        total = add_results(total, gate, picking, {d: results[d] for d in near[:2]})
-        output = add_results(total, gate, picking, {d: results[d] for d in second + near[2:]}, gain)
+        total = add_results(stream, gate, picking, {d: results[d] for d in [0] + first}, pitch)
+        total = add_results(total, gate, picking, {d: results[d] for d in near[:2]}, pitch)
+        output = add_results(total, gate, picking, {d: results[d] for d in second + near[2:]}, pitch, gain)
     else:
         home = jnp.zeros((1,), jnp.int32)
         own_in, own_out, stream, expert_in, slot, message = prepare(
-            frames, frame_counts, home, ids, conv_kernel, w_in, w_out, chips, cap, cap, 1
+            frames, frame_counts, home, ids, conv_kernel, w_in, w_out, chips, cap, cap, 1, False
         )
         gate, picking = gate_and_picking(frame_counts, expert_in, router, ids, slot, cap)
         other_in, other_out = load(other_in, other_out)
-        (result,) = run_expert([exchange(message, "expert", chips)], (own_in, other_in, own_out, other_out))
-        output = add_results(stream, gate, picking, {0: exchange(result, "expert", chips)}, gain)
+        (result,) = run_expert([exchange(message, "expert", chips)], (own_in, other_in, own_out, other_out), chips * cap)
+        output = add_results(stream, gate, picking, {0: exchange(result, "expert", chips)}, chips * cap, gain)
     return output.reshape(1, length, width)
 
 

time: 60.2 us -> 58.5 us (0.972)
  waiting for transfers between devices: 9.05 us -> 7.52 us
    ppermute x16, waiting for transfers between devices: 9.05 us -> 7.52 us  [xor_route(): return lax.ppermute(block, axis, [(i, i ^ distance) for i in range(count)])]
  transfers between devices with their start and end apart: 16 -> 16, of which waited for: 3 -> 3; matrix products, arithmetic and copies ran while one was open for 0% -> 0% of each run, Pallas kernels for 37% -> 39%
where the time goes in v5:
time: 58.5 us; the launch traced here: 58.3 us
  starting transfers between devices  25.9 us (44%)
  Pallas kernels  24.1 us (41%)
  waiting for transfers between devices  7.52 us (13%)
  between operations  0.79 us (1%)
    ppermute x16, starting transfers between devices, xor_route(): return lax.ppermute(block, axis, [(i, i ^ distance) for i in range(count)])  25.9 us
    pallas_call x3, Pallas kernels, run_expert(): pl.pallas_call(functools.partial(expert_kernel, count, span, min(1024, hi...  10.9 us
    ppermute x16, waiting for transfers between devices, xor_route(): return lax.ppermute(block, axis, [(i, i ^ distance) for i in range(count)])  7.52 us
    pallas_call x1, Pallas kernels, prepare(): pl.pallas_call(functools.partial(pre_kernel, cap, pitch), in_specs=[pl.Bl...  6.79 us
    pallas_call x1, Pallas kernels, load(): pl.pallas_call(functools.partial(load_kernel, count), in_specs=[pl.BlockS...  3.48 us
    pallas_call x3, Pallas kernels, add_results(): pl.pallas_call(functools.partial(close_kernel if last else add_kernel, le...  2.43 us
  transfers between devices with their start and end apart: 16, of which 3 were waited for; matrix products, arithmetic and copies ran while one was open for 0% of the time, Pallas kernels for 39%

profile of v5, /device:TPU:0, one launch (start us, length us, event | category | flops | bytes accessed | tf_op | source)
XLA Modules:
  0.0 58.3 jit_solution(11497987258446944325)
XLA Ops:
  0.0 0.5 collective-permute-start.5
  0.5 0.1 collective-permute-start.6
  1.2 6.8 %prepare.1 = (bf16[1024,2048]{1,0:T(8,128)(2,1)S(1)}, bf16[2048,1024]{1,0:T(8,128)(2,1)S(1)}, bf16[384,1024]{1,0:T(8,128)(2,1)S(1)}, bf16[384,1024]{1,0:T(8,128)...) custom-call(s32[1]{0:T(128)S(6)} %copy.9.count_ref, ...), custom_call_target="tpu_custom_call" | custom-call | flops 1 | bytes 1 | tf_op jit(solution)/shard_map/prepare/pallas_call | solution.py:229
  8.0 4.1 %collective-permute-start.3 = (bf16[120,512]{1,0:T(8,128)(2,1)S(1)}, bf16[120,512]{1,0:T(8,128)(2,1)S(1)}, u32[]{:S(2)}, u32[]{:S(2)}) collective-permute-start(bf16[120,512]{1,0:T(8,128)(2,1)S(1)} %get-tuple-element.47), channel_id=1, source_target_pairs={{0,8},{1,9},{2,10},{3,11},{4,12},{5,13},{6,14},{7,15},{8,0},{9,1},... | collective-permute-start | bytes 368648 | tf_op jit(solution)/shard_map/ppermute | solution.py:20
  12.1 1.3 %collective-permute-start.4 = (bf16[120,512]{1,0:T(8,128)(2,1)S(1)}, bf16[120,512]{1,0:T(8,128)(2,1)S(1)}, u32[]{:S(2)}, u32[]{:S(2)}) collective-permute-start(bf16[120,512]{1,0:T(8,128)(2,1)S(1)} %get-tuple-element.48), channel_id=1, source_target_pairs={{0,12},{1,13},{2,14},{3,15},{4,8},{5,9},{6,10},{7,11},{8,4},{9,5},... | collective-permute-start | bytes 368648 | tf_op jit(solution)/shard_map/ppermute | solution.py:20
  13.4 1.5 %collective-permute-start = (bf16[120,512]{1,0:T(8,128)(2,1)S(1)}, bf16[120,512]{1,0:T(8,128)(2,1)S(1)}, u32[]{:S(2)}, u32[]{:S(2)}) collective-permute-start(bf16[120,512]{1,0:T(8,128)(2,1)S(1)} %get-tuple-element.44), channel_id=1, source_target_pairs={{0,2},{1,3},{2,0},{3,1},{4,6},{5,7},{6,4},{7,5},{8,10},{9,11},{10,... | collective-permute-start | bytes 368648 | tf_op jit(solution)/shard_map/ppermute | solution.py:20
  14.9 0.0 collective-permute-done.5.refs_0_
  14.9 0.2 collective-permute-start.1
  15.2 0.0 collective-permute-done.6.refs_1_
  15.2 2.3 %collective-permute-start.2 = (bf16[120,512]{1,0:T(8,128)(2,1)S(1)}, bf16[120,512]{1,0:T(8,128)(2,1)S(1)}, u32[]{:S(2)}, u32[]{:S(2)}) collective-permute-start(bf16[120,512]{1,0:T(8,128)(2,1)S(1)} %get-tuple-element.46), channel_id=1, source_target_pairs={{0,6},{1,7},{2,4},{3,5},{4,2},{5,3},{6,0},{7,1},{8,14},{9,15},{10,... | collective-permute-start | bytes 368648 | tf_op jit(solution)/shard_map/ppermute | solution.py:20
  17.5 3.5 %load.1 = (bf16[1024,2048]{1,0:T(8,128)(2,1)S(1)}, bf16[2048,1024]{1,0:T(8,128)(2,1)S(1)}) custom-call(bf16[1024,2048]{1,0:T(8,128)(2,1)} %collective-permute-done.5.refs_0_, bf16[2048,1024]{1,0:T(8,128)(2,1)} %collective-permute-done.6.refs_1_), custom_call_target="tpu_custom_call" | custom-call | flops 1 | bytes 1 | tf_op jit(solution)/shard_map/load/pallas_call | solution.py:272
  21.0 0.5 collective-permute-done.3.refs_0_
  21.5 2.1 %collective-permute-start.11 = (bf16[120,512]{1,0:T(8,128)(2,1)S(1)}, bf16[120,512]{1,0:T(8,128)(2,1)S(1)}, u32[]{:S(2)}, u32[]{:S(2)}) collective-permute-start(bf16[120,512]{1,0:T(8,128)(2,1)S(1)} %get-tuple-element.63), channel_id=1, source_target_pairs={{0,10},{1,11},{2,8},{3,9},{4,14},{5,15},{6,12},{7,13},{8,2},{9,3},... | collective-permute-start | bytes 368648 | tf_op jit(solution)/shard_map/ppermute | solution.py:20
  23.6 0.0 collective-permute-done.4.refs_1_
  23.6 1.9 %collective-permute-start.12 = (bf16[120,512]{1,0:T(8,128)(2,1)S(1)}, bf16[120,512]{1,0:T(8,128)(2,1)S(1)}, u32[]{:S(2)}, u32[]{:S(2)}) collective-permute-start(bf16[120,512]{1,0:T(8,128)(2,1)S(1)} %get-tuple-element.64), channel_id=1, source_target_pairs={{0,14},{1,15},{2,12},{3,13},{4,10},{5,11},{6,8},{7,9},{8,6},{9,7},... | collective-permute-start | bytes 368648 | tf_op jit(solution)/shard_map/ppermute | solution.py:20
  25.5 2.9 %expert.3 = (bf16[120,512]{1,0:T(8,128)(2,1)S(1)}, bf16[120,512]{1,0:T(8,128)(2,1)S(1)}) custom-call(bf16[120,512]{1,0:T(8,128)(2,1)S(1)} %collective-permute-done.3.refs_0_, bf16[120,512]{1,0:T(8,128)(2,1)S(1)} %collective-permute-done.4.refs_1_, bf16[1024,2048]{1,0:T(8,128)(2,1)S(1)} %get-tuple-element.49.refs_2_.refs_4_, ...), custom_call_target="tpu_custom_call" | custom-call | flops 1 | bytes 1 | tf_op jit(solution)/shard_map/expert/pallas_call | solution.py:359
  28.3 0.0 collective-permute-done.refs_1_
  28.4 2.0 %collective-permute-start.7 = (bf16[120,512]{1,0:T(8,128)(2,1)S(1)}, bf16[120,512]{1,0:T(8,128)(2,1)S(1)}, u32[]{:S(2)}, u32[]{:S(2)}) collective-permute-start(bf16[120,512]{1,0:T(8,128)(2,1)S(1)} %get-tuple-element.53), channel_id=1, source_target_pairs={{0,8},{1,9},{2,10},{3,11},{4,12},{5,13},{6,14},{7,15},{8,0},{9,1},... | collective-permute-start | bytes 368648 | tf_op jit(solution)/shard_map/ppermute | solution.py:20
  30.4 0.0 collective-permute-done.1.refs_2_
  30.4 2.6 %collective-permute-start.8 = (bf16[120,512]{1,0:T(8,128)(2,1)S(1)}, bf16[120,512]{1,0:T(8,128)(2,1)S(1)}, u32[]{:S(2)}, u32[]{:S(2)}) collective-permute-start(bf16[120,512]{1,0:T(8,128)(2,1)S(1)} %get-tuple-element.54), channel_id=1, source_target_pairs={{0,12},{1,13},{2,14},{3,15},{4,8},{5,9},{6,10},{7,11},{8,4},{9,5},... | collective-permute-start | bytes 368648 | tf_op jit(solution)/shard_map/ppermute | solution.py:20
  33.0 0.0 collective-permute-done.2.refs_3_
  33.0 5.1 %expert.4 = (bf16[120,512]{1,0:T(8,128)(2,1)S(1)}, bf16[120,512]{1,0:T(8,128)(2,1)S(1)}, bf16[120,512]{1,0:T(8,128)(2,1)S(1)}, bf16[120,512]{1,0:T(8,128)(2,1)S(1)}) custom-call(bf16[120,512]{1,0:T(8,128)(2,1)S(1)} %get-tuple-element.43.refs_0_, bf16[120,512]{1,0:T(8,128)(2,1)S(1)} %collective-permute-done.refs_1_, ...), custom_call_target="tpu_custom_call" | custom-call | flops 1 | bytes 1 | tf_op jit(solution)/shard_map/expert/pallas_call | solution.py:359
  38.1 0.6 collective-permute-start.9
  38.7 0.9 %collective-permute-done.11.refs_0_ = bf16[120,512]{1,0:T(8,128)(2,1)S(1)} collective-permute-done((bf16[120,512]{1,0:T(8,128)(2,1)S(1)}, bf16[120,512]{1,0:T(8,128)(2,1)S(1)}, u32[]{:S(2)}, u32[]{:S(2)}) %collective-permute-start.11) | collective-permute-done | bytes 122912 | tf_op jit(solution)/shard_map/ppermute | solution.py:20
  39.6 0.0 collective-permute-start.10
  39.6 0.0 collective-permute-done.12.refs_1_
  39.6 0.0 copy-start
  39.6 0.0 copy-start.1
  39.6 2.9 %expert.5 = (bf16[120,512]{1,0:T(8,128)(2,1)S(1)}, bf16[120,512]{1,0:T(8,128)(2,1)S(1)}) custom-call(bf16[120,512]{1,0:T(8,128)(2,1)S(1)} %collective-permute-done.11.refs_0_, bf16[120,512]{1,0:T(8,128)(2,1)S(1)} %collective-permute-done.12.refs_1_, bf16[1024,2048]{1,0:T(8,128)(2,1)S(1)} %get-tuple-element.49.refs_2_.refs_4_, ...), custom_call_target="tpu_custom_call" | custom-call | flops 1 | bytes 1 | tf_op jit(solution)/shard_map/expert/pallas_call | solution.py:359
  42.5 0.0 copy-start.2
  42.5 4.2 %collective-permute-start.13 = (bf16[120,512]{1,0:T(8,128)(2,1)S(1)}, bf16[120,512]{1,0:T(8,128)(2,1)S(1)}, u32[]{:S(2)}, u32[]{:S(2)}) collective-permute-start(bf16[120,512]{1,0:T(8,128)(2,1)S(1)} %get-tuple-element.68), channel_id=1, source_target_pairs={{0,10},{1,11},{2,8},{3,9},{4,14},{5,15},{6,12},{7,13},{8,2},{9,3},... | collective-permute-start | bytes 368648 | tf_op jit(solution)/shard_map/ppermute | solution.py:20
  46.7 0.0 collective-permute-done.7.refs_1_
  46.7 0.0 collective-permute-start.15
  46.7 0.0 collective-permute-done.8.refs_2_
  46.7 2.5 %collective-permute-start.14 = (bf16[120,512]{1,0:T(8,128)(2,1)S(1)}, bf16[120,512]{1,0:T(8,128)(2,1)S(1)}, u32[]{:S(2)}, u32[]{:S(2)}) collective-permute-start(bf16[120,512]{1,0:T(8,128)(2,1)S(1)} %get-tuple-element.69), channel_id=1, source_target_pairs={{0,14},{1,15},{2,12},{3,13},{4,10},{5,11},{6,8},{7,9},{8,6},{9,7},... | collective-permute-start | bytes 368648 | tf_op jit(solution)/shard_map/ppermute | solution.py:20
  49.2 0.0 copy-done
  49.2 0.0 copy-done.1
  49.2 0.5 gate.1
  49.8 0.4 add.3.so_far_ref
  50.2 0.0 collective-permute-done.9.refs_0_
  50.2 0.0 collective-permute-done.10.refs_1_
  50.2 0.4 add.4.so_far_ref
  50.6 6.1 %collective-permute-done.15.refs_2_ = bf16[120,512]{1,0:T(8,128)(2,1)S(1)} collective-permute-done((bf16[120,512]{1,0:T(8,128)(2,1)S(1)}, bf16[120,512]{1,0:T(8,128)(2,1)S(1)}, u32[]{:S(2)}, u32[]{:S(2)}) %collective-permute-start.15) | collective-permute-done | bytes 122912 | tf_op jit(solution)/shard_map/ppermute | solution.py:20
  56.7 0.0 collective-permute-done.13.refs_0_
  56.7 0.0 collective-permute-done.14.refs_1_
  56.7 0.0 copy-done.2
  56.7 1.6 %finish.1 = bf16[384,1024]{1,0:T(8,128)(2,1)} custom-call(bf16[384,512]{1,0:T(8,128)(2,1)S(1)} %get-tuple-element.40.picking_ref, f32[384,1024]{1,0:T(8,128)S(1)} %add.4.so_far_ref, f32[384,1]{1,0:T(8,128)S(1)} %get-tuple-element.42.gate_ref, f32[1,1024]{1,0:T(1,128)S(1)} %bitcast.8, bf16[120,512]{1,0:T(8,128)(2,1)S(1)} %collective-permute-done.13.refs_0_, ...), custom_call_target="tpu_custom_call" | custom-call | flops 1 | bytes 1 | tf_op jit(solution)/shard_map/finish/pallas_call | solution.py:412
Async XLA Ops:
  0.0 14.9 %collective-permute-start.5 = (bf16[1024,2048]{1,0:T(8,128)(2,1)}, bf16[1024,2048]{1,0:T(8,128)(2,1)}, u32[]{:S(2)}, u32[]{:S(2)}) collective-permute-start(bf16[1024,2048]{1,0:T(8,128)(2,1)} %in_hbm.1), channel_id=1, source_target_pairs={{0,1},{1,0},{2,3},{3,2},{4,5},{5,4},{6,7},{7,6},{8,9},{9,8},{10,11... | collective-permute-start | bytes 12582920 | tf_op jit(solution)/shard_map/ppermute | solution.py:20
  0.5 14.7 %collective-permute-start.6 = (bf16[2048,1024]{1,0:T(8,128)(2,1)}, bf16[2048,1024]{1,0:T(8,128)(2,1)}, u32[]{:S(2)}, u32[]{:S(2)}) collective-permute-start(bf16[2048,1024]{1,0:T(8,128)(2,1)} %out_hbm.1), channel_id=1, source_target_pairs={{0,1},{1,0},{2,3},{3,2},{4,5},{5,4},{6,7},{7,6},{8,9},{9,8},{10,11... | collective-permute-start | bytes 12582920 | tf_op jit(solution)/shard_map/ppermute | solution.py:20
  8.0 13.5 %collective-permute-start.3 = (bf16[120,512]{1,0:T(8,128)(2,1)S(1)}, bf16[120,512]{1,0:T(8,128)(2,1)S(1)}, u32[]{:S(2)}, u32[]{:S(2)}) collective-permute-start(bf16[120,512]{1,0:T(8,128)(2,1)S(1)} %get-tuple-element.47), channel_id=1, source_target_pairs={{0,8},{1,9},{2,10},{3,11},{4,12},{5,13},{6,14},{7,15},{8,0},{9,1},... | collective-permute-start | bytes 368648 | tf_op jit(solution)/shard_map/ppermute | solution.py:20
  12.1 11.5 %collective-permute-start.4 = (bf16[120,512]{1,0:T(8,128)(2,1)S(1)}, bf16[120,512]{1,0:T(8,128)(2,1)S(1)}, u32[]{:S(2)}, u32[]{:S(2)}) collective-permute-start(bf16[120,512]{1,0:T(8,128)(2,1)S(1)} %get-tuple-element.48), channel_id=1, source_target_pairs={{0,12},{1,13},{2,14},{3,15},{4,8},{5,9},{6,10},{7,11},{8,4},{9,5},... | collective-permute-start | bytes 368648 | tf_op jit(solution)/shard_map/ppermute | solution.py:20
  13.4 14.9 %collective-permute-start = (bf16[120,512]{1,0:T(8,128)(2,1)S(1)}, bf16[120,512]{1,0:T(8,128)(2,1)S(1)}, u32[]{:S(2)}, u32[]{:S(2)}) collective-permute-start(bf16[120,512]{1,0:T(8,128)(2,1)S(1)} %get-tuple-element.44), channel_id=1, source_target_pairs={{0,2},{1,3},{2,0},{3,1},{4,6},{5,7},{6,4},{7,5},{8,10},{9,11},{10,... | collective-permute-start | bytes 368648 | tf_op jit(solution)/shard_map/ppermute | solution.py:20
  14.9 15.5 %collective-permute-start.1 = (bf16[120,512]{1,0:T(8,128)(2,1)S(1)}, bf16[120,512]{1,0:T(8,128)(2,1)S(1)}, u32[]{:S(2)}, u32[]{:S(2)}) collective-permute-start(bf16[120,512]{1,0:T(8,128)(2,1)S(1)} %get-tuple-element.45), channel_id=1, source_target_pairs={{0,4},{1,5},{2,6},{3,7},{4,0},{5,1},{6,2},{7,3},{8,12},{9,13},{10,... | collective-permute-start | bytes 368648 | tf_op jit(solution)/shard_map/ppermute | solution.py:20
  15.2 17.8 %collective-permute-start.2 = (bf16[120,512]{1,0:T(8,128)(2,1)S(1)}, bf16[120,512]{1,0:T(8,128)(2,1)S(1)}, u32[]{:S(2)}, u32[]{:S(2)}) collective-permute-start(bf16[120,512]{1,0:T(8,128)(2,1)S(1)} %get-tuple-element.46), channel_id=1, source_target_pairs={{0,6},{1,7},{2,4},{3,5},{4,2},{5,3},{6,0},{7,1},{8,14},{9,15},{10,... | collective-permute-start | bytes 368648 | tf_op jit(solution)/shard_map/ppermute | solution.py:20
  21.5 18.1 %collective-permute-start.11 = (bf16[120,512]{1,0:T(8,128)(2,1)S(1)}, bf16[120,512]{1,0:T(8,128)(2,1)S(1)}, u32[]{:S(2)}, u32[]{:S(2)}) collective-permute-start(bf16[120,512]{1,0:T(8,128)(2,1)S(1)} %get-tuple-element.63), channel_id=1, source_target_pairs={{0,10},{1,11},{2,8},{3,9},{4,14},{5,15},{6,12},{7,13},{8,2},{9,3},... | collective-permute-start | bytes 368648 | tf_op jit(solution)/shard_map/ppermute | solution.py:20
  23.6 16.0 %collective-permute-start.12 = (bf16[120,512]{1,0:T(8,128)(2,1)S(1)}, bf16[120,512]{1,0:T(8,128)(2,1)S(1)}, u32[]{:S(2)}, u32[]{:S(2)}) collective-permute-start(bf16[120,512]{1,0:T(8,128)(2,1)S(1)} %get-tuple-element.64), channel_id=1, source_target_pairs={{0,14},{1,15},{2,12},{3,13},{4,10},{5,11},{6,8},{7,9},{8,6},{9,7},... | collective-permute-start | bytes 368648 | tf_op jit(solution)/shard_map/ppermute | solution.py:20
  28.4 18.4 %collective-permute-start.7 = (bf16[120,512]{1,0:T(8,128)(2,1)S(1)}, bf16[120,512]{1,0:T(8,128)(2,1)S(1)}, u32[]{:S(2)}, u32[]{:S(2)}) collective-permute-start(bf16[120,512]{1,0:T(8,128)(2,1)S(1)} %get-tuple-element.53), channel_id=1, source_target_pairs={{0,8},{1,9},{2,10},{3,11},{4,12},{5,13},{6,14},{7,15},{8,0},{9,1},... | collective-permute-start | bytes 368648 | tf_op jit(solution)/shard_map/ppermute | solution.py:20
  30.4 16.4 %collective-permute-start.8 = (bf16[120,512]{1,0:T(8,128)(2,1)S(1)}, bf16[120,512]{1,0:T(8,128)(2,1)S(1)}, u32[]{:S(2)}, u32[]{:S(2)}) collective-permute-start(bf16[120,512]{1,0:T(8,128)(2,1)S(1)} %get-tuple-element.54), channel_id=1, source_target_pairs={{0,12},{1,13},{2,14},{3,15},{4,8},{5,9},{6,10},{7,11},{8,4},{9,5},... | collective-permute-start | bytes 368648 | tf_op jit(solution)/shard_map/ppermute | solution.py:20
  38.1 12.1 %collective-permute-start.9 = (bf16[120,512]{1,0:T(8,128)(2,1)S(1)}, bf16[120,512]{1,0:T(8,128)(2,1)S(1)}, u32[]{:S(2)}, u32[]{:S(2)}) collective-permute-start(bf16[120,512]{1,0:T(8,128)(2,1)S(1)} %get-tuple-element.59), channel_id=1, source_target_pairs={{0,2},{1,3},{2,0},{3,1},{4,6},{5,7},{6,4},{7,5},{8,10},{9,11},{10,... | collective-permute-start | bytes 368648 | tf_op jit(solution)/shard_map/ppermute | solution.py:20
  39.6 10.7 %collective-permute-start.10 = (bf16[120,512]{1,0:T(8,128)(2,1)S(1)}, bf16[120,512]{1,0:T(8,128)(2,1)S(1)}, u32[]{:S(2)}, u32[]{:S(2)}) collective-permute-start(bf16[120,512]{1,0:T(8,128)(2,1)S(1)} %get-tuple-element.60), channel_id=1, source_target_pairs={{0,4},{1,5},{2,6},{3,7},{4,0},{5,1},{6,2},{7,3},{8,12},{9,13},{10,... | collective-permute-start | bytes 368648 | tf_op jit(solution)/shard_map/ppermute | solution.py:20
  39.6 9.7 %copy-start = (bf16[1024,8]{0,1:T(8,128)(2,1)S(1)}, bf16[1024,8]{0,1:T(8,128)(2,1)}, u32[]{:S(2)}) copy-start(bf16[1024,8]{0,1:T(8,128)(2,1)} %param.12) | copy-start | bytes 49156
  39.6 9.7 %copy-start.1 = (s32[1,384,1]{1,2,0:T(1,128)S(1)}, s32[1,384,1]{1,2,0:T(1,128)}, u32[]{:S(2)}) copy-start(s32[1,384,1]{1,2,0:T(1,128)} %param.10) | copy-start | bytes 4612
  42.5 14.3 %copy-start.2 = (f32[1024]{0:T(1024)S(1)}, f32[1024]{0:T(1024)}, u32[]{:S(2)}) copy-start(f32[1024]{0:T(1024)} %param.15) | copy-start | bytes 12292
  42.5 14.2 %collective-permute-start.13 = (bf16[120,512]{1,0:T(8,128)(2,1)S(1)}, bf16[120,512]{1,0:T(8,128)(2,1)S(1)}, u32[]{:S(2)}, u32[]{:S(2)}) collective-permute-start(bf16[120,512]{1,0:T(8,128)(2,1)S(1)} %get-tuple-element.68), channel_id=1, source_target_pairs={{0,10},{1,11},{2,8},{3,9},{4,14},{5,15},{6,12},{7,13},{8,2},{9,3},... | collective-permute-start | bytes 368648 | tf_op jit(solution)/shard_map/ppermute | solution.py:20
  46.7 10.0 %collective-permute-start.15 = (bf16[120,512]{1,0:T(8,128)(2,1)S(1)}, bf16[120,512]{1,0:T(8,128)(2,1)S(1)}, u32[]{:S(2)}, u32[]{:S(2)}) collective-permute-start(bf16[120,512]{1,0:T(8,128)(2,1)S(1)} %get-tuple-element.70), channel_id=1, source_target_pairs={{0,6},{1,7},{2,4},{3,5},{4,2},{5,3},{6,0},{7,1},{8,14},{9,15},{10,... | collective-permute-start | bytes 368648 | tf_op jit(solution)/shard_map/ppermute | solution.py:20
  46.7 10.0 %collective-permute-start.14 = (bf16[120,512]{1,0:T(8,128)(2,1)S(1)}, bf16[120,512]{1,0:T(8,128)(2,1)S(1)}, u32[]{:S(2)}, u32[]{:S(2)}) collective-permute-start(bf16[120,512]{1,0:T(8,128)(2,1)S(1)} %get-tuple-element.69), channel_id=1, source_target_pairs={{0,14},{1,15},{2,12},{3,13},{4,10},{5,11},{6,8},{7,9},{8,6},{9,7},... | collective-permute-start | bytes 368648 | tf_op jit(solution)/shard_map/ppermute | solution.py:20

commit v6 on v5

--- a/solution.py
+++ b/solution.py
@@ -451,11 +451,11 @@
             arrived[d] = send(part, d)
         first_out = run_expert([arrived[d] for d in first], weights, pitch)
         results = {}
-        for d, part in zip(first, first_out):
-            results[d] = send(part, d)
         gate, picking = gate_and_picking(frame_counts, expert_in, router, ids, slot, pitch)
         close = run_expert([messages[0]] + after([arrived[d] for d in near], first_out), weights, pitch)
         results[0] = close[0]
+        for d, part in zip(first, after(first_out, close)):
+            results[d] = send(part, d)
         second_out = run_expert(after([arrived[d] for d in second], (first_out, close)), weights, pitch)
         for d, part in zip(second, second_out):
             results[d] = send(part, d)

time: 58.5 us -> 57.9 us (0.990)
  starting transfers between devices: 25.9 us -> 24.6 us
  waiting for transfers between devices: 7.52 us -> 8.21 us
    ppermute x16, starting transfers between devices: 25.9 us -> 24.6 us  [xor_route(): return lax.ppermute(block, axis, [(i, i ^ distance) for i in range(count)])]
    ppermute x16, waiting for transfers between devices: 7.52 us -> 8.21 us  [xor_route(): return lax.ppermute(block, axis, [(i, i ^ distance) for i in range(count)])]
  transfers between devices with their start and end apart: 16 -> 16, of which waited for: 3 -> 4; matrix products, arithmetic and copies ran while one was open for 0% -> 0% of each run, Pallas kernels for 39% -> 39%
where the time goes in v6:
time: 57.9 us; the launch traced here: 57.8 us
  starting transfers between devices  24.6 us (42%)
  Pallas kernels  24.1 us (42%)
  waiting for transfers between devices  8.21 us (14%)
  between operations  0.8 us (1%)
    ppermute x16, starting transfers between devices, xor_route(): return lax.ppermute(block, axis, [(i, i ^ distance) for i in range(count)])  24.6 us
    pallas_call x3, Pallas kernels, run_expert(): pl.pallas_call(functools.partial(expert_kernel, count, span, min(1024, hi...  10.9 us
    ppermute x16, waiting for transfers between devices, xor_route(): return lax.ppermute(block, axis, [(i, i ^ distance) for i in range(count)])  8.21 us
    pallas_call x1, Pallas kernels, prepare(): pl.pallas_call(functools.partial(pre_kernel, cap, pitch), in_specs=[pl.Bl...  6.79 us
    pallas_call x1, Pallas kernels, load(): pl.pallas_call(functools.partial(load_kernel, count), in_specs=[pl.BlockS...  3.48 us
    pallas_call x3, Pallas kernels, add_results(): pl.pallas_call(functools.partial(close_kernel if last else add_kernel, le...  2.43 us
  transfers between devices with their start and end apart: 16, of which 4 were waited for; matrix products, arithmetic and copies ran while one was open for 0% of the time, Pallas kernels for 39%

profile of v6, /device:TPU:0, one launch (start us, length us, event | category | flops | bytes accessed | tf_op | source)
XLA Modules:
  0.0 57.8 jit_solution(902440173491380211)
XLA Ops:
  0.0 0.5 collective-permute-start.5
  0.5 0.1 collective-permute-start.6
  1.2 6.8 %prepare.1 = (bf16[1024,2048]{1,0:T(8,128)(2,1)S(1)}, bf16[2048,1024]{1,0:T(8,128)(2,1)S(1)}, bf16[384,1024]{1,0:T(8,128)(2,1)S(1)}, bf16[384,1024]{1,0:T(8,128)...) custom-call(s32[1]{0:T(128)S(6)} %copy.9.count_ref, ...), custom_call_target="tpu_custom_call" | custom-call | flops 1 | bytes 1 | tf_op jit(solution)/shard_map/prepare/pallas_call | solution.py:229
  8.0 4.1 %collective-permute-start.3 = (bf16[120,512]{1,0:T(8,128)(2,1)S(1)}, bf16[120,512]{1,0:T(8,128)(2,1)S(1)}, u32[]{:S(2)}, u32[]{:S(2)}) collective-permute-start(bf16[120,512]{1,0:T(8,128)(2,1)S(1)} %get-tuple-element.49), channel_id=1, source_target_pairs={{0,8},{1,9},{2,10},{3,11},{4,12},{5,13},{6,14},{7,15},{8,0},{9,1},... | collective-permute-start | bytes 368648 | tf_op jit(solution)/shard_map/ppermute | solution.py:20
  12.1 1.3 %collective-permute-start.4 = (bf16[120,512]{1,0:T(8,128)(2,1)S(1)}, bf16[120,512]{1,0:T(8,128)(2,1)S(1)}, u32[]{:S(2)}, u32[]{:S(2)}) collective-permute-start(bf16[120,512]{1,0:T(8,128)(2,1)S(1)} %get-tuple-element.50), channel_id=1, source_target_pairs={{0,12},{1,13},{2,14},{3,15},{4,8},{5,9},{6,10},{7,11},{8,4},{9,5},... | collective-permute-start | bytes 368648 | tf_op jit(solution)/shard_map/ppermute | solution.py:20
  13.4 1.5 %collective-permute-start = (bf16[120,512]{1,0:T(8,128)(2,1)S(1)}, bf16[120,512]{1,0:T(8,128)(2,1)S(1)}, u32[]{:S(2)}, u32[]{:S(2)}) collective-permute-start(bf16[120,512]{1,0:T(8,128)(2,1)S(1)} %get-tuple-element.46), channel_id=1, source_target_pairs={{0,2},{1,3},{2,0},{3,1},{4,6},{5,7},{6,4},{7,5},{8,10},{9,11},{10,... | collective-permute-start | bytes 368648 | tf_op jit(solution)/shard_map/ppermute | solution.py:20
  14.9 0.0 collective-permute-done.5.refs_0_
  14.9 0.2 collective-permute-start.1
  15.2 0.0 collective-permute-done.6.refs_1_
  15.2 2.3 %collective-permute-start.2 = (bf16[120,512]{1,0:T(8,128)(2,1)S(1)}, bf16[120,512]{1,0:T(8,128)(2,1)S(1)}, u32[]{:S(2)}, u32[]{:S(2)}) collective-permute-start(bf16[120,512]{1,0:T(8,128)(2,1)S(1)} %get-tuple-element.48), channel_id=1, source_target_pairs={{0,6},{1,7},{2,4},{3,5},{4,2},{5,3},{6,0},{7,1},{8,14},{9,15},{10,... | collective-permute-start | bytes 368648 | tf_op jit(solution)/shard_map/ppermute | solution.py:20
  17.5 3.5 %load.1 = (bf16[1024,2048]{1,0:T(8,128)(2,1)S(1)}, bf16[2048,1024]{1,0:T(8,128)(2,1)S(1)}) custom-call(bf16[1024,2048]{1,0:T(8,128)(2,1)} %collective-permute-done.5.refs_0_, bf16[2048,1024]{1,0:T(8,128)(2,1)} %collective-permute-done.6.refs_1_), custom_call_target="tpu_custom_call" | custom-call | flops 1 | bytes 1 | tf_op jit(solution)/shard_map/load/pallas_call | solution.py:272
  21.0 0.5 collective-permute-done.3.refs_0_
  21.5 2.1 %collective-permute-start.11 = (bf16[120,512]{1,0:T(8,128)(2,1)S(1)}, bf16[120,512]{1,0:T(8,128)(2,1)S(1)}, u32[]{:S(2)}, u32[]{:S(2)}) collective-permute-start(bf16[120,512]{1,0:T(8,128)(2,1)S(1)} %get-tuple-element.68), channel_id=1, source_target_pairs={{0,10},{1,11},{2,8},{3,9},{4,14},{5,15},{6,12},{7,13},{8,2},{9,3},... | collective-permute-start | bytes 368648 | tf_op jit(solution)/shard_map/ppermute | solution.py:20
  23.6 0.0 collective-permute-done.4.refs_1_
  23.6 1.9 %collective-permute-start.12 = (bf16[120,512]{1,0:T(8,128)(2,1)S(1)}, bf16[120,512]{1,0:T(8,128)(2,1)S(1)}, u32[]{:S(2)}, u32[]{:S(2)}) collective-permute-start(bf16[120,512]{1,0:T(8,128)(2,1)S(1)} %get-tuple-element.69), channel_id=1, source_target_pairs={{0,14},{1,15},{2,12},{3,13},{4,10},{5,11},{6,8},{7,9},{8,6},{9,7},... | collective-permute-start | bytes 368648 | tf_op jit(solution)/shard_map/ppermute | solution.py:20
  25.5 2.9 %expert.3 = (bf16[120,512]{1,0:T(8,128)(2,1)S(1)}, bf16[120,512]{1,0:T(8,128)(2,1)S(1)}) custom-call(bf16[120,512]{1,0:T(8,128)(2,1)S(1)} %collective-permute-done.3.refs_0_, bf16[120,512]{1,0:T(8,128)(2,1)S(1)} %collective-permute-done.4.refs_1_, bf16[1024,2048]{1,0:T(8,128)(2,1)S(1)} %get-tuple-element.51.refs_2_.refs_4_, ...), custom_call_target="tpu_custom_call" | custom-call | flops 1 | bytes 1 | tf_op jit(solution)/shard_map/expert/pallas_call | solution.py:359
  28.3 0.0 collective-permute-done.refs_1_
  28.4 0.0 collective-permute-done.1.refs_2_
  28.4 0.0 collective-permute-done.2.refs_3_
  28.4 5.1 %expert.4 = (bf16[120,512]{1,0:T(8,128)(2,1)S(1)}, bf16[120,512]{1,0:T(8,128)(2,1)S(1)}, bf16[120,512]{1,0:T(8,128)(2,1)S(1)}, bf16[120,512]{1,0:T(8,128)(2,1)S(1)}) custom-call(bf16[120,512]{1,0:T(8,128)(2,1)S(1)} %get-tuple-element.45.refs_0_, bf16[120,512]{1,0:T(8,128)(2,1)S(1)} %collective-permute-done.refs_1_, ...), custom_call_target="tpu_custom_call" | custom-call | flops 1 | bytes 1 | tf_op jit(solution)/shard_map/expert/pallas_call | solution.py:359
  33.5 0.0 copy-start
  33.5 0.0 copy-start.1
  33.5 2.0 %collective-permute-start.7 = (bf16[120,512]{1,0:T(8,128)(2,1)S(1)}, bf16[120,512]{1,0:T(8,128)(2,1)S(1)}, u32[]{:S(2)}, u32[]{:S(2)}) collective-permute-start(bf16[120,512]{1,0:T(8,128)(2,1)S(1)} %get-tuple-element.64), channel_id=1, source_target_pairs={{0,8},{1,9},{2,10},{3,11},{4,12},{5,13},{6,14},{7,15},{8,0},{9,1},... | collective-permute-start | bytes 368648 | tf_op jit(solution)/shard_map/ppermute | solution.py:20
  35.6 2.6 %collective-permute-start.8 = (bf16[120,512]{1,0:T(8,128)(2,1)S(1)}, bf16[120,512]{1,0:T(8,128)(2,1)S(1)}, u32[]{:S(2)}, u32[]{:S(2)}) collective-permute-start(bf16[120,512]{1,0:T(8,128)(2,1)S(1)} %get-tuple-element.65), channel_id=1, source_target_pairs={{0,12},{1,13},{2,14},{3,15},{4,8},{5,9},{6,10},{7,11},{8,4},{9,5},... | collective-permute-start | bytes 368648 | tf_op jit(solution)/shard_map/ppermute | solution.py:20
  38.2 0.5 collective-permute-start.9
  38.7 0.0 collective-permute-done.11.refs_0_
  38.7 0.0 collective-permute-start.10
  38.7 0.0 collective-permute-done.12.refs_1_
  38.7 2.9 %expert.5 = (bf16[120,512]{1,0:T(8,128)(2,1)S(1)}, bf16[120,512]{1,0:T(8,128)(2,1)S(1)}) custom-call(bf16[120,512]{1,0:T(8,128)(2,1)S(1)} %collective-permute-done.11.refs_0_, bf16[120,512]{1,0:T(8,128)(2,1)S(1)} %collective-permute-done.12.refs_1_, bf16[1024,2048]{1,0:T(8,128)(2,1)S(1)} %get-tuple-element.51.refs_2_.refs_4_, ...), custom_call_target="tpu_custom_call" | custom-call | flops 1 | bytes 1 | tf_op jit(solution)/shard_map/expert/pallas_call | solution.py:359
  41.6 0.0 copy-start.2
  41.6 2.8 %collective-permute-start.13 = (bf16[120,512]{1,0:T(8,128)(2,1)S(1)}, bf16[120,512]{1,0:T(8,128)(2,1)S(1)}, u32[]{:S(2)}, u32[]{:S(2)}) collective-permute-start(bf16[120,512]{1,0:T(8,128)(2,1)S(1)} %get-tuple-element.72), channel_id=1, source_target_pairs={{0,10},{1,11},{2,8},{3,9},{4,14},{5,15},{6,12},{7,13},{8,2},{9,3},... | collective-permute-start | bytes 368648 | tf_op jit(solution)/shard_map/ppermute | solution.py:20
  44.4 1.5 %collective-permute-done.7.refs_1_ = bf16[120,512]{1,0:T(8,128)(2,1)S(1)} collective-permute-done((bf16[120,512]{1,0:T(8,128)(2,1)S(1)}, bf16[120,512]{1,0:T(8,128)(2,1)S(1)}, u32[]{:S(2)}, u32[]{:S(2)}) %collective-permute-start.7) | collective-permute-done | bytes 122912 | tf_op jit(solution)/shard_map/ppermute | solution.py:20
  45.9 0.0 collective-permute-start.15
  45.9 0.0 collective-permute-done.8.refs_2_
  45.9 2.7 %collective-permute-start.14 = (bf16[120,512]{1,0:T(8,128)(2,1)S(1)}, bf16[120,512]{1,0:T(8,128)(2,1)S(1)}, u32[]{:S(2)}, u32[]{:S(2)}) collective-permute-start(bf16[120,512]{1,0:T(8,128)(2,1)S(1)} %get-tuple-element.73), channel_id=1, source_target_pairs={{0,14},{1,15},{2,12},{3,13},{4,10},{5,11},{6,8},{7,9},{8,6},{9,7},... | collective-permute-start | bytes 368648 | tf_op jit(solution)/shard_map/ppermute | solution.py:20
  48.6 0.0 copy-done
  48.6 0.0 copy-done.1
  48.7 0.5 gate.1
  49.2 0.4 add.3.so_far_ref
  49.6 0.0 collective-permute-done.9.refs_0_
  49.6 0.0 collective-permute-done.10.refs_1_
  49.6 0.4 add.4.so_far_ref
  50.0 5.0 %collective-permute-done.15.refs_2_ = bf16[120,512]{1,0:T(8,128)(2,1)S(1)} collective-permute-done((bf16[120,512]{1,0:T(8,128)(2,1)S(1)}, bf16[120,512]{1,0:T(8,128)(2,1)S(1)}, u32[]{:S(2)}, u32[]{:S(2)}) %collective-permute-start.15) | collective-permute-done | bytes 122912 | tf_op jit(solution)/shard_map/ppermute | solution.py:20
  55.0 1.2 %collective-permute-done.13.refs_0_ = bf16[120,512]{1,0:T(8,128)(2,1)S(1)} collective-permute-done((bf16[120,512]{1,0:T(8,128)(2,1)S(1)}, bf16[120,512]{1,0:T(8,128)(2,1)S(1)}, u32[]{:S(2)}, u32[]{:S(2)}) %collective-permute-start.13) | collective-permute-done | bytes 122912 | tf_op jit(solution)/shard_map/ppermute | solution.py:20
  56.2 0.0 collective-permute-done.14.refs_1_
  56.2 0.0 copy-done.2
  56.2 1.6 %finish.1 = bf16[384,1024]{1,0:T(8,128)(2,1)} custom-call(bf16[384,512]{1,0:T(8,128)(2,1)S(1)} %get-tuple-element.42.picking_ref, f32[384,1024]{1,0:T(8,128)S(1)} %add.4.so_far_ref, f32[384,1]{1,0:T(8,128)S(1)} %get-tuple-element.44.gate_ref, f32[1,1024]{1,0:T(1,128)S(1)} %bitcast.8, bf16[120,512]{1,0:T(8,128)(2,1)S(1)} %collective-permute-done.13.refs_0_, ...), custom_call_target="tpu_custom_call" | custom-call | flops 1 | bytes 1 | tf_op jit(solution)/shard_map/finish/pallas_call | solution.py:412
Async XLA Ops:
  0.0 14.9 %collective-permute-start.5 = (bf16[1024,2048]{1,0:T(8,128)(2,1)}, bf16[1024,2048]{1,0:T(8,128)(2,1)}, u32[]{:S(2)}, u32[]{:S(2)}) collective-permute-start(bf16[1024,2048]{1,0:T(8,128)(2,1)} %in_hbm.1), channel_id=1, source_target_pairs={{0,1},{1,0},{2,3},{3,2},{4,5},{5,4},{6,7},{7,6},{8,9},{9,8},{10,11... | collective-permute-start | bytes 12582920 | tf_op jit(solution)/shard_map/ppermute | solution.py:20
  0.5 14.7 %collective-permute-start.6 = (bf16[2048,1024]{1,0:T(8,128)(2,1)}, bf16[2048,1024]{1,0:T(8,128)(2,1)}, u32[]{:S(2)}, u32[]{:S(2)}) collective-permute-start(bf16[2048,1024]{1,0:T(8,128)(2,1)} %out_hbm.1), channel_id=1, source_target_pairs={{0,1},{1,0},{2,3},{3,2},{4,5},{5,4},{6,7},{7,6},{8,9},{9,8},{10,11... | collective-permute-start | bytes 12582920 | tf_op jit(solution)/shard_map/ppermute | solution.py:20
  8.0 13.5 %collective-permute-start.3 = (bf16[120,512]{1,0:T(8,128)(2,1)S(1)}, bf16[120,512]{1,0:T(8,128)(2,1)S(1)}, u32[]{:S(2)}, u32[]{:S(2)}) collective-permute-start(bf16[120,512]{1,0:T(8,128)(2,1)S(1)} %get-tuple-element.49), channel_id=1, source_target_pairs={{0,8},{1,9},{2,10},{3,11},{4,12},{5,13},{6,14},{7,15},{8,0},{9,1},... | collective-permute-start | bytes 368648 | tf_op jit(solution)/shard_map/ppermute | solution.py:20
  12.1 11.5 %collective-permute-start.4 = (bf16[120,512]{1,0:T(8,128)(2,1)S(1)}, bf16[120,512]{1,0:T(8,128)(2,1)S(1)}, u32[]{:S(2)}, u32[]{:S(2)}) collective-permute-start(bf16[120,512]{1,0:T(8,128)(2,1)S(1)} %get-tuple-element.50), channel_id=1, source_target_pairs={{0,12},{1,13},{2,14},{3,15},{4,8},{5,9},{6,10},{7,11},{8,4},{9,5},... | collective-permute-start | bytes 368648 | tf_op jit(solution)/shard_map/ppermute | solution.py:20
  13.4 14.9 %collective-permute-start = (bf16[120,512]{1,0:T(8,128)(2,1)S(1)}, bf16[120,512]{1,0:T(8,128)(2,1)S(1)}, u32[]{:S(2)}, u32[]{:S(2)}) collective-permute-start(bf16[120,512]{1,0:T(8,128)(2,1)S(1)} %get-tuple-element.46), channel_id=1, source_target_pairs={{0,2},{1,3},{2,0},{3,1},{4,6},{5,7},{6,4},{7,5},{8,10},{9,11},{10,... | collective-permute-start | bytes 368648 | tf_op jit(solution)/shard_map/ppermute | solution.py:20
  14.9 13.4 %collective-permute-start.1 = (bf16[120,512]{1,0:T(8,128)(2,1)S(1)}, bf16[120,512]{1,0:T(8,128)(2,1)S(1)}, u32[]{:S(2)}, u32[]{:S(2)}) collective-permute-start(bf16[120,512]{1,0:T(8,128)(2,1)S(1)} %get-tuple-element.47), channel_id=1, source_target_pairs={{0,4},{1,5},{2,6},{3,7},{4,0},{5,1},{6,2},{7,3},{8,12},{9,13},{10,... | collective-permute-start | bytes 368648 | tf_op jit(solution)/shard_map/ppermute | solution.py:20
  15.2 13.2 %collective-permute-start.2 = (bf16[120,512]{1,0:T(8,128)(2,1)S(1)}, bf16[120,512]{1,0:T(8,128)(2,1)S(1)}, u32[]{:S(2)}, u32[]{:S(2)}) collective-permute-start(bf16[120,512]{1,0:T(8,128)(2,1)S(1)} %get-tuple-element.48), channel_id=1, source_target_pairs={{0,6},{1,7},{2,4},{3,5},{4,2},{5,3},{6,0},{7,1},{8,14},{9,15},{10,... | collective-permute-start | bytes 368648 | tf_op jit(solution)/shard_map/ppermute | solution.py:20
  21.5 17.2 %collective-permute-start.11 = (bf16[120,512]{1,0:T(8,128)(2,1)S(1)}, bf16[120,512]{1,0:T(8,128)(2,1)S(1)}, u32[]{:S(2)}, u32[]{:S(2)}) collective-permute-start(bf16[120,512]{1,0:T(8,128)(2,1)S(1)} %get-tuple-element.68), channel_id=1, source_target_pairs={{0,10},{1,11},{2,8},{3,9},{4,14},{5,15},{6,12},{7,13},{8,2},{9,3},... | collective-permute-start | bytes 368648 | tf_op jit(solution)/shard_map/ppermute | solution.py:20
  23.6 15.1 %collective-permute-start.12 = (bf16[120,512]{1,0:T(8,128)(2,1)S(1)}, bf16[120,512]{1,0:T(8,128)(2,1)S(1)}, u32[]{:S(2)}, u32[]{:S(2)}) collective-permute-start(bf16[120,512]{1,0:T(8,128)(2,1)S(1)} %get-tuple-element.69), channel_id=1, source_target_pairs={{0,14},{1,15},{2,12},{3,13},{4,10},{5,11},{6,8},{7,9},{8,6},{9,7},... | collective-permute-start | bytes 368648 | tf_op jit(solution)/shard_map/ppermute | solution.py:20
  33.5 15.1 %copy-start = (bf16[1024,8]{0,1:T(8,128)(2,1)S(1)}, bf16[1024,8]{0,1:T(8,128)(2,1)}, u32[]{:S(2)}) copy-start(bf16[1024,8]{0,1:T(8,128)(2,1)} %param.12) | copy-start | bytes 49156
  33.5 15.1 %copy-start.1 = (s32[1,384,1]{1,2,0:T(1,128)S(1)}, s32[1,384,1]{1,2,0:T(1,128)}, u32[]{:S(2)}) copy-start(s32[1,384,1]{1,2,0:T(1,128)} %param.10) | copy-start | bytes 4612
  33.5 12.4 %collective-permute-start.7 = (bf16[120,512]{1,0:T(8,128)(2,1)S(1)}, bf16[120,512]{1,0:T(8,128)(2,1)S(1)}, u32[]{:S(2)}, u32[]{:S(2)}) collective-permute-start(bf16[120,512]{1,0:T(8,128)(2,1)S(1)} %get-tuple-element.64), channel_id=1, source_target_pairs={{0,8},{1,9},{2,10},{3,11},{4,12},{5,13},{6,14},{7,15},{8,0},{9,1},... | collective-permute-start | bytes 368648 | tf_op jit(solution)/shard_map/ppermute | solution.py:20
  35.6 10.4 %collective-permute-start.8 = (bf16[120,512]{1,0:T(8,128)(2,1)S(1)}, bf16[120,512]{1,0:T(8,128)(2,1)S(1)}, u32[]{:S(2)}, u32[]{:S(2)}) collective-permute-start(bf16[120,512]{1,0:T(8,128)(2,1)S(1)} %get-tuple-element.65), channel_id=1, source_target_pairs={{0,12},{1,13},{2,14},{3,15},{4,8},{5,9},{6,10},{7,11},{8,4},{9,5},... | collective-permute-start | bytes 368648 | tf_op jit(solution)/shard_map/ppermute | solution.py:20
  38.2 11.4 %collective-permute-start.9 = (bf16[120,512]{1,0:T(8,128)(2,1)S(1)}, bf16[120,512]{1,0:T(8,128)(2,1)S(1)}, u32[]{:S(2)}, u32[]{:S(2)}) collective-permute-start(bf16[120,512]{1,0:T(8,128)(2,1)S(1)} %get-tuple-element.61), channel_id=1, source_target_pairs={{0,2},{1,3},{2,0},{3,1},{4,6},{5,7},{6,4},{7,5},{8,10},{9,11},{10,... | collective-permute-start | bytes 368648 | tf_op jit(solution)/shard_map/ppermute | solution.py:20
  38.7 10.9 %collective-permute-start.10 = (bf16[120,512]{1,0:T(8,128)(2,1)S(1)}, bf16[120,512]{1,0:T(8,128)(2,1)S(1)}, u32[]{:S(2)}, u32[]{:S(2)}) collective-permute-start(bf16[120,512]{1,0:T(8,128)(2,1)S(1)} %get-tuple-element.62), channel_id=1, source_target_pairs={{0,4},{1,5},{2,6},{3,7},{4,0},{5,1},{6,2},{7,3},{8,12},{9,13},{10,... | collective-permute-start | bytes 368648 | tf_op jit(solution)/shard_map/ppermute | solution.py:20
  41.6 14.6 %copy-start.2 = (f32[1024]{0:T(1024)S(1)}, f32[1024]{0:T(1024)}, u32[]{:S(2)}) copy-start(f32[1024]{0:T(1024)} %param.15) | copy-start | bytes 12292
  41.6 14.6 %collective-permute-start.13 = (bf16[120,512]{1,0:T(8,128)(2,1)S(1)}, bf16[120,512]{1,0:T(8,128)(2,1)S(1)}, u32[]{:S(2)}, u32[]{:S(2)}) collective-permute-start(bf16[120,512]{1,0:T(8,128)(2,1)S(1)} %get-tuple-element.72), channel_id=1, source_target_pairs={{0,10},{1,11},{2,8},{3,9},{4,14},{5,15},{6,12},{7,13},{8,2},{9,3},... | collective-permute-start | bytes 368648 | tf_op jit(solution)/shard_map/ppermute | solution.py:20
  45.9 9.1 %collective-permute-start.15 = (bf16[120,512]{1,0:T(8,128)(2,1)S(1)}, bf16[120,512]{1,0:T(8,128)(2,1)S(1)}, u32[]{:S(2)}, u32[]{:S(2)}) collective-permute-start(bf16[120,512]{1,0:T(8,128)(2,1)S(1)} %get-tuple-element.74), channel_id=1, source_target_pairs={{0,6},{1,7},{2,4},{3,5},{4,2},{5,3},{6,0},{7,1},{8,14},{9,15},{10,... | collective-permute-start | bytes 368648 | tf_op jit(solution)/shard_map/ppermute | solution.py:20
  45.9 10.2 %collective-permute-start.14 = (bf16[120,512]{1,0:T(8,128)(2,1)S(1)}, bf16[120,512]{1,0:T(8,128)(2,1)S(1)}, u32[]{:S(2)}, u32[]{:S(2)}) collective-permute-start(bf16[120,512]{1,0:T(8,128)(2,1)S(1)} %get-tuple-element.73), channel_id=1, source_target_pairs={{0,14},{1,15},{2,12},{3,13},{4,10},{5,11},{6,8},{7,9},{8,6},{9,7},... | collective-permute-start | bytes 368648 | tf_op jit(solution)/shard_map/ppermute | solution.py:20

commit v7 on v6

--- a/solution.py
+++ b/solution.py
@@ -357,7 +357,7 @@
     count = len(parts)
     hidden = weights[0].shape[1]
     return pl.pallas_call(
-        functools.partial(expert_kernel, count, span, min(1024, hidden)),
+        functools.partial(expert_kernel, count, span, min(2048, hidden)),
         in_specs=[whole] * (count + 4),
         out_specs=[whole] * count,
         out_shape=[jax.ShapeDtypeStruct(parts[0].shape, jnp.bfloat16)] * count,

time: 57.9 us -> 57.3 us (0.990)
  Pallas kernels: 24.1 us -> 22.8 us
    pallas_call x3, Pallas kernels: 10.9 us -> 9.6 us  [run_expert(): pl.pallas_call(functools.partial(expert_kernel, count, span, min(2048, hi...]
  transfers between devices with their start and end apart: 16 -> 16, of which waited for: 4 -> 3; matrix products, arithmetic and copies ran while one was open for 0% -> 0% of each run, Pallas kernels for 39% -> 37%
where the time goes in v7:
time: 57.3 us; the launch traced here: 56.8 us
  starting transfers between devices  25.1 us (44%)
  Pallas kernels  22.8 us (40%)
  waiting for transfers between devices  8.05 us (14%)
  between operations  0.81 us (1%)
    ppermute x16, starting transfers between devices, xor_route(): return lax.ppermute(block, axis, [(i, i ^ distance) for i in range(count)])  25.1 us
    pallas_call x3, Pallas kernels, run_expert(): pl.pallas_call(functools.partial(expert_kernel, count, span, min(2048, hi...  9.6 us
    ppermute x16, waiting for transfers between devices, xor_route(): return lax.ppermute(block, axis, [(i, i ^ distance) for i in range(count)])  8.05 us
    pallas_call x1, Pallas kernels, prepare(): pl.pallas_call(functools.partial(pre_kernel, cap, pitch), in_specs=[pl.Bl...  6.79 us
    pallas_call x1, Pallas kernels, load(): pl.pallas_call(functools.partial(load_kernel, count), in_specs=[pl.BlockS...  3.48 us
    pallas_call x3, Pallas kernels, add_results(): pl.pallas_call(functools.partial(close_kernel if last else add_kernel, le...  2.43 us
  transfers between devices with their start and end apart: 16, of which 3 were waited for; matrix products, arithmetic and copies ran while one was open for 0% of the time, Pallas kernels for 37%

profile of v7, /device:TPU:0, one launch (start us, length us, event | category | flops | bytes accessed | tf_op | source)
XLA Modules:
  0.0 56.8 jit_solution(10189790494106498301)
XLA Ops:
  0.0 0.5 collective-permute-start.5
  0.5 0.1 collective-permute-start.6
  1.2 6.8 %prepare.1 = (bf16[1024,2048]{1,0:T(8,128)(2,1)S(1)}, bf16[2048,1024]{1,0:T(8,128)(2,1)S(1)}, bf16[384,1024]{1,0:T(8,128)(2,1)S(1)}, bf16[384,1024]{1,0:T(8,128)...) custom-call(s32[1]{0:T(128)S(6)} %copy.9.count_ref, ...), custom_call_target="tpu_custom_call" | custom-call | flops 1 | bytes 1 | tf_op jit(solution)/shard_map/prepare/pallas_call | solution.py:229
  8.0 4.1 %collective-permute-start.3 = (bf16[120,512]{1,0:T(8,128)(2,1)S(1)}, bf16[120,512]{1,0:T(8,128)(2,1)S(1)}, u32[]{:S(2)}, u32[]{:S(2)}) collective-permute-start(bf16[120,512]{1,0:T(8,128)(2,1)S(1)} %get-tuple-element.49), channel_id=1, source_target_pairs={{0,8},{1,9},{2,10},{3,11},{4,12},{5,13},{6,14},{7,15},{8,0},{9,1},... | collective-permute-start | bytes 368648 | tf_op jit(solution)/shard_map/ppermute | solution.py:20
  12.1 1.3 %collective-permute-start.4 = (bf16[120,512]{1,0:T(8,128)(2,1)S(1)}, bf16[120,512]{1,0:T(8,128)(2,1)S(1)}, u32[]{:S(2)}, u32[]{:S(2)}) collective-permute-start(bf16[120,512]{1,0:T(8,128)(2,1)S(1)} %get-tuple-element.50), channel_id=1, source_target_pairs={{0,12},{1,13},{2,14},{3,15},{4,8},{5,9},{6,10},{7,11},{8,4},{9,5},... | collective-permute-start | bytes 368648 | tf_op jit(solution)/shard_map/ppermute | solution.py:20
  13.4 1.5 %collective-permute-start = (bf16[120,512]{1,0:T(8,128)(2,1)S(1)}, bf16[120,512]{1,0:T(8,128)(2,1)S(1)}, u32[]{:S(2)}, u32[]{:S(2)}) collective-permute-start(bf16[120,512]{1,0:T(8,128)(2,1)S(1)} %get-tuple-element.46), channel_id=1, source_target_pairs={{0,2},{1,3},{2,0},{3,1},{4,6},{5,7},{6,4},{7,5},{8,10},{9,11},{10,... | collective-permute-start | bytes 368648 | tf_op jit(solution)/shard_map/ppermute | solution.py:20
  14.9 0.0 collective-permute-done.5.refs_0_
  14.9 0.2 collective-permute-start.1
  15.2 0.0 collective-permute-done.6.refs_1_
  15.2 2.3 %collective-permute-start.2 = (bf16[120,512]{1,0:T(8,128)(2,1)S(1)}, bf16[120,512]{1,0:T(8,128)(2,1)S(1)}, u32[]{:S(2)}, u32[]{:S(2)}) collective-permute-start(bf16[120,512]{1,0:T(8,128)(2,1)S(1)} %get-tuple-element.48), channel_id=1, source_target_pairs={{0,6},{1,7},{2,4},{3,5},{4,2},{5,3},{6,0},{7,1},{8,14},{9,15},{10,... | collective-permute-start | bytes 368648 | tf_op jit(solution)/shard_map/ppermute | solution.py:20
  17.5 3.5 %load.1 = (bf16[1024,2048]{1,0:T(8,128)(2,1)S(1)}, bf16[2048,1024]{1,0:T(8,128)(2,1)S(1)}) custom-call(bf16[1024,2048]{1,0:T(8,128)(2,1)} %collective-permute-done.5.refs_0_, bf16[2048,1024]{1,0:T(8,128)(2,1)} %collective-permute-done.6.refs_1_), custom_call_target="tpu_custom_call" | custom-call | flops 1 | bytes 1 | tf_op jit(solution)/shard_map/load/pallas_call | solution.py:272
  21.0 0.5 collective-permute-done.3.refs_0_
  21.5 2.1 %collective-permute-start.11 = (bf16[120,512]{1,0:T(8,128)(2,1)S(1)}, bf16[120,512]{1,0:T(8,128)(2,1)S(1)}, u32[]{:S(2)}, u32[]{:S(2)}) collective-permute-start(bf16[120,512]{1,0:T(8,128)(2,1)S(1)} %get-tuple-element.68), channel_id=1, source_target_pairs={{0,10},{1,11},{2,8},{3,9},{4,14},{5,15},{6,12},{7,13},{8,2},{9,3},... | collective-permute-start | bytes 368648 | tf_op jit(solution)/shard_map/ppermute | solution.py:20
  23.6 0.0 collective-permute-done.4.refs_1_
  23.6 1.9 %collective-permute-start.12 = (bf16[120,512]{1,0:T(8,128)(2,1)S(1)}, bf16[120,512]{1,0:T(8,128)(2,1)S(1)}, u32[]{:S(2)}, u32[]{:S(2)}) collective-permute-start(bf16[120,512]{1,0:T(8,128)(2,1)S(1)} %get-tuple-element.69), channel_id=1, source_target_pairs={{0,14},{1,15},{2,12},{3,13},{4,10},{5,11},{6,8},{7,9},{8,6},{9,7},... | collective-permute-start | bytes 368648 | tf_op jit(solution)/shard_map/ppermute | solution.py:20
  25.5 2.5 %expert.3 = (bf16[120,512]{1,0:T(8,128)(2,1)S(1)}, bf16[120,512]{1,0:T(8,128)(2,1)S(1)}) custom-call(bf16[120,512]{1,0:T(8,128)(2,1)S(1)} %collective-permute-done.3.refs_0_, bf16[120,512]{1,0:T(8,128)(2,1)S(1)} %collective-permute-done.4.refs_1_, bf16[1024,2048]{1,0:T(8,128)(2,1)S(1)} %get-tuple-element.51.refs_2_.refs_4_, ...), custom_call_target="tpu_custom_call" | custom-call | flops 1 | bytes 1 | tf_op jit(solution)/shard_map/expert/pallas_call | solution.py:359
  27.9 0.0 collective-permute-done.refs_1_
  28.0 0.0 collective-permute-done.1.refs_2_
  28.0 0.0 collective-permute-done.2.refs_3_
  28.0 4.6 %expert.4 = (bf16[120,512]{1,0:T(8,128)(2,1)S(1)}, bf16[120,512]{1,0:T(8,128)(2,1)S(1)}, bf16[120,512]{1,0:T(8,128)(2,1)S(1)}, bf16[120,512]{1,0:T(8,128)(2,1)S(1)}) custom-call(bf16[120,512]{1,0:T(8,128)(2,1)S(1)} %get-tuple-element.45.refs_0_, bf16[120,512]{1,0:T(8,128)(2,1)S(1)} %collective-permute-done.refs_1_, ...), custom_call_target="tpu_custom_call" | custom-call | flops 1 | bytes 1 | tf_op jit(solution)/shard_map/expert/pallas_call | solution.py:359
  32.6 0.0 copy-start
  32.6 0.0 copy-start.1
  32.7 2.0 %collective-permute-start.7 = (bf16[120,512]{1,0:T(8,128)(2,1)S(1)}, bf16[120,512]{1,0:T(8,128)(2,1)S(1)}, u32[]{:S(2)}, u32[]{:S(2)}) collective-permute-start(bf16[120,512]{1,0:T(8,128)(2,1)S(1)} %get-tuple-element.64), channel_id=1, source_target_pairs={{0,8},{1,9},{2,10},{3,11},{4,12},{5,13},{6,14},{7,15},{8,0},{9,1},... | collective-permute-start | bytes 368648 | tf_op jit(solution)/shard_map/ppermute | solution.py:20
  34.7 2.6 %collective-permute-start.8 = (bf16[120,512]{1,0:T(8,128)(2,1)S(1)}, bf16[120,512]{1,0:T(8,128)(2,1)S(1)}, u32[]{:S(2)}, u32[]{:S(2)}) collective-permute-start(bf16[120,512]{1,0:T(8,128)(2,1)S(1)} %get-tuple-element.65), channel_id=1, source_target_pairs={{0,12},{1,13},{2,14},{3,15},{4,8},{5,9},{6,10},{7,11},{8,4},{9,5},... | collective-permute-start | bytes 368648 | tf_op jit(solution)/shard_map/ppermute | solution.py:20
  37.3 0.5 collective-permute-start.9
  37.8 0.0 collective-permute-done.11.refs_0_
  37.8 0.0 collective-permute-start.10
  37.8 0.0 collective-permute-done.12.refs_1_
  37.8 2.5 %expert.5 = (bf16[120,512]{1,0:T(8,128)(2,1)S(1)}, bf16[120,512]{1,0:T(8,128)(2,1)S(1)}) custom-call(bf16[120,512]{1,0:T(8,128)(2,1)S(1)} %collective-permute-done.11.refs_0_, bf16[120,512]{1,0:T(8,128)(2,1)S(1)} %collective-permute-done.12.refs_1_, bf16[1024,2048]{1,0:T(8,128)(2,1)S(1)} %get-tuple-element.51.refs_2_.refs_4_, ...), custom_call_target="tpu_custom_call" | custom-call | flops 1 | bytes 1 | tf_op jit(solution)/shard_map/expert/pallas_call | solution.py:359
  40.3 0.0 copy-start.2
  40.3 2.8 %collective-permute-start.13 = (bf16[120,512]{1,0:T(8,128)(2,1)S(1)}, bf16[120,512]{1,0:T(8,128)(2,1)S(1)}, u32[]{:S(2)}, u32[]{:S(2)}) collective-permute-start(bf16[120,512]{1,0:T(8,128)(2,1)S(1)} %get-tuple-element.72), channel_id=1, source_target_pairs={{0,10},{1,11},{2,8},{3,9},{4,14},{5,15},{6,12},{7,13},{8,2},{9,3},... | collective-permute-start | bytes 368648 | tf_op jit(solution)/shard_map/ppermute | solution.py:20
  43.1 2.0 %collective-permute-done.7.refs_1_ = bf16[120,512]{1,0:T(8,128)(2,1)S(1)} collective-permute-done((bf16[120,512]{1,0:T(8,128)(2,1)S(1)}, bf16[120,512]{1,0:T(8,128)(2,1)S(1)}, u32[]{:S(2)}, u32[]{:S(2)}) %collective-permute-start.7) | collective-permute-done | bytes 122912 | tf_op jit(solution)/shard_map/ppermute | solution.py:20
  45.1 0.0 collective-permute-start.15
  45.1 0.0 collective-permute-done.8.refs_2_
  45.1 3.2 %collective-permute-start.14 = (bf16[120,512]{1,0:T(8,128)(2,1)S(1)}, bf16[120,512]{1,0:T(8,128)(2,1)S(1)}, u32[]{:S(2)}, u32[]{:S(2)}) collective-permute-start(bf16[120,512]{1,0:T(8,128)(2,1)S(1)} %get-tuple-element.73), channel_id=1, source_target_pairs={{0,14},{1,15},{2,12},{3,13},{4,10},{5,11},{6,8},{7,9},{8,6},{9,7},... | collective-permute-start | bytes 368648 | tf_op jit(solution)/shard_map/ppermute | solution.py:20
  48.3 0.0 copy-done
  48.3 0.0 copy-done.1
  48.3 0.5 gate.1
  48.8 0.4 add.3.so_far_ref
  49.2 0.0 collective-permute-done.9.refs_0_
  49.2 0.0 collective-permute-done.10.refs_1_
  49.2 0.4 add.4.so_far_ref
  49.7 5.5 %collective-permute-done.15.refs_2_ = bf16[120,512]{1,0:T(8,128)(2,1)S(1)} collective-permute-done((bf16[120,512]{1,0:T(8,128)(2,1)S(1)}, bf16[120,512]{1,0:T(8,128)(2,1)S(1)}, u32[]{:S(2)}, u32[]{:S(2)}) %collective-permute-start.15) | collective-permute-done | bytes 122912 | tf_op jit(solution)/shard_map/ppermute | solution.py:20
  55.2 0.0 collective-permute-done.13.refs_0_
  55.2 0.0 collective-permute-done.14.refs_1_
  55.2 0.0 copy-done.2
  55.2 1.6 %finish.1 = bf16[384,1024]{1,0:T(8,128)(2,1)} custom-call(bf16[384,512]{1,0:T(8,128)(2,1)S(1)} %get-tuple-element.42.picking_ref, f32[384,1024]{1,0:T(8,128)S(1)} %add.4.so_far_ref, f32[384,1]{1,0:T(8,128)S(1)} %get-tuple-element.44.gate_ref, f32[1,1024]{1,0:T(1,128)S(1)} %bitcast.8, bf16[120,512]{1,0:T(8,128)(2,1)S(1)} %collective-permute-done.13.refs_0_, ...), custom_call_target="tpu_custom_call" | custom-call | flops 1 | bytes 1 | tf_op jit(solution)/shard_map/finish/pallas_call | solution.py:412
Async XLA Ops:
  0.0 14.9 %collective-permute-start.5 = (bf16[1024,2048]{1,0:T(8,128)(2,1)}, bf16[1024,2048]{1,0:T(8,128)(2,1)}, u32[]{:S(2)}, u32[]{:S(2)}) collective-permute-start(bf16[1024,2048]{1,0:T(8,128)(2,1)} %in_hbm.1), channel_id=1, source_target_pairs={{0,1},{1,0},{2,3},{3,2},{4,5},{5,4},{6,7},{7,6},{8,9},{9,8},{10,11... | collective-permute-start | bytes 12582920 | tf_op jit(solution)/shard_map/ppermute | solution.py:20
  0.5 14.7 %collective-permute-start.6 = (bf16[2048,1024]{1,0:T(8,128)(2,1)}, bf16[2048,1024]{1,0:T(8,128)(2,1)}, u32[]{:S(2)}, u32[]{:S(2)}) collective-permute-start(bf16[2048,1024]{1,0:T(8,128)(2,1)} %out_hbm.1), channel_id=1, source_target_pairs={{0,1},{1,0},{2,3},{3,2},{4,5},{5,4},{6,7},{7,6},{8,9},{9,8},{10,11... | collective-permute-start | bytes 12582920 | tf_op jit(solution)/shard_map/ppermute | solution.py:20
  8.0 13.5 %collective-permute-start.3 = (bf16[120,512]{1,0:T(8,128)(2,1)S(1)}, bf16[120,512]{1,0:T(8,128)(2,1)S(1)}, u32[]{:S(2)}, u32[]{:S(2)}) collective-permute-start(bf16[120,512]{1,0:T(8,128)(2,1)S(1)} %get-tuple-element.49), channel_id=1, source_target_pairs={{0,8},{1,9},{2,10},{3,11},{4,12},{5,13},{6,14},{7,15},{8,0},{9,1},... | collective-permute-start | bytes 368648 | tf_op jit(solution)/shard_map/ppermute | solution.py:20
  12.1 11.5 %collective-permute-start.4 = (bf16[120,512]{1,0:T(8,128)(2,1)S(1)}, bf16[120,512]{1,0:T(8,128)(2,1)S(1)}, u32[]{:S(2)}, u32[]{:S(2)}) collective-permute-start(bf16[120,512]{1,0:T(8,128)(2,1)S(1)} %get-tuple-element.50), channel_id=1, source_target_pairs={{0,12},{1,13},{2,14},{3,15},{4,8},{5,9},{6,10},{7,11},{8,4},{9,5},... | collective-permute-start | bytes 368648 | tf_op jit(solution)/shard_map/ppermute | solution.py:20
  13.4 14.5 %collective-permute-start = (bf16[120,512]{1,0:T(8,128)(2,1)S(1)}, bf16[120,512]{1,0:T(8,128)(2,1)S(1)}, u32[]{:S(2)}, u32[]{:S(2)}) collective-permute-start(bf16[120,512]{1,0:T(8,128)(2,1)S(1)} %get-tuple-element.46), channel_id=1, source_target_pairs={{0,2},{1,3},{2,0},{3,1},{4,6},{5,7},{6,4},{7,5},{8,10},{9,11},{10,... | collective-permute-start | bytes 368648 | tf_op jit(solution)/shard_map/ppermute | solution.py:20
  14.9 13.0 %collective-permute-start.1 = (bf16[120,512]{1,0:T(8,128)(2,1)S(1)}, bf16[120,512]{1,0:T(8,128)(2,1)S(1)}, u32[]{:S(2)}, u32[]{:S(2)}) collective-permute-start(bf16[120,512]{1,0:T(8,128)(2,1)S(1)} %get-tuple-element.47), channel_id=1, source_target_pairs={{0,4},{1,5},{2,6},{3,7},{4,0},{5,1},{6,2},{7,3},{8,12},{9,13},{10,... | collective-permute-start | bytes 368648 | tf_op jit(solution)/shard_map/ppermute | solution.py:20
  15.2 12.8 %collective-permute-start.2 = (bf16[120,512]{1,0:T(8,128)(2,1)S(1)}, bf16[120,512]{1,0:T(8,128)(2,1)S(1)}, u32[]{:S(2)}, u32[]{:S(2)}) collective-permute-start(bf16[120,512]{1,0:T(8,128)(2,1)S(1)} %get-tuple-element.48), channel_id=1, source_target_pairs={{0,6},{1,7},{2,4},{3,5},{4,2},{5,3},{6,0},{7,1},{8,14},{9,15},{10,... | collective-permute-start | bytes 368648 | tf_op jit(solution)/shard_map/ppermute | solution.py:20
  21.5 16.3 %collective-permute-start.11 = (bf16[120,512]{1,0:T(8,128)(2,1)S(1)}, bf16[120,512]{1,0:T(8,128)(2,1)S(1)}, u32[]{:S(2)}, u32[]{:S(2)}) collective-permute-start(bf16[120,512]{1,0:T(8,128)(2,1)S(1)} %get-tuple-element.68), channel_id=1, source_target_pairs={{0,10},{1,11},{2,8},{3,9},{4,14},{5,15},{6,12},{7,13},{8,2},{9,3},... | collective-permute-start | bytes 368648 | tf_op jit(solution)/shard_map/ppermute | solution.py:20
  23.6 14.2 %collective-permute-start.12 = (bf16[120,512]{1,0:T(8,128)(2,1)S(1)}, bf16[120,512]{1,0:T(8,128)(2,1)S(1)}, u32[]{:S(2)}, u32[]{:S(2)}) collective-permute-start(bf16[120,512]{1,0:T(8,128)(2,1)S(1)} %get-tuple-element.69), channel_id=1, source_target_pairs={{0,14},{1,15},{2,12},{3,13},{4,10},{5,11},{6,8},{7,9},{8,6},{9,7},... | collective-permute-start | bytes 368648 | tf_op jit(solution)/shard_map/ppermute | solution.py:20
  32.6 15.6 %copy-start = (bf16[1024,8]{0,1:T(8,128)(2,1)S(1)}, bf16[1024,8]{0,1:T(8,128)(2,1)}, u32[]{:S(2)}) copy-start(bf16[1024,8]{0,1:T(8,128)(2,1)} %param.12) | copy-start | bytes 49156
  32.6 15.6 %copy-start.1 = (s32[1,384,1]{1,2,0:T(1,128)S(1)}, s32[1,384,1]{1,2,0:T(1,128)}, u32[]{:S(2)}) copy-start(s32[1,384,1]{1,2,0:T(1,128)} %param.10) | copy-start | bytes 4612
  32.7 12.4 %collective-permute-start.7 = (bf16[120,512]{1,0:T(8,128)(2,1)S(1)}, bf16[120,512]{1,0:T(8,128)(2,1)S(1)}, u32[]{:S(2)}, u32[]{:S(2)}) collective-permute-start(bf16[120,512]{1,0:T(8,128)(2,1)S(1)} %get-tuple-element.64), channel_id=1, source_target_pairs={{0,8},{1,9},{2,10},{3,11},{4,12},{5,13},{6,14},{7,15},{8,0},{9,1},... | collective-permute-start | bytes 368648 | tf_op jit(solution)/shard_map/ppermute | solution.py:20
  34.7 10.4 %collective-permute-start.8 = (bf16[120,512]{1,0:T(8,128)(2,1)S(1)}, bf16[120,512]{1,0:T(8,128)(2,1)S(1)}, u32[]{:S(2)}, u32[]{:S(2)}) collective-permute-start(bf16[120,512]{1,0:T(8,128)(2,1)S(1)} %get-tuple-element.65), channel_id=1, source_target_pairs={{0,12},{1,13},{2,14},{3,15},{4,8},{5,9},{6,10},{7,11},{8,4},{9,5},... | collective-permute-start | bytes 368648 | tf_op jit(solution)/shard_map/ppermute | solution.py:20
  37.3 11.9 %collective-permute-start.9 = (bf16[120,512]{1,0:T(8,128)(2,1)S(1)}, bf16[120,512]{1,0:T(8,128)(2,1)S(1)}, u32[]{:S(2)}, u32[]{:S(2)}) collective-permute-start(bf16[120,512]{1,0:T(8,128)(2,1)S(1)} %get-tuple-element.61), channel_id=1, source_target_pairs={{0,2},{1,3},{2,0},{3,1},{4,6},{5,7},{6,4},{7,5},{8,10},{9,11},{10,... | collective-permute-start | bytes 368648 | tf_op jit(solution)/shard_map/ppermute | solution.py:20
  37.8 11.4 %collective-permute-start.10 = (bf16[120,512]{1,0:T(8,128)(2,1)S(1)}, bf16[120,512]{1,0:T(8,128)(2,1)S(1)}, u32[]{:S(2)}, u32[]{:S(2)}) collective-permute-start(bf16[120,512]{1,0:T(8,128)(2,1)S(1)} %get-tuple-element.62), channel_id=1, source_target_pairs={{0,4},{1,5},{2,6},{3,7},{4,0},{5,1},{6,2},{7,3},{8,12},{9,13},{10,... | collective-permute-start | bytes 368648 | tf_op jit(solution)/shard_map/ppermute | solution.py:20
  40.3 14.9 %copy-start.2 = (f32[1024]{0:T(1024)S(1)}, f32[1024]{0:T(1024)}, u32[]{:S(2)}) copy-start(f32[1024]{0:T(1024)} %param.15) | copy-start | bytes 12292
  40.3 14.8 %collective-permute-start.13 = (bf16[120,512]{1,0:T(8,128)(2,1)S(1)}, bf16[120,512]{1,0:T(8,128)(2,1)S(1)}, u32[]{:S(2)}, u32[]{:S(2)}) collective-permute-start(bf16[120,512]{1,0:T(8,128)(2,1)S(1)} %get-tuple-element.72), channel_id=1, source_target_pairs={{0,10},{1,11},{2,8},{3,9},{4,14},{5,15},{6,12},{7,13},{8,2},{9,3},... | collective-permute-start | bytes 368648 | tf_op jit(solution)/shard_map/ppermute | solution.py:20
  45.1 10.1 %collective-permute-start.15 = (bf16[120,512]{1,0:T(8,128)(2,1)S(1)}, bf16[120,512]{1,0:T(8,128)(2,1)S(1)}, u32[]{:S(2)}, u32[]{:S(2)}) collective-permute-start(bf16[120,512]{1,0:T(8,128)(2,1)S(1)} %get-tuple-element.74), channel_id=1, source_target_pairs={{0,6},{1,7},{2,4},{3,5},{4,2},{5,3},{6,0},{7,1},{8,14},{9,15},{10,... | collective-permute-start | bytes 368648 | tf_op jit(solution)/shard_map/ppermute | solution.py:20
  45.1 10.1 %collective-permute-start.14 = (bf16[120,512]{1,0:T(8,128)(2,1)S(1)}, bf16[120,512]{1,0:T(8,128)(2,1)S(1)}, u32[]{:S(2)}, u32[]{:S(2)}) collective-permute-start(bf16[120,512]{1,0:T(8,128)(2,1)S(1)} %get-tuple-element.73), channel_id=1, source_target_pairs={{0,14},{1,15},{2,12},{3,13},{4,10},{5,11},{6,8},{7,9},{8,6},{9,7},... | collective-permute-start | bytes 368648 | tf_op jit(solution)/shard_map/ppermute | solution.py:20
